TPU v7x, 32 devices: a whole 2x2x4 slice. The times are simulated.
32 devices in a mesh: seq: 8 (over z, y), doc: 4 (over x, core).
Axes of the slice: x: 2, y: 2, z: 4, core: 2. Of those that a mesh axis runs over, the one named last changes fastest.
Arguments:
- byte_q: bfloat16 [16384, 1024], P(('doc', 'seq')), parts along dimension 0, may hold values from -6 to 6
- byte_k: bfloat16 [16384, 1024], P(('doc', 'seq')), parts along dimension 0, may hold values from -6 to 6
- byte_v: bfloat16 [16384, 1024], P(('doc', 'seq')), parts along dimension 0, may hold values from -6 to 6
- byte_gain: bfloat16 [1024], replicated, may hold values from 0.2 to 4.5
- pool_query: bfloat16 [8, 128], replicated, may hold values from -12 to 12
- w_up: bfloat16 [1024, 2048], P('seq'), may hold values from -1 to 1
- patch_gain: bfloat16 [2048], replicated, may hold values from 0.099609375 to 1.8984375
- w_kv: bfloat16 [2048, 1024], P('seq'), may hold values from -1 to 1
- out_gain: bfloat16 [2048], replicated, may hold values from 0.2 to 4.5
- dec_gain: bfloat16 [1024], replicated, may hold values from 0.099609375 to 1.8984375
- patch_start: int32 [32, 80], P('doc'), parts along dimension 0, may hold values from 0 to 512, as said below
Outputs:
- byte_out: bfloat16 [16384, 1024], P(('doc', 'seq')), parts along dimension 0
- patch_out: bfloat16 [2560, 2048], P(('doc', 'seq')), parts along dimension 0
There are 4 independent parts, one for each index of `doc`. A program takes and returns all parts, laid end to end along the dimension named above; an argument that names none is the same for every part. Nothing has to cross between parts.
Inputs may be any that keep to these rules, and one draw needn't show every extreme that they name: `patch_start`: row r lists the patch starts of block r: 0 first, strictly rising over its live slots, then 512 in every unused slot; each row has at least 20 live slots, and some row has all 80 live.
All inputs are finite; a program needn't handle non-finite values.
Results may differ from a plain program's by a relative error of at most 0.0085.
Values may be sent and summed in bfloat16 or wider, within the bound.
No kernel may reach another device: no remote copies, remote signals or barrier semaphores. Data moves between devices by JAX's collectives and lax.ppermute only.
A program may use at most 128 MiB of HBM per device.

v0:
```python
import jax
import jax.numpy as jnp
from jax import lax
from jax.sharding import PartitionSpec as P

HB = 8
HD = 128
PATCH_QUERY_HEADS = 32
PATCH_KEY_HEADS = 8
PATCH_HEAD_SIZE = 64
PATCH_SLOTS = 80


epsilon = 1e-06


def passed_along(value, axis, steps):
    count = lax.axis_size(axis)
    first, last = (max(0, -steps), min(count, count - steps))
    return lax.ppermute(value, axis, [(source, source + steps) for source in range(first, last)])


def normed(matrix, gains):
    return (
        matrix
        * lax.rsqrt(jnp.mean(matrix * matrix, axis=-1, keepdims=True) + epsilon)
        * gains.astype(jnp.float32)
    )


def masked_weights(scores, allowed):
    scores = jnp.where(allowed, scores, -jnp.inf)
    peak = jnp.max(scores, axis=-1, keepdims=True)
    expo = jnp.where(allowed, jnp.exp(scores - peak), 0.0)
    return (expo / jnp.sum(expo, axis=-1, keepdims=True)).astype(jnp.bfloat16)


def byte_attention(query_rows, key_rows, value_rows, leading):
    nbytes = query_rows.shape[0]
    reach = key_rows.shape[0] - nbytes
    query_head_rows = query_rows.reshape(nbytes, HB, HD).transpose(1, 0, 2)
    key_head_rows = key_rows.reshape(nbytes + reach, HB, HD).transpose(1, 0, 2)
    value_head_rows = value_rows.reshape(nbytes + reach, HB, HD).transpose(1, 0, 2)
    row_pos = jnp.arange(nbytes, dtype=jnp.int32)[:, None]
    col_pos = jnp.arange(nbytes + reach, dtype=jnp.int32)[None, :]
    allowed = (
        (col_pos > row_pos)
        & (col_pos <= row_pos + reach)
        & ((col_pos >= reach) | jnp.logical_not(leading))
    )

    def one_head(operands):
        head_query, head_key, head_value = operands
        scores = jnp.dot(head_query, head_key.T, preferred_element_type=jnp.float32) * HD ** (-0.5)
        weights = masked_weights(scores, allowed)
        return jnp.dot(weights, head_value, preferred_element_type=jnp.float32)

    mixed = lax.map(one_head, (query_head_rows, key_head_rows, value_head_rows))
    return mixed.transpose(1, 0, 2).reshape(nbytes, HB * HD)


def segments(starts, nbytes):
    positions = jnp.arange(nbytes, dtype=jnp.int32)
    segment = jnp.sum((starts[None, :] <= positions[:, None]).astype(jnp.int32), axis=1) - 1
    member = segment[None, :] == jnp.arange(starts.shape[0], dtype=jnp.int32)[:, None]
    return (segment, member)


def pool(encoded, member, pool_query):
    nbytes = encoded.shape[0]
    enc_heads = encoded.reshape(nbytes, HB, HD)
    scores = jnp.einsum(
        "bhd,hd->bh", enc_heads, pool_query, preferred_element_type=jnp.float32
    ) * HD ** (-0.5)
    inside = member[:, :, None]
    highest = jnp.max(jnp.where(inside, scores[None], -jnp.inf), axis=1)
    own_max = jnp.max(jnp.where(inside, highest[:, None, :], -jnp.inf), axis=0)
    expo = jnp.exp(scores - own_max)
    totals = jnp.sum(jnp.where(inside, expo[None], 0.0), axis=1)
    divisor = jnp.max(jnp.where(inside, totals[:, None, :], 0.0), axis=0)
    weights = (expo / divisor).astype(jnp.bfloat16)
    spread = jnp.where(inside, weights[None], jnp.zeros((), jnp.bfloat16))
    pooled = jnp.einsum("pbh,bhd->phd", spread, enc_heads, preferred_element_type=jnp.float32)
    return pooled.reshape(member.shape[0], HB * HD).astype(jnp.bfloat16)


def decode(encoded, patch_rows, segment):
    nbytes = encoded.shape[0]
    slot_total_count = patch_rows.shape[0]
    enc_heads = encoded.reshape(nbytes, HB, HD)
    packed = patch_rows.reshape(slot_total_count, HB, 2, HD)
    scores = jnp.einsum(
        "bhd,phd->hbp", enc_heads, packed[:, :, 0], preferred_element_type=jnp.float32
    ) * HD ** (-0.5)
    allowed = jnp.arange(slot_total_count, dtype=jnp.int32)[None, :] <= segment[:, None]
    weights = masked_weights(scores, allowed[None])
    mixed = jnp.einsum("hbp,phd->bhd", weights, packed[:, :, 1], preferred_element_type=jnp.float32)
    return mixed.reshape(nbytes, HB * HD)


def per_device(
    byte_q,
    byte_k,
    byte_v,
    byte_gain,
    pool_query,
    w_up,
    patch_gain,
    w_kv,
    out_gain,
    dec_gain,
    patch_start,
):
    nbytes = byte_q.shape[0]
    device = lax.axis_index("seq")
    head_groups = PATCH_QUERY_HEADS // PATCH_KEY_HEADS
    tails = passed_along((byte_k, byte_v), "seq", 1)
    key_rows = jnp.concatenate([tails[0], byte_k], axis=0)
    value_rows = jnp.concatenate([tails[1], byte_v], axis=0)
    encoded = normed(byte_attention(byte_q, key_rows, value_rows, device == 0), byte_gain).astype(
        jnp.bfloat16
    )
    starts = lax.dynamic_index_in_dim(patch_start, device, 0, keepdims=False)
    segment, member = segments(starts, nbytes)
    pooled = pool(encoded, member, pool_query)
    columns = pooled
    lifted = jnp.dot(
        columns, lax.all_gather(w_up, "seq", axis=0, tiled=True), preferred_element_type=jnp.float32
    )
    patch_input = normed(lifted, patch_gain).astype(jnp.bfloat16)
    columns = patch_input
    key_value_pairs = jnp.dot(
        columns, lax.all_gather(w_kv, "seq", axis=0, tiled=True), preferred_element_type=jnp.float32
    ).astype(jnp.bfloat16)
    counts = jnp.sum((patch_start < nbytes).astype(jnp.int32), axis=1)
    live_grid = jnp.arange(PATCH_SLOTS, dtype=jnp.int32)[None, :] < counts[:, None]
    is_live = live_grid.reshape(-1)
    query_start = device * PATCH_SLOTS
    query_pos = query_start + jnp.arange(PATCH_SLOTS, dtype=jnp.int32)
    query_head_rows = patch_input.reshape(
        PATCH_SLOTS, PATCH_KEY_HEADS, head_groups, PATCH_HEAD_SIZE
    ).transpose(1, 2, 0, 3)
    start_state = (
        jnp.full((PATCH_KEY_HEADS, head_groups, PATCH_SLOTS), -1e30, jnp.float32),
        jnp.zeros((PATCH_KEY_HEADS, head_groups, PATCH_SLOTS), jnp.float32),
        jnp.zeros((PATCH_KEY_HEADS, head_groups, PATCH_SLOTS, PATCH_HEAD_SIZE), jnp.float32),
    )
    block_rows = lax.all_gather(key_value_pairs, "seq", axis=0, tiled=True)
    row_count = block_rows.shape[0]

    def compute():
        peak_old, norm_sum, summed = start_state
        key_head_rows = block_rows[:, : PATCH_KEY_HEADS * PATCH_HEAD_SIZE].reshape(
            row_count, PATCH_KEY_HEADS, PATCH_HEAD_SIZE
        )
        value_head_rows = block_rows[:, PATCH_KEY_HEADS * PATCH_HEAD_SIZE :].reshape(
            row_count, PATCH_KEY_HEADS, PATCH_HEAD_SIZE
        )
        key_pos = jnp.arange(row_count, dtype=jnp.int32)
        allowed = (key_pos[None, :] <= query_pos[:, None]) & is_live[None, :]
        scores = jnp.einsum(
            "kgqd,pkd->kgqp", query_head_rows, key_head_rows, preferred_element_type=jnp.float32
        ) * PATCH_HEAD_SIZE ** (-0.5)
        scores = jnp.where(allowed, scores, -1e30)
        peak_new = jnp.maximum(peak_old, jnp.max(scores, axis=-1))
        expo = jnp.where(allowed, jnp.exp(scores - peak_new[..., None]), 0.0)
        norm_sum = jnp.sum(expo, axis=-1)
        summed = jnp.einsum(
            "kgqp,pkd->kgqd",
            expo.astype(jnp.bfloat16),
            value_head_rows,
            preferred_element_type=jnp.float32,
        )
        return (peak_new, norm_sum, summed)

    peak_end, norm_sum, summed = lax.cond(
        jnp.int32(0) <= query_start + PATCH_SLOTS - 1, compute, lambda: start_state
    )
    mixed = summed / norm_sum[..., None]
    mixed = mixed.transpose(2, 0, 1, 3).reshape(PATCH_SLOTS, PATCH_QUERY_HEADS * PATCH_HEAD_SIZE)
    alive = lax.dynamic_index_in_dim(live_grid, device, 0, keepdims=False)
    patch_out = (normed(mixed, out_gain) * alive[:, None].astype(jnp.float32)).astype(jnp.bfloat16)
    byte_out = normed(decode(encoded, patch_out, segment), dec_gain).astype(jnp.bfloat16)
    return (byte_out, patch_out)


def solution(mesh):
    placed = (
        P(("doc", "seq"), None),
        P(("doc", "seq"), None),
        P(("doc", "seq"), None),
        P(),
        P(),
        P("seq", None),
        P(),
        P("seq", None),
        P(),
        P(),
        P("doc", None),
    )
    return jax.shard_map(
        per_device,
        mesh=mesh,
        in_specs=placed,
        out_specs=(P(("doc", "seq"), None), P(("doc", "seq"), None)),
        check_vma=False,
    )
```

profile of v0, /device:TPU:0, one launch (start us, length us, event | category | flops | bytes accessed | tf_op | source)
XLA Modules:
  0.0 257.3 jit_solution(3354933284865370100)
XLA Ops:
  7.2 0.7 all-gather.4.cloned.1.call-update
  8.0 2.3 copy.35
  10.3 6.0 %collective-permute-start.1 = (bf16[512,1024]{0,1:T(8,128)(2,1)}, bf16[512,1024]{0,1:T(8,128)(2,1)}, u32[]{:S(2)}, u32[]{:S(2)}) collective-permute-start(bf16[512,1024]{0,1:T(8,128)(2,1)} %copy.35), channel_id=1, source_target_pairs={{0,4},{4,8},{8,12},{12,16},{16,20},{20,24},{24,28},{1,5},{5,9},{9,... | collective-permute-start | bytes 3145736 | tf_op jit(solution)/shard_map/ppermute | solution.py:20
  16.3 0.5 copy.33
  16.8 3.5 %collective-permute-start = (bf16[512,1024]{0,1:T(8,128)(2,1)S(1)}, bf16[512,1024]{0,1:T(8,128)(2,1)}, u32[]{:S(2)}, u32[]{:S(2)}) collective-permute-start(bf16[512,1024]{0,1:T(8,128)(2,1)S(1)} %copy.33), channel_id=1, source_target_pairs={{0,4},{4,8},{8,12},{12,16},{16,20},{20,24},{24,28},{1,5},{5,9},{9,... | collective-permute-start | bytes 3145736 | tf_op jit(solution)/shard_map/ppermute | solution.py:20
  20.4 2.3 copy.32
  23.0 21.8 %collective-permute-done.1 = bf16[512,1024]{0,1:T(8,128)(2,1)} collective-permute-done((bf16[512,1024]{0,1:T(8,128)(2,1)}, bf16[512,1024]{0,1:T(8,128)(2,1)}, u32[]{:S(2)}, u32[]{:S(2)}) %collective-permute-start.1) | collective-permute-done | bytes 1048608 | tf_op jit(solution)/shard_map/ppermute | solution.py:20
  44.8 3.2 %pad_maximum_fusion.1 = bf16[1024,1024]{0,1:T(8,128)(2,1)} fusion(bf16[512,1024]{0,1:T(8,128)(2,1)} %copy.35, bf16[512,1024]{0,1:T(8,128)(2,1)} %collective-permute-done.1), kind=kLoop, calls=%fused_computation.42 | loop fusion | flops 4194304 | bytes 4194304 | tf_op jit(solution)/shard_map/concatenate | solution.py:119
  48.0 23.5 %collective-permute-done = bf16[512,1024]{0,1:T(8,128)(2,1)} collective-permute-done((bf16[512,1024]{0,1:T(8,128)(2,1)S(1)}, bf16[512,1024]{0,1:T(8,128)(2,1)}, u32[]{:S(2)}, u32[]{:S(2)}) %collective-permute-start) | collective-permute-done | bytes 1048608 | tf_op jit(solution)/shard_map/ppermute | solution.py:20
  71.4 2.9 %pad_maximum_fusion = bf16[1024,1024]{0,1:T(8,128)(2,1)} fusion(bf16[512,1024]{0,1:T(8,128)(2,1)S(1)} %copy.33, bf16[512,1024]{0,1:T(8,128)(2,1)} %collective-permute-done), kind=kLoop, calls=%fused_computation.41 | loop fusion | flops 4194304 | bytes 4194304 | tf_op jit(solution)/shard_map/concatenate | solution.py:118
  74.3 37.3 %while.11 = (s32[]{:T(128)}, f32[8,512,128]{2,1,0:T(8,128)S(1)}, bf16[8,512,128]{1,2,0:T(8,128)(2,1)}, bf16[8,1024,128]{1,2,0:T(8,128)(2,1)}, bf16[8,1024,128]{1...) while((s32[]{:T(128)}, f32[8,512,128]{2,1,0:T(8,128)S(1)}, ...), condition=%wide.region_3.4_spmd.clone, body=%wide.region_0.3_spmd.clone.sunk | while | flops 282065920 | bytes 7230549 | solution.py:58
  74.3 1.8 fusion.95
  76.0 0.9 fusion.96
  77.0 1.9 fusion.97
  78.9 1.8 fusion.95
  80.7 0.9 fusion.96
  81.6 1.9 fusion.97
  83.6 1.8 fusion.95
  85.4 0.9 fusion.96
  86.3 1.9 fusion.97
  88.3 1.8 fusion.95
  90.0 0.9 fusion.96
  91.0 1.9 fusion.97
  92.9 1.8 fusion.95
  94.7 0.9 fusion.96
  95.6 1.9 fusion.97
  97.6 1.8 fusion.95
  99.4 0.9 fusion.96
  100.3 1.9 fusion.97
  102.3 1.8 fusion.95
  104.0 0.9 fusion.96
  105.0 1.9 fusion.97
  106.9 1.8 fusion.95
  108.7 0.9 fusion.96
  109.6 1.9 fusion.97
  111.6 0.2 multiply_reduce_fusion
  111.8 0.3 fusion.43
  112.2 0.4 fusion.64
  112.5 0.3 fusion.76
  112.8 0.3 fusion.77
  113.1 0.3 fusion.42
  113.4 1.6 all-gather.4.cloned.1.call-done
  115.0 3.2 %multiply_reduce_fusion.1 = (f32[80]{0:T(128)S(1)}, f32[80,2048]{1,0:T(8,128)S(1)}) fusion(bf16[1024,2048]{1,0:T(8,128)(2,1)} %all-gather.4.cloned.1.call-done, bf16[8,10,8,128]{3,2,1,0:T(8,128)(2,1)S(1)} %fusion.42), kind=kOutput, calls=%fused_computation.74 | convolution fusion | flops 335871936 | bytes 5013824 | tf_op jit(solution)/shard_map/dot_general | solution.py:127
  118.2 0.1 multiply_convert_fusion.3
  118.4 70.8 %all-gather.6.cloned.1.call-done = bf16[2048,1024]{1,0:T(8,128)(2,1)} async-done(((bf16[256,1024]{1,0:T(8,128)(2,1)}), bf16[2048,1024]{1,0:T(8,128)(2,1)}) %all-gather.6.cloned.1.call-update) | async-done | bytes 4194320 | tf_op jit(solution)/shard_map/all_gather | solution.py:133
  189.2 3.7 %convolution_convert_fusion = bf16[80,1024]{1,0:T(8,128)(2,1)} fusion(bf16[80,2048]{1,0:T(8,128)(2,1)S(1)} %multiply_convert_fusion.3, bf16[2048,1024]{1,0:T(8,128)(2,1)} %all-gather.6.cloned.1.call-done), kind=kOutput, calls=%fused_computation.60 | convolution fusion | flops 335626240 | bytes 4685824 | tf_op jit(solution)/shard_map/dot_general | solution.py:132
  193.2 0.3 copy.41
  193.5 39.6 %all-gather.8.cloned.1.call-done = bf16[640,1024]{1,0:T(8,128)(2,1)} async-done(((bf16[80,1024]{1,0:T(8,128)(2,1)}), bf16[640,1024]{1,0:T(8,128)(2,1)}) %all-gather.8.cloned.1.call-update) | async-done | bytes 1310736 | tf_op jit(solution)/shard_map/all_gather | solution.py:148
  233.1 8.0 %conditional.1 = (f32[8,4,80]{2,1,0:T(4,128)S(1)}, f32[8,4,80,64]{2,3,1,0:T(8,128)S(1)}) conditional(s32[]{:T(128)} %convert_element_type.73, () %tuple.20, (s32[]{:T(128)}, s32[80]{0:T(128)S(1)}, pred[8,80]{1,0:T(8,128)(4,1)S(1)}, bf16[640,1024]{1,0:T(8,128)(2,1)}, bf16[8,4,80,64]{2,3,1,0:T(8,128)(2,1)S(1)}) %tuple.61), branch_computations={%region_12.13_spmd, %region_13.16_spmd} | conditional | flops 440829504 | bytes 27466580 | solution.py:176
  233.3 1.7 copy.42
  235.2 1.4 fusion.2
  236.6 2.3 fusion.5
  238.9 2.2 fusion.4
  241.1 0.3 fusion.47
  241.5 0.3 copy.43
  241.8 1.1 fusion.46
  242.9 0.2 multiply_convert_fusion.2
  243.1 0.5 fusion.41
  243.6 0.7 fusion.78
  244.3 0.3 copy-done.1
  244.6 0.9 copy.46
  245.6 2.0 fusion.33
  247.6 1.9 copy.45
  249.6 1.2 multiply_convert_fusion
  (49 shorter events, 1.0 us)
Async XLA Ops:
  7.2 105.0 %copy-start = (bf16[8,128]{1,0:T(8,128)(2,1)S(1)}, bf16[8,128]{1,0:T(8,128)(2,1)}, u32[]{:S(2)}) copy-start(bf16[8,128]{1,0:T(8,128)(2,1)} %param.19) | copy-start | bytes 6148
  7.2 9.1 %copy-start.2 = (bf16[512,1024]{1,0:T(8,128)(2,1)S(1)}, bf16[512,1024]{1,0:T(8,128)(2,1)}, u32[]{:S(2)}) copy-start(bf16[512,1024]{1,0:T(8,128)(2,1)} %param.16) | copy-start | bytes 3145732
  7.2 107.8 %all-gather.4.cloned.1.call-start = ((), (), s32[]{:S(2)}) async-start(), calls=%async_computation | async-start | bytes 4718592 | tf_op jit(solution)/shard_map/all_gather | solution.py:128
  7.9 181.3 %all-gather.6.cloned.1.call-start = ((), (), s32[]{:S(2)}) async-start(), calls=%async_computation.1 | async-start | bytes 4718592 | tf_op jit(solution)/shard_map/all_gather | solution.py:133
  10.3 12.5 %copy-start.3 = (bf16[2048]{0:T(1024)(128)(2,1)S(1)}, bf16[2048]{0:T(1024)(128)(2,1)}, u32[]{:S(2)}) copy-start(bf16[2048]{0:T(1024)(128)(2,1)} %param.21) | copy-start | bytes 12292
  10.3 12.5 %copy-start.5 = (s32[8,80]{1,0:T(8,128)S(1)}, s32[8,80]{1,0:T(8,128)}, u32[]{:S(2)}) copy-start(s32[8,80]{1,0:T(8,128)} %param.25) | copy-start | bytes 7684
  10.3 12.6 %copy-start.6 = (bf16[1024]{0:T(1024)(128)(2,1)S(1)}, bf16[1024]{0:T(1024)(128)(2,1)}, u32[]{:S(2)}) copy-start(bf16[1024]{0:T(1024)(128)(2,1)} %param.18) | copy-start | bytes 6148
  10.3 34.5 %collective-permute-start.1 = (bf16[512,1024]{0,1:T(8,128)(2,1)}, bf16[512,1024]{0,1:T(8,128)(2,1)}, u32[]{:S(2)}, u32[]{:S(2)}) collective-permute-start(bf16[512,1024]{0,1:T(8,128)(2,1)} %copy.35), channel_id=1, source_target_pairs={{0,4},{4,8},{8,12},{12,16},{16,20},{20,24},{24,28},{1,5},{5,9},{9,... | collective-permute-start | bytes 3145736 | tf_op jit(solution)/shard_map/ppermute | solution.py:20
  16.8 54.6 %collective-permute-start = (bf16[512,1024]{0,1:T(8,128)(2,1)S(1)}, bf16[512,1024]{0,1:T(8,128)(2,1)}, u32[]{:S(2)}, u32[]{:S(2)}) collective-permute-start(bf16[512,1024]{0,1:T(8,128)(2,1)S(1)} %copy.33), channel_id=1, source_target_pairs={{0,4},{4,8},{8,12},{12,16},{16,20},{20,24},{24,28},{1,5},{5,9},{9,... | collective-permute-start | bytes 3145736 | tf_op jit(solution)/shard_map/ppermute | solution.py:20
  20.4 212.8 %all-gather.8.cloned.1.call-start = ((), (), s32[]{:S(2)}) async-start(), calls=%async_computation.2 | async-start | bytes 1474560 | tf_op jit(solution)/shard_map/all_gather | solution.py:148
  118.4 74.6 %copy-start.4 = (bf16[2048]{0:T(1024)(128)(2,1)S(1)}, bf16[2048]{0:T(1024)(128)(2,1)}, u32[]{:S(2)}) copy-start(bf16[2048]{0:T(1024)(128)(2,1)} %param.23) | copy-start | bytes 12292
  118.4 74.6 %copy-start.7 = (bf16[1024]{0:T(1024)(128)(2,1)S(1)}, bf16[1024]{0:T(1024)(128)(2,1)}, u32[]{:S(2)}) copy-start(bf16[1024]{0:T(1024)(128)(2,1)} %param.24) | copy-start | bytes 6148
  243.6 1.0 copy-start.1
Sparse Core Ops, SparseCore 0:
  10.2 104.8 all-gather.3
  117.2 71.9 all-gather.5
  193.0 40.0 all-gather.7
where the time goes:
time: 258 us; the launch traced here: 257 us
  waiting for transfers between devices  158 us (61%)
  matrix products  44.1 us (17%)
  other arithmetic  20.4 us (8%)
  between operations  14 us (5%)
  local copies, waits for them, and re-layouts  10.9 us (4%)
  starting transfers between devices  9.63 us (4%)
    all_gather x1, waiting for transfers between devices, per_device(): lax.all_gather(w_kv, 'seq', axis=0, tiled=True)  70.8 us
    ppermute x2, waiting for transfers between devices, passed_along(): lax.ppermute(value, axis, [(source, source + steps) for source in range(f...  45.3 us
    all_gather x1, waiting for transfers between devices, per_device(): block_rows = lax.all_gather(key_value_pairs, 'seq', axis=0, tiled=True)  39.6 us
    dot_general x8, matrix products, one_head(): return jnp.dot(weights, head_value, preferred_element_type=jnp.float32)  15.4 us
    dot_general x8, matrix products, one_head(): jnp.dot(head_query, head_key.T, preferred_element_type=jnp.float32)  14.1 us
    ppermute x2, starting transfers between devices, passed_along(): lax.ppermute(value, axis, [(source, source + steps) for source in range(f...  9.51 us
    reduce_sum x8, other arithmetic, masked_weights(): return (expo / jnp.sum(expo, axis=-1, keepdims=True)).astype(jnp.bfloat16)  7.59 us
    unnamed x20, local copies, waits for them, and re-layouts  6.43 us
  transfers between devices with their start and end apart: 5, of which 5 were waited for; matrix products, arithmetic and copies ran while one was open for 21% of the time, Pallas kernels for 0%

commit v1 on v0

v1 whole, which is shorter than its diff:
```python
import functools

import jax
import jax.numpy as jnp
from jax import lax
from jax.experimental import pallas as pl
from jax.experimental.pallas import tpu as pltpu
from jax.sharding import PartitionSpec as P

PATCH_QUERY_HEADS = 32
PATCH_KEY_HEADS = 8
LOG2E = 1.4426950408889634
LOW = -1e30
TILE = 128
epsilon = 1e-06
VMEM = pl.BlockSpec(memory_space=pltpu.VMEM)
ANY = pl.BlockSpec(memory_space=pl.ANY)


def dot_t(a, b):
    return lax.dot_general(a, b, (((1,), (1,)), ((), ())), preferred_element_type=jnp.float32)


def dot(a, b):
    return jnp.dot(a, b, preferred_element_type=jnp.float32)


def own_kernel(q_ref, k_ref, v_ref, mix_ref, lse_ref):
    head = pl.program_id(0)
    nbytes, size = q_ref.shape
    factor = size ** (-0.5) * LOG2E
    row = lax.broadcasted_iota(jnp.int32, (TILE, TILE), 0)
    col = lax.broadcasted_iota(jnp.int32, (TILE, TILE), 1)
    causal = col <= row
    values = jnp.concatenate([v_ref[...], jnp.ones((nbytes, size), jnp.bfloat16)], axis=1)
    lane = lax.broadcasted_iota(jnp.int32, (TILE, TILE), 1)

    for start in range(0, nbytes, TILE):
        end = start + TILE
        scores = dot_t(q_ref[start:end, :], k_ref[:end, :])
        last = jnp.where(causal, scores[:, start:end], LOW)
        scores = last if start == 0 else jnp.concatenate([scores[:, :start], last], axis=1)
        peak = jnp.max(scores, axis=1, keepdims=True)
        expo = jnp.exp2((scores - peak) * factor).astype(jnp.bfloat16)
        total = dot(expo, values[:end])
        mix_ref[start:end, :] = total[:, :size] / total[:, size:]
        lse = peak * factor + jnp.log2(total[:, size:])
        lse_ref[start:end, :] = jnp.where(lane == head, lse, lse_ref[start:end, :])


def own_attention(q, k, v):
    nbytes, width = q.shape
    block = pl.BlockSpec((nbytes, TILE), lambda h: (0, h))
    return pl.pallas_call(
        own_kernel,
        grid=(width // TILE,),
        in_specs=[block] * 3,
        out_specs=[block, pl.BlockSpec((nbytes, TILE), lambda h: (0, 0))],
        out_shape=[
            jax.ShapeDtypeStruct((nbytes, width), jnp.float32),
            jax.ShapeDtypeStruct((nbytes, TILE), jnp.float32),
        ],
        compiler_params=pltpu.CompilerParams(vmem_limit_bytes=24 * 2**20),
        name="own_attention",
    )(q, k, v)


def cross_kernel(
    lead_ref, q_ref, k_ref, v_ref, own_ref, lse_ref, gain_ref, query_ref, start_ref, next_ref,
    enc_ref, pooled_ref, mix_ref,
):
    head = pl.program_id(0)
    heads = pl.num_programs(0)
    nbytes, size = q_ref.shape
    slots = start_ref.shape[0]
    width = mix_ref.shape[1]
    factor = size ** (-0.5) * LOG2E
    row = lax.broadcasted_iota(jnp.int32, (TILE, TILE), 0)
    col = lax.broadcasted_iota(jnp.int32, (TILE, TILE), 1)
    later = (col > row) & (lead_ref[0] == 0)
    bias = jnp.where(lead_ref[0] == 0, 0.0, LOW)
    values = jnp.concatenate([v_ref[...], jnp.ones((nbytes, size), jnp.bfloat16)], axis=1)
    lane = lax.broadcasted_iota(jnp.int32, (TILE, TILE), 1)

    for start in range(0, nbytes, TILE):
        end = start + TILE
        scores = dot_t(q_ref[start:end, :], k_ref[start:, :])
        first = jnp.where(later, scores[:, :TILE], LOW)
        if end < nbytes:
            scores = jnp.concatenate([first, scores[:, TILE:] + bias], axis=1)
        else:
            scores = first
        lse = jnp.sum(jnp.where(lane == head, lse_ref[start:end, :], 0.0), axis=1, keepdims=True)
        peak = jnp.maximum(jnp.max(scores, axis=1, keepdims=True) * factor, lse)
        expo = jnp.exp2(scores * factor - peak).astype(jnp.bfloat16)
        total = dot(expo, values[start:])
        share = jnp.exp2(lse - peak)
        columns = pl.ds(pl.multiple_of(head * size, size), size)
        mix_ref[start:end, columns] = (own_ref[start:end, :] * share + total[:, :size]) / (
            share + total[:, size:]
        )

    @pl.when(head == heads - 1)
    def _():
        for start in range(0, nbytes, TILE):
            end = start + TILE
            mix = mix_ref[start:end, :]
            scale = lax.rsqrt(jnp.mean(mix * mix, axis=1, keepdims=True) + epsilon)
            enc_ref[start:end, :] = (mix * scale * gain_ref[...]).astype(jnp.bfloat16)
        enc = enc_ref[...]
        n_heads = query_ref.shape[0]
        wide = jnp.concatenate([query_ref[...].astype(jnp.float32)] * n_heads, axis=1)
        head_row = lax.broadcasted_iota(jnp.int32, wide.shape, 0)
        head_col = lax.broadcasted_iota(jnp.int32, wide.shape, 1) // size
        wide = jnp.where(head_row == head_col, wide, 0.0).astype(jnp.bfloat16)
        scores = dot_t(wide, enc) * factor
        place = lax.broadcasted_iota(jnp.int32, (slots, nbytes), 1)
        member = (place >= start_ref[...]) & (place < next_ref[...])
        for h in range(n_heads):
            inside = jnp.where(member, scores[h : h + 1, :], LOW)
            peak = jnp.max(inside, axis=1, keepdims=True)
            expo = jnp.where(member, jnp.exp2(inside - peak), 0.0)
            total = jnp.sum(expo, axis=1, keepdims=True)
            weights = (expo * jnp.where(total > 0, 1.0 / total, 0.0)).astype(jnp.bfloat16)
            pooled_ref[:, h * size : (h + 1) * size] = dot(
                weights, enc[:, h * size : (h + 1) * size]
            ).astype(jnp.bfloat16)


def cross_attention(leading, q, k, v, own, lse, gain, pool_query, starts, ends):
    nbytes, width = q.shape
    slots = starts.shape[0]
    block = pl.BlockSpec((nbytes, TILE), lambda h: (0, h))

    def whole(*shape):
        return pl.BlockSpec(shape, lambda h: (0,) * len(shape))

    return pl.pallas_call(
        cross_kernel,
        grid=(width // TILE,),
        in_specs=[
            pl.BlockSpec(memory_space=pltpu.SMEM),
            block,
            block,
            block,
            block,
            whole(nbytes, TILE),
            whole(1, width),
            whole(*pool_query.shape),
            whole(slots, 1),
            whole(slots, 1),
        ],
        out_specs=[whole(nbytes, width), whole(slots, width)],
        out_shape=[
            jax.ShapeDtypeStruct((nbytes, width), jnp.bfloat16),
            jax.ShapeDtypeStruct((slots, width), jnp.bfloat16),
        ],
        scratch_shapes=[pltpu.VMEM((nbytes, width), jnp.float32)],
        compiler_params=pltpu.CompilerParams(vmem_limit_bytes=32 * 2**20),
        name="cross_attention",
    )(leading, q, k, v, own, lse, gain, pool_query, starts, ends)


def patch_kernel(n_blocks, plan, n_weights, at_ref, *refs):
    blocks = refs[:n_blocks]
    weights = refs[n_blocks : n_blocks + n_weights]
    (
        enc_ref, bias_ref, pgain_ref, ogain_ref, dgain_ref, start_col_ref, start_row_ref,
        byte_ref, patch_ref, up_ref, kv_w_ref, kv_ref, mix_ref, in_ref, sems,
    ) = refs[n_blocks + n_weights :]
    copies = plan(at_ref, weights, up_ref, kv_w_ref)
    copies = [
        pltpu.make_async_copy(source, target, sems.at[i]) for i, (source, target) in enumerate(copies)
    ]
    for copy in copies:
        copy.start()
    for copy in copies:
        copy.wait()

    slots = patch_ref.shape[0]
    offset = 0
    for b, block in enumerate(blocks):
        rows = block.shape[0]
        step = rows if rows <= 4 * slots else 4 * slots
        for r in range(0, rows, step):
            lifted = dot(block[r : r + step, :], up_ref[...])
            scale = lax.rsqrt(jnp.mean(lifted * lifted, axis=1, keepdims=True) + epsilon)
            patch_in = (lifted * scale * pgain_ref[...]).astype(jnp.bfloat16)
            if b == 0:
                in_ref[...] = patch_in[:slots]
            kv_ref[offset + r : offset + r + step, :] = dot(patch_in, kv_w_ref[...]).astype(
                jnp.bfloat16
            )
        offset += rows

    size = patch_ref.shape[1] // PATCH_QUERY_HEADS
    rows = kv_ref.shape[0]
    half_width = PATCH_KEY_HEADS * size
    factor = size ** (-0.5) * LOG2E
    groups = PATCH_QUERY_HEADS // PATCH_KEY_HEADS
    pair = 2 * size
    lane_half = lax.broadcasted_iota(jnp.int32, (slots, pair), 1) // size
    ones = jnp.ones((rows, pair), jnp.bfloat16)
    for kp in range(PATCH_KEY_HEADS // 2):
        keys = kv_ref[:, kp * pair : (kp + 1) * pair]
        values = jnp.concatenate(
            [kv_ref[:, half_width + kp * pair : half_width + (kp + 1) * pair], ones], axis=1
        )
        for half in range(2):
            first = (2 * kp + half) * groups
            queries = []
            for g in range(groups):
                at = (first + g) // 2 * pair
                q = in_ref[:, at : at + pair].astype(jnp.float32)
                if g % 2 != half:
                    q = pltpu.roll(q, size, 1)
                queries.append(jnp.where(lane_half == half, q, 0.0).astype(jnp.bfloat16))
            scores = dot_t(jnp.concatenate(queries, axis=0), keys)
            outs = []
            for g in range(groups):
                part = scores[g * slots : (g + 1) * slots, :] * factor + bias_ref[...]
                peak = jnp.max(part, axis=1, keepdims=True)
                outs.append(jnp.exp2(part - peak).astype(jnp.bfloat16))
            total = dot(jnp.concatenate(outs, axis=0), values)
            mixed = total[:, :pair] / total[:, pair:]
            for g in range(0, groups, 2):
                two = [mixed[(g + i) * slots : (g + i + 1) * slots, :] for i in range(2)]
                two = [t if i == half else pltpu.roll(t, size, 1) for i, t in enumerate(two)]
                at = (first + g) // 2 * pair
                mix_ref[:, at : at + pair] = jnp.where(lane_half == 0, two[0], two[1])

    nbytes = enc_ref.shape[0]
    mix = mix_ref[...]
    scale = lax.rsqrt(jnp.mean(mix * mix, axis=1, keepdims=True) + epsilon)
    alive = jnp.where(start_col_ref[...] < nbytes, 1.0, 0.0)
    patch_ref[...] = (mix * scale * ogain_ref[...] * alive).astype(jnp.bfloat16)

    width = enc_ref.shape[1]
    size = TILE
    factor = size ** (-0.5) * LOG2E
    ones = jnp.ones((slots, size), jnp.bfloat16)
    for start in range(0, nbytes, TILE):
        place = lax.broadcasted_iota(jnp.int32, (TILE, slots), 0) + start
        allowed = start_row_ref[...] <= place
        crosses = []
        squares = jnp.zeros((TILE, size), jnp.float32)
        for h in range(width // size):
            scores = dot_t(
                enc_ref[start : start + TILE, h * size : (h + 1) * size],
                patch_ref[:, 2 * h * size : (2 * h + 1) * size],
            )
            scores = jnp.where(allowed, scores * factor, LOW)
            peak = jnp.max(scores, axis=1, keepdims=True)
            expo = jnp.exp2(scores - peak).astype(jnp.bfloat16)
            values = jnp.concatenate(
                [patch_ref[:, (2 * h + 1) * size : (2 * h + 2) * size], ones], axis=1
            )
            total = dot(expo, values)
            cross = total[:, :size] / total[:, size:]
            squares += cross * cross
            crosses.append(cross)
        scale = lax.rsqrt(jnp.sum(squares, axis=1, keepdims=True) / width + epsilon)
        for h, cross in enumerate(crosses):
            at = h * size
            byte_ref[start : start + TILE, at : at + size] = (
                cross * scale * dgain_ref[:, at : at + size]
            ).astype(jnp.bfloat16)


def patches(at, blocks, weights, plan, n_copies, up_shape, kv_shape, encoded, bias, gains, starts_col, starts_row, n_patch_width):
    rows = sum(b.shape[0] for b in blocks)
    slots = starts_col.shape[0]
    return pl.pallas_call(
        functools.partial(patch_kernel, len(blocks), plan, len(weights)),
        in_specs=[pl.BlockSpec(memory_space=pltpu.SMEM)]
        + [VMEM] * len(blocks)
        + [ANY] * len(weights)
        + [VMEM] * 7,
        out_specs=[VMEM, VMEM],
        out_shape=[
            jax.ShapeDtypeStruct(encoded.shape, jnp.bfloat16),
            jax.ShapeDtypeStruct((slots, n_patch_width), jnp.bfloat16),
        ],
        scratch_shapes=[
            pltpu.VMEM(up_shape, jnp.bfloat16),
            pltpu.VMEM(kv_shape, jnp.bfloat16),
            pltpu.VMEM((rows, kv_shape[1]), jnp.bfloat16),
            pltpu.VMEM((slots, n_patch_width), jnp.float32),
            pltpu.VMEM((slots, n_patch_width), jnp.bfloat16),
            pltpu.SemaphoreType.DMA((n_copies,)),
        ],
        compiler_params=pltpu.CompilerParams(vmem_limit_bytes=48 * 2**20),
        name="patches",
    )(at, *blocks, *weights, encoded, bias, *gains, starts_col, starts_row)


def exchanged(value, axis, mask):
    return lax.ppermute(value, axis, [(i, i ^ mask) for i in range(lax.axis_size(axis))])


def passed_along(value, axis, steps):
    count = lax.axis_size(axis)
    return lax.ppermute(value, axis, [(i, i + steps) for i in range(count - steps)])


def whole_plan(at_ref, weights, up_ref, kv_ref):
    return [(weights[0], up_ref), (weights[1], kv_ref)]


def quarter_plan(at_ref, weights, up_ref, kv_ref):
    z, doc = at_ref[0] // 2, at_ref[1]
    up_rows, up_cols = up_ref.shape[0] // 4, up_ref.shape[1] // 4
    kv_rows, kv_cols = kv_ref.shape[0] // 8, kv_ref.shape[1] // 4
    copies = []
    for i, ref in enumerate(weights):
        block, part = i // 4, i % 4
        zb, q = z ^ block, doc ^ part
        cols = pl.ds(pl.multiple_of(q * up_cols, up_cols), up_cols)
        rows = pl.ds(pl.multiple_of(zb * up_rows, up_rows), up_rows)
        copies.append((ref.at[:up_rows, :], up_ref.at[rows, cols]))
        cols = pl.ds(pl.multiple_of(q * kv_cols, kv_cols), kv_cols)
        for y in range(2):
            rows = pl.ds(pl.multiple_of((2 * zb + y) * kv_rows, kv_rows), kv_rows)
            copies.append((ref.at[up_rows:, y * kv_cols : (y + 1) * kv_cols], kv_ref.at[rows, cols]))
    return copies


def quarter_weights(w_up, w_kv):
    doc = lax.axis_index("doc")
    y = lax.axis_index("seq") % 2
    up = lax.dynamic_slice_in_dim(w_up, doc * (w_up.shape[1] // 4), w_up.shape[1] // 4, 1)
    kv = lax.dynamic_slice_in_dim(w_kv, doc * (w_kv.shape[1] // 4), w_kv.shape[1] // 4, 1)
    n = up.shape[0]
    piece = jnp.concatenate([up, jnp.concatenate([kv[:n], kv[n:]], axis=1)], axis=0)
    other = exchanged(piece, "seq", 1)
    low, high = jnp.where(y == 0, piece, other), jnp.where(y == 0, other, piece)

    def unpacked(p):
        w = p.shape[1] // 2
        return jnp.concatenate([p[n:, :w], p[n:, w:]], axis=0)

    mine = jnp.concatenate(
        [low[:n], high[:n], jnp.concatenate([unpacked(low), unpacked(high)], axis=1)], axis=0
    )
    blocks = [mine] + [exchanged(mine, "seq", 2 * j) for j in range(1, 4)]
    out = []
    for block in blocks:
        across = exchanged(block, "doc", 2)
        out += [block, exchanged(block, "doc", 1), across, exchanged(across, "doc", 1)]
    return out


def per_device(
    byte_q, byte_k, byte_v, byte_gain, pool_query, w_up, patch_gain, w_kv, out_gain, dec_gain,
    patch_start,
):
    nbytes = byte_q.shape[0]
    slots = patch_start.shape[1]
    device = lax.axis_index("seq")
    doc = lax.axis_index("doc")
    n_seq, n_doc = lax.axis_size("seq"), lax.axis_size("doc")
    paired = n_seq == 8 and n_doc == 4

    k_tail = passed_along(byte_k, "seq", 1)
    v_tail = passed_along(byte_v, "seq", 1)
    if paired:
        weights = quarter_weights(w_up, w_kv)
        plan, n_copies = quarter_plan, 3 * len(weights)
    else:
        weights = [lax.all_gather(w, "seq", axis=0, tiled=True) for w in (w_up, w_kv)]
        plan, n_copies = whole_plan, 2

    own, lse = own_attention(byte_q, byte_k, byte_v)
    starts = lax.dynamic_index_in_dim(patch_start, device, 0, keepdims=False)
    ends = jnp.concatenate([starts[1:], jnp.full((1,), nbytes, jnp.int32)])
    row = lambda g: g.astype(jnp.float32)[None, :]
    encoded, pooled = cross_attention(
        (device == 0).astype(jnp.int32)[None], byte_q, k_tail, v_tail, own, lse, row(byte_gain),
        pool_query, starts[:, None], ends[:, None],
    )

    place = jnp.arange(slots, dtype=jnp.int32)
    own_allowed = (place[None, :] <= place[:, None]) & (starts < nbytes)[None, :]
    if paired:
        zs = [exchanged(pooled, "seq", 2 * j) for j in range(1, 4)]
        ys = [exchanged(b, "seq", 1) for b in [pooled] + zs]
        blocks = [pooled] + zs + ys
        order = jnp.stack([device ^ m for m in (2, 4, 6, 1, 3, 5, 7)])
    else:
        blocks = [pooled, lax.all_gather(pooled, "seq", axis=0, tiled=True)]
        order = jnp.arange(n_seq, dtype=jnp.int32)
    live = (patch_start < nbytes)[order] & (order < device)[:, None]
    allowed = jnp.concatenate(
        [own_allowed, jnp.broadcast_to(live.reshape(1, -1), (slots, live.size))], axis=1
    )
    bias = jnp.where(allowed, 0.0, LOW).astype(jnp.float32)
    at = jnp.stack([device, doc]).astype(jnp.int32)
    byte_out, patch_out = patches(
        at, blocks, weights, plan, n_copies,
        (w_up.shape[0] * n_seq, w_up.shape[1]), (w_kv.shape[0] * n_seq, w_kv.shape[1]),
        encoded, bias, [row(patch_gain), row(out_gain), row(dec_gain)],
        starts[:, None], starts[None, :], w_up.shape[1],
    )
    return (byte_out, patch_out)


def solution(mesh):
    placed = (
        P(("doc", "seq"), None),
        P(("doc", "seq"), None),
        P(("doc", "seq"), None),
        P(),
        P(),
        P("seq", None),
        P(),
        P("seq", None),
        P(),
        P(),
        P("doc", None),
    )
    return jax.shard_map(
        per_device,
        mesh=mesh,
        in_specs=placed,
        out_specs=(P(("doc", "seq"), None), P(("doc", "seq"), None)),
        check_vma=False,
    )
```

time: 258 us -> 209 us (0.81)
  waiting for transfers between devices: 158 us -> 80.5 us
  starting transfers between devices: 9.63 us -> 69.4 us
  Pallas kernels: 0 us -> 47.5 us
  matrix products: 44.1 us -> 0 us
  other arithmetic: 20.4 us -> 0.46 us
  between operations: 14 us -> 1.09 us
    all_gather x3 -> x0, waiting for transfers between devices: 112 us -> none  [the longest x1 70.8 us: per_device(): lax.all_gather(w_kv, 'seq', axis=0, tiled=True)]
    ppermute x2 -> x25, starting transfers between devices: 9.51 us -> 69.4 us  [the longest x23 61.6 us: exchanged(): lax.ppermute(value, axis, [(i, i ^ mask) for i in range(lax.axis_size(axi...]
    pallas_call x0 -> x3, Pallas kernels: none -> 47.5 us  [the longest x1 26.9 us: patches(): pl.pallas_call(functools.partial(patch_kernel, len(blocks), plan, len(wei...]
    dot_general x24 -> x0, matrix products: 43.4 us -> none  [the longest x8 15.4 us: one_head(): return jnp.dot(weights, head_value, preferred_element_type=jnp.float32)]
    ppermute x2 -> x25, waiting for transfers between devices: 45.3 us -> 80.5 us  [the longest x23 80.5 us: exchanged(): lax.ppermute(value, axis, [(i, i ^ mask) for i in range(lax.axis_size(axi...]
    reduce_sum x13 -> x0, other arithmetic: 10.5 us -> none  [the longest x8 7.59 us: masked_weights(): return (expo / jnp.sum(expo, axis=-1, keepdims=True)).astype(jnp.bfloat16)]
    concatenate x2, other arithmetic: 6.05 us -> 0.06 us  [the longest x1 0.04 us: quarter_weights(): jnp.concatenate([low[:n], high[:n], jnp.concatenate([unpacked(low), unpac...]
    convert_element_type x10 -> x0, other arithmetic: 3.01 us -> none  [the longest x2 1.31 us: per_device(): (normed(mixed, out_gain) * alive[:, None].astype(jnp.float32)).astype(jnp...]
  transfers between devices with their start and end apart: 5 -> 25, of which waited for: 5 -> 8; matrix products, arithmetic and copies ran while one was open for 21% -> 1% of each run, Pallas kernels for 0% -> 10%
where the time goes in v1:
time: 209 us; the launch traced here: 208 us
  waiting for transfers between devices  80.5 us (39%)
  starting transfers between devices  69.4 us (33%)
  Pallas kernels  47.5 us (23%)
  local copies, waits for them, and re-layouts  9.48 us (5%)
    ppermute x23, waiting for transfers between devices, exchanged(): lax.ppermute(value, axis, [(i, i ^ mask) for i in range(lax.axis_size(axi...  80.5 us
    ppermute x23, starting transfers between devices, exchanged(): lax.ppermute(value, axis, [(i, i ^ mask) for i in range(lax.axis_size(axi...  61.6 us
    pallas_call x1, Pallas kernels, patches(): pl.pallas_call(functools.partial(patch_kernel, len(blocks), plan, len(wei...  26.9 us
    pallas_call x1, Pallas kernels, own_attention(): pl.pallas_call(own_kernel, grid=(width // TILE,), in_specs=[block] * 3, o...  10.6 us
    pallas_call x1, Pallas kernels, cross_attention(): pl.pallas_call(cross_kernel, grid=(width // TILE,), in_specs=[pl.BlockSpe...  9.94 us
    ppermute x2, starting transfers between devices, passed_along(): lax.ppermute(value, axis, [(i, i + steps) for i in range(count - steps)])  7.84 us
    unnamed x30, local copies, waits for them, and re-layouts  7.19 us
  transfers between devices with their start and end apart: 25, of which 8 were waited for; matrix products, arithmetic and copies ran while one was open for 1% of the time, Pallas kernels for 10%

profile of v1, /device:TPU:0, one launch (start us, length us, event | category | flops | bytes accessed | tf_op | source)
XLA Modules:
  0.0 208.4 jit_solution(10013619315844075235)
XLA Ops:
  0.6 0.0 copy-start
  0.7 1.0 copy-done
  1.7 1.0 constant_dynamic-slice_fusion
  2.8 3.0 %collective-permute-start.9 = (bf16[256,512]{1,0:T(8,128)(2,1)S(1)}, bf16[256,512]{1,0:T(8,128)(2,1)S(1)}, u32[]{:S(2)}, u32[]{:S(2)}) collective-permute-start(bf16[256,512]{1,0:T(8,128)(2,1)S(1)} %maximum_maximum_fusion.1), channel_id=1, source_target_pairs={{0,4},{4,0},{8,12},{12,8},{16,20},{20,16},{24,28},{28,24},{1,5},{5... | collective-permute-start | bytes 786440 | tf_op jit(solution)/shard_map/ppermute | solution.py:298
  5.8 2.9 %collective-permute-start = (bf16[512,1024]{1,0:T(8,128)(2,1)}, bf16[512,1024]{1,0:T(8,128)(2,1)}, u32[]{:S(2)}, u32[]{:S(2)}) collective-permute-start(bf16[512,1024]{1,0:T(8,128)(2,1)} %k_ref.1), channel_id=1, source_target_pairs={{0,4},{4,8},{8,12},{12,16},{16,20},{20,24},{24,28},{1,5},{5,9},{9,... | collective-permute-start | bytes 3145736 | tf_op jit(solution)/shard_map/ppermute | solution.py:303
  8.7 4.9 %collective-permute-start.1 = (bf16[512,1024]{1,0:T(8,128)(2,1)}, bf16[512,1024]{1,0:T(8,128)(2,1)}, u32[]{:S(2)}, u32[]{:S(2)}) collective-permute-start(bf16[512,1024]{1,0:T(8,128)(2,1)} %v_ref.1), channel_id=1, source_target_pairs={{0,4},{4,8},{8,12},{12,16},{16,20},{20,24},{24,28},{1,5},{5,9},{9,... | collective-permute-start | bytes 3145736 | tf_op jit(solution)/shard_map/ppermute | solution.py:303
  13.6 0.0 collective-permute-done.9
  13.6 0.1 broadcast_select_fusion.1
  13.8 0.0 copy-start.13
  13.8 0.0 copy-start.10
  13.8 0.0 copy-start.7
  13.9 1.6 collective-permute-start.11
  15.4 45.1 %collective-permute-start.13 = (bf16[512,512]{1,0:T(8,128)(2,1)S(1)}, bf16[512,512]{1,0:T(8,128)(2,1)}, u32[]{:S(2)}, u32[]{:S(2)}) collective-permute-start(bf16[512,512]{1,0:T(8,128)(2,1)S(1)} %maximum_maximum_fusion.refs_8_), channel_id=1, source_target_pairs={{0,8},{4,12},{8,0},{12,4},{16,24},{20,28},{24,16},{28,20},{1,9},{5... | collective-permute-start | bytes 1572872 | tf_op jit(solution)/shard_map/ppermute | solution.py:298
  60.5 0.0 collective-permute-start.10
  60.6 0.0 copy-start.5
  60.6 1.2 copy-done.5
  61.8 10.6 %own_attention.1 = (f32[512,1024]{1,0:T(8,128)S(1)}, f32[512,128]{1,0:T(8,128)S(1)}) custom-call(bf16[512,1024]{1,0:T(8,128)(2,1)S(1)} %copy-done.1, bf16[512,1024]{1,0:T(8,128)(2,1)S(1)} %copy-done.4, bf16[512,1024]{1,0:T(8,128)(2,1)S(1)} %copy-done.5), custom_call_target="tpu_custom_call" | custom-call | tf_op jit(solution)/shard_map/own_attention/pallas_call | solution.py:54
  72.4 1.3 copy-done.2
  73.8 0.1 copy.13.start_ref.refs_29_
  73.9 2.7 %collective-permute-start.17 = (bf16[512,512]{1,0:T(8,128)(2,1)S(1)}, bf16[512,512]{1,0:T(8,128)(2,1)}, u32[]{:S(2)}, u32[]{:S(2)}) collective-permute-start(bf16[512,512]{1,0:T(8,128)(2,1)S(1)} %maximum_maximum_fusion.refs_8_), channel_id=1, source_target_pairs={{0,16},{4,20},{8,24},{12,28},{16,0},{20,4},{24,8},{28,12},{1,17},{... | collective-permute-start | bytes 1572872 | tf_op jit(solution)/shard_map/ppermute | solution.py:298
  76.5 0.0 collective-permute-done.13.refs_12_
  76.5 0.1 collective-permute-start.21
  76.6 0.1 slice_bitcast_fusion
  76.7 0.0 collective-permute-done.k_ref
  76.7 0.2 collective-permute-start.12
  76.9 0.1 add_bitcast_fusion
  77.0 0.1 copy.14.next_ref
  77.1 0.0 collective-permute-done.1.v_ref
  77.1 0.4 collective-permute-start.14
  77.4 1.6 copy-done.3
  79.0 9.9 %cross_attention.1 = (bf16[512,1024]{1,0:T(8,128)(2,1)S(1)}, bf16[80,1024]{1,0:T(8,128)(2,1)}) custom-call(s32[1]{0:T(128)} %bitcast.2.lead_ref, bf16[512,1024]{1,0:T(8,128)(2,1)S(1)} %copy-done.1, bf16[512,1024]{1,0:T(8,128)(2,1)} %collective-permute-done.k_ref, bf16[512,1024]{1,0:T(8,128)(2,1)} %collective-permute-done.1.v_ref, f32[512,1024]{1,0:T(8,128)S(1)} %copy-done.3, ...), custom_call_target="tpu_custom_call" | custom-call | tf_op jit(solution)/shard_map/cross_attention/pallas_call | solution.py:138
  89.0 1.0 copy-done.6
  90.0 0.0 collective-permute-done.10.refs_9_
  90.0 0.8 collective-permute-start.2
  90.8 0.1 stack.59
  90.9 0.1 stack.67
  91.0 20.8 %collective-permute-done.17.refs_16_ = bf16[512,512]{1,0:T(8,128)(2,1)} collective-permute-done((bf16[512,512]{1,0:T(8,128)(2,1)S(1)}, bf16[512,512]{1,0:T(8,128)(2,1)}, u32[]{:S(2)}, u32[]{:S(2)}) %collective-permute-start.17) | collective-permute-done | bytes 524320 | tf_op jit(solution)/shard_map/ppermute | solution.py:298
  111.8 0.0 collective-permute-start.3
  111.8 0.0 collective-permute-done.21.refs_20_
  111.8 3.0 %collective-permute-start.4 = (bf16[80,1024]{1,0:T(8,128)(2,1)}, bf16[80,1024]{1,0:T(8,128)(2,1)S(1)}, u32[]{:S(2)}, u32[]{:S(2)}) collective-permute-start(bf16[80,1024]{1,0:T(8,128)(2,1)} %get-tuple-element.8.refs_0_), channel_id=1, source_target_pairs={{0,24},{4,28},{8,16},{12,20},{16,8},{20,12},{24,0},{28,4},{1,25},{... | collective-permute-start | bytes 491528 | tf_op jit(solution)/shard_map/ppermute | solution.py:298
  114.8 0.3 collective-permute-done.2.refs_1_
  115.1 0.0 collective-permute-start.5
  115.1 18.3 %collective-permute-done.3.refs_2_ = bf16[80,1024]{1,0:T(8,128)(2,1)S(1)} collective-permute-done((bf16[80,1024]{1,0:T(8,128)(2,1)}, bf16[80,1024]{1,0:T(8,128)(2,1)S(1)}, u32[]{:S(2)}, u32[]{:S(2)}) %collective-permute-start.3) | collective-permute-done | bytes 163872 | tf_op jit(solution)/shard_map/ppermute | solution.py:298
  133.4 0.5 collective-permute-start.15
  134.0 1.6 collective-permute-start.19
  135.5 0.0 collective-permute-done.12.refs_11_
  135.5 0.5 collective-permute-start.23
  136.1 0.0 collective-permute-done.14.refs_13_
  136.1 0.1 collective-permute-start.22
  136.2 0.6 gather_fusion
  136.7 0.1 broadcast_and_fusion
  136.8 0.1 reshape.364
  136.9 0.1 pad.1.clone
  137.0 11.4 %collective-permute-done.15.refs_14_ = bf16[512,512]{1,0:T(8,128)(2,1)S(1)} collective-permute-done((bf16[512,512]{1,0:T(8,128)(2,1)}, bf16[512,512]{1,0:T(8,128)(2,1)S(1)}, u32[]{:S(2)}, u32[]{:S(2)}) %collective-permute-start.15) | collective-permute-done | bytes 524320 | tf_op jit(solution)/shard_map/ppermute | solution.py:298
  148.4 11.3 %collective-permute-done.19.refs_18_ = bf16[512,512]{1,0:T(8,128)(2,1)} collective-permute-done((bf16[512,512]{1,0:T(8,128)(2,1)}, bf16[512,512]{1,0:T(8,128)(2,1)}, u32[]{:S(2)}, u32[]{:S(2)}) %collective-permute-start.19) | collective-permute-done | bytes 524320 | tf_op jit(solution)/shard_map/ppermute | solution.py:298
  159.8 10.3 %collective-permute-done.23.refs_22_ = bf16[512,512]{1,0:T(8,128)(2,1)} collective-permute-done((bf16[512,512]{1,0:T(8,128)(2,1)}, bf16[512,512]{1,0:T(8,128)(2,1)}, u32[]{:S(2)}, u32[]{:S(2)}) %collective-permute-start.23) | collective-permute-done | bytes 524320 | tf_op jit(solution)/shard_map/ppermute | solution.py:298
  170.1 0.1 collective-permute-start.7
  170.2 2.0 collective-permute-start.8
  172.3 0.1 pad_add_fusion.at_ref
  172.4 4.8 %collective-permute-done.7.refs_6_ = bf16[80,1024]{1,0:T(8,128)(2,1)S(1)} collective-permute-done((bf16[80,1024]{1,0:T(8,128)(2,1)S(1)}, bf16[80,1024]{1,0:T(8,128)(2,1)S(1)}, u32[]{:S(2)}, u32[]{:S(2)}) %collective-permute-start.7) | collective-permute-done | bytes 163872 | tf_op jit(solution)/shard_map/ppermute | solution.py:298
  177.2 3.1 %collective-permute-done.8.refs_7_ = bf16[80,1024]{1,0:T(8,128)(2,1)S(1)} collective-permute-done((bf16[80,1024]{1,0:T(8,128)(2,1)S(1)}, bf16[80,1024]{1,0:T(8,128)(2,1)S(1)}, u32[]{:S(2)}, u32[]{:S(2)}) %collective-permute-start.8) | collective-permute-done | bytes 163872 | tf_op jit(solution)/shard_map/ppermute | solution.py:298
  180.3 0.8 copy-done.8
  181.1 0.2 copy-done.9
  181.3 26.9 %patches.1 = (bf16[512,1024]{1,0:T(8,128)(2,1)}, bf16[80,2048]{1,0:T(8,128)(2,1)}) custom-call(s32[2]{0:T(128)S(1)} %pad_add_fusion.at_ref, bf16[80,1024]{1,0:T(8,128)(2,1)} %get-tuple-element.8.refs_0_, bf16[80,1024]{1,0:T(8,128)(2,1)S(1)} %collective-permute-done.2.refs_1_, bf16[80,1024]{1,0:T(8,128)(2,1)S(1)} %collective-permute-done.3.refs_2_, ...), custom_call_target="tpu_custom_call" | custom-call | tf_op jit(solution)/shard_map/patches/pallas_call | solution.py:273
  (49 shorter events, 0.3 us)
Async XLA Ops:
  0.6 1.0 copy-start
  1.7 58.9 %copy-start.1 = (bf16[512,1024]{1,0:T(8,128)(2,1)S(1)}, bf16[512,1024]{1,0:T(8,128)(2,1)}, u32[]{:S(2)}) copy-start(bf16[512,1024]{1,0:T(8,128)(2,1)} %q_ref.3) | copy-start | bytes 3145732
  1.7 58.9 %copy-start.4 = (bf16[512,1024]{1,0:T(8,128)(2,1)S(1)}, bf16[512,1024]{1,0:T(8,128)(2,1)}, u32[]{:S(2)}) copy-start(bf16[512,1024]{1,0:T(8,128)(2,1)} %k_ref.1) | copy-start | bytes 3145732
  2.8 10.9 %collective-permute-start.9 = (bf16[256,512]{1,0:T(8,128)(2,1)S(1)}, bf16[256,512]{1,0:T(8,128)(2,1)S(1)}, u32[]{:S(2)}, u32[]{:S(2)}) collective-permute-start(bf16[256,512]{1,0:T(8,128)(2,1)S(1)} %maximum_maximum_fusion.1), channel_id=1, source_target_pairs={{0,4},{4,0},{8,12},{12,8},{16,20},{20,16},{24,28},{28,24},{1,5},{5... | collective-permute-start | bytes 786440 | tf_op jit(solution)/shard_map/ppermute | solution.py:298
  5.8 70.9 %collective-permute-start = (bf16[512,1024]{1,0:T(8,128)(2,1)}, bf16[512,1024]{1,0:T(8,128)(2,1)}, u32[]{:S(2)}, u32[]{:S(2)}) collective-permute-start(bf16[512,1024]{1,0:T(8,128)(2,1)} %k_ref.1), channel_id=1, source_target_pairs={{0,4},{4,8},{8,12},{12,16},{16,20},{20,24},{24,28},{1,5},{5,9},{9,... | collective-permute-start | bytes 3145736 | tf_op jit(solution)/shard_map/ppermute | solution.py:303
  8.7 68.4 %collective-permute-start.1 = (bf16[512,1024]{1,0:T(8,128)(2,1)}, bf16[512,1024]{1,0:T(8,128)(2,1)}, u32[]{:S(2)}, u32[]{:S(2)}) collective-permute-start(bf16[512,1024]{1,0:T(8,128)(2,1)} %v_ref.1), channel_id=1, source_target_pairs={{0,4},{4,8},{8,12},{12,16},{16,20},{20,24},{24,28},{1,5},{5,9},{9,... | collective-permute-start | bytes 3145736 | tf_op jit(solution)/shard_map/ppermute | solution.py:303
  13.8 59.9 %copy-start.13 = (bf16[1024]{0:T(1024)(128)(2,1)S(1)}, bf16[1024]{0:T(1024)(128)(2,1)}, u32[]{:S(2)}) copy-start(bf16[1024]{0:T(1024)(128)(2,1)} %param.14) | copy-start | bytes 6148
  13.8 59.9 %copy-start.10 = (s32[8,80]{1,0:T(8,128)S(1)}, s32[8,80]{1,0:T(8,128)}, u32[]{:S(2)}) copy-start(s32[8,80]{1,0:T(8,128)} %param.21) | copy-start | bytes 7684
  13.8 63.6 %copy-start.7 = (bf16[8,128]{1,0:T(8,128)(2,1)S(1)}, bf16[8,128]{1,0:T(8,128)(2,1)}, u32[]{:S(2)}) copy-start(bf16[8,128]{1,0:T(8,128)(2,1)} %query_ref.1) | copy-start | bytes 6148
  13.9 60.0 %collective-permute-start.11 = (bf16[512,512]{1,0:T(8,128)(2,1)S(1)}, bf16[512,512]{1,0:T(8,128)(2,1)}, u32[]{:S(2)}, u32[]{:S(2)}) collective-permute-start(bf16[512,512]{1,0:T(8,128)(2,1)S(1)} %maximum_maximum_fusion.refs_8_), channel_id=1, source_target_pairs={{0,2},{1,3},{2,0},{3,1},{4,6},{5,7},{6,4},{7,5},{8,10},{9,11},{10,... | collective-permute-start | bytes 1572872 | tf_op jit(solution)/shard_map/ppermute | solution.py:298
  15.4 61.1 %collective-permute-start.13 = (bf16[512,512]{1,0:T(8,128)(2,1)S(1)}, bf16[512,512]{1,0:T(8,128)(2,1)}, u32[]{:S(2)}, u32[]{:S(2)}) collective-permute-start(bf16[512,512]{1,0:T(8,128)(2,1)S(1)} %maximum_maximum_fusion.refs_8_), channel_id=1, source_target_pairs={{0,8},{4,12},{8,0},{12,4},{16,24},{20,28},{24,16},{28,20},{1,9},{5... | collective-permute-start | bytes 1572872 | tf_op jit(solution)/shard_map/ppermute | solution.py:298
  60.5 29.4 %collective-permute-start.10 = (bf16[512,512]{1,0:T(8,128)(2,1)S(1)}, bf16[512,512]{1,0:T(8,128)(2,1)}, u32[]{:S(2)}, u32[]{:S(2)}) collective-permute-start(bf16[512,512]{1,0:T(8,128)(2,1)S(1)} %maximum_maximum_fusion.refs_8_), channel_id=1, source_target_pairs={{0,1},{1,0},{2,3},{3,2},{4,5},{5,4},{6,7},{7,6},{8,9},{9,8},{10,11... | collective-permute-start | bytes 1572872 | tf_op jit(solution)/shard_map/ppermute | solution.py:298
  60.6 1.2 copy-start.5
  72.4 1.4 copy-start.2
  73.9 37.9 %collective-permute-start.17 = (bf16[512,512]{1,0:T(8,128)(2,1)S(1)}, bf16[512,512]{1,0:T(8,128)(2,1)}, u32[]{:S(2)}, u32[]{:S(2)}) collective-permute-start(bf16[512,512]{1,0:T(8,128)(2,1)S(1)} %maximum_maximum_fusion.refs_8_), channel_id=1, source_target_pairs={{0,16},{4,20},{8,24},{12,28},{16,0},{20,4},{24,8},{28,12},{1,17},{... | collective-permute-start | bytes 1572872 | tf_op jit(solution)/shard_map/ppermute | solution.py:298
  76.5 35.3 %collective-permute-start.21 = (bf16[512,512]{1,0:T(8,128)(2,1)S(1)}, bf16[512,512]{1,0:T(8,128)(2,1)}, u32[]{:S(2)}, u32[]{:S(2)}) collective-permute-start(bf16[512,512]{1,0:T(8,128)(2,1)S(1)} %maximum_maximum_fusion.refs_8_), channel_id=1, source_target_pairs={{0,24},{4,28},{8,16},{12,20},{16,8},{20,12},{24,0},{28,4},{1,25},{... | collective-permute-start | bytes 1572872 | tf_op jit(solution)/shard_map/ppermute | solution.py:298
  76.7 58.9 %collective-permute-start.12 = (bf16[512,512]{1,0:T(8,128)(2,1)}, bf16[512,512]{1,0:T(8,128)(2,1)S(1)}, u32[]{:S(2)}, u32[]{:S(2)}) collective-permute-start(bf16[512,512]{1,0:T(8,128)(2,1)} %collective-permute-done.11.refs_10_), channel_id=1, source_target_pairs={{0,1},{1,0},{2,3},{3,2},{4,5},{5,4},{6,7},{7,6},{8,9},{9,8},{10,11... | collective-permute-start | bytes 1572872 | tf_op jit(solution)/shard_map/ppermute | solution.py:298
  77.1 59.0 %collective-permute-start.14 = (bf16[512,512]{1,0:T(8,128)(2,1)}, bf16[512,512]{1,0:T(8,128)(2,1)S(1)}, u32[]{:S(2)}, u32[]{:S(2)}) collective-permute-start(bf16[512,512]{1,0:T(8,128)(2,1)} %collective-permute-done.13.refs_12_), channel_id=1, source_target_pairs={{0,1},{1,0},{2,3},{3,2},{4,5},{5,4},{6,7},{7,6},{8,9},{9,8},{10,11... | collective-permute-start | bytes 1572872 | tf_op jit(solution)/shard_map/ppermute | solution.py:298
  77.4 1.6 copy-start.3
  79.0 93.2 %copy-start.11 = (bf16[2048]{0:T(1024)(128)(2,1)S(1)}, bf16[2048]{0:T(1024)(128)(2,1)}, u32[]{:S(2)}) copy-start(bf16[2048]{0:T(1024)(128)(2,1)} %param.17) | copy-start | bytes 12292
  79.0 93.2 %copy-start.12 = (bf16[2048]{0:T(1024)(128)(2,1)S(1)}, bf16[2048]{0:T(1024)(128)(2,1)}, u32[]{:S(2)}) copy-start(bf16[2048]{0:T(1024)(128)(2,1)} %param.19) | copy-start | bytes 12292
  79.0 93.2 %copy-start.14 = (bf16[1024]{0:T(1024)(128)(2,1)S(1)}, bf16[1024]{0:T(1024)(128)(2,1)}, u32[]{:S(2)}) copy-start(bf16[1024]{0:T(1024)(128)(2,1)} %param.20) | copy-start | bytes 6148
  89.0 1.0 copy-start.6
  90.0 25.1 %collective-permute-start.2 = (bf16[80,1024]{1,0:T(8,128)(2,1)}, bf16[80,1024]{1,0:T(8,128)(2,1)S(1)}, u32[]{:S(2)}, u32[]{:S(2)}) collective-permute-start(bf16[80,1024]{1,0:T(8,128)(2,1)} %get-tuple-element.8.refs_0_), channel_id=1, source_target_pairs={{0,8},{4,12},{8,0},{12,4},{16,24},{20,28},{24,16},{28,20},{1,9},{5... | collective-permute-start | bytes 491528 | tf_op jit(solution)/shard_map/ppermute | solution.py:298
  111.8 21.6 %collective-permute-start.3 = (bf16[80,1024]{1,0:T(8,128)(2,1)}, bf16[80,1024]{1,0:T(8,128)(2,1)S(1)}, u32[]{:S(2)}, u32[]{:S(2)}) collective-permute-start(bf16[80,1024]{1,0:T(8,128)(2,1)} %get-tuple-element.8.refs_0_), channel_id=1, source_target_pairs={{0,16},{4,20},{8,24},{12,28},{16,0},{20,4},{24,8},{28,12},{1,17},{... | collective-permute-start | bytes 491528 | tf_op jit(solution)/shard_map/ppermute | solution.py:298
  111.8 22.2 %collective-permute-start.4 = (bf16[80,1024]{1,0:T(8,128)(2,1)}, bf16[80,1024]{1,0:T(8,128)(2,1)S(1)}, u32[]{:S(2)}, u32[]{:S(2)}) collective-permute-start(bf16[80,1024]{1,0:T(8,128)(2,1)} %get-tuple-element.8.refs_0_), channel_id=1, source_target_pairs={{0,24},{4,28},{8,16},{12,20},{16,8},{20,12},{24,0},{28,4},{1,25},{... | collective-permute-start | bytes 491528 | tf_op jit(solution)/shard_map/ppermute | solution.py:298
  115.1 18.9 %collective-permute-start.5 = (bf16[80,1024]{1,0:T(8,128)(2,1)}, bf16[80,1024]{1,0:T(8,128)(2,1)S(1)}, u32[]{:S(2)}, u32[]{:S(2)}) collective-permute-start(bf16[80,1024]{1,0:T(8,128)(2,1)} %get-tuple-element.8.refs_0_), channel_id=1, source_target_pairs={{0,4},{4,0},{8,12},{12,8},{16,20},{20,16},{24,28},{28,24},{1,5},{5... | collective-permute-start | bytes 491528 | tf_op jit(solution)/shard_map/ppermute | solution.py:298
  133.4 15.0 %collective-permute-start.15 = (bf16[512,512]{1,0:T(8,128)(2,1)}, bf16[512,512]{1,0:T(8,128)(2,1)S(1)}, u32[]{:S(2)}, u32[]{:S(2)}) collective-permute-start(bf16[512,512]{1,0:T(8,128)(2,1)} %collective-permute-done.13.refs_12_), channel_id=1, source_target_pairs={{0,2},{1,3},{2,0},{3,1},{4,6},{5,7},{6,4},{7,5},{8,10},{9,11},{10,... | collective-permute-start | bytes 1572872 | tf_op jit(solution)/shard_map/ppermute | solution.py:298
  134.0 14.5 %collective-permute-start.18 = (bf16[512,512]{1,0:T(8,128)(2,1)}, bf16[512,512]{1,0:T(8,128)(2,1)}, u32[]{:S(2)}, u32[]{:S(2)}) collective-permute-start(bf16[512,512]{1,0:T(8,128)(2,1)} %collective-permute-done.17.refs_16_), channel_id=1, source_target_pairs={{0,1},{1,0},{2,3},{3,2},{4,5},{5,4},{6,7},{7,6},{8,9},{9,8},{10,11... | collective-permute-start | bytes 1572872 | tf_op jit(solution)/shard_map/ppermute | solution.py:298
  134.0 25.8 %collective-permute-start.19 = (bf16[512,512]{1,0:T(8,128)(2,1)}, bf16[512,512]{1,0:T(8,128)(2,1)}, u32[]{:S(2)}, u32[]{:S(2)}) collective-permute-start(bf16[512,512]{1,0:T(8,128)(2,1)} %collective-permute-done.17.refs_16_), channel_id=1, source_target_pairs={{0,2},{1,3},{2,0},{3,1},{4,6},{5,7},{6,4},{7,5},{8,10},{9,11},{10,... | collective-permute-start | bytes 1572872 | tf_op jit(solution)/shard_map/ppermute | solution.py:298
  135.5 34.5 %collective-permute-start.23 = (bf16[512,512]{1,0:T(8,128)(2,1)}, bf16[512,512]{1,0:T(8,128)(2,1)}, u32[]{:S(2)}, u32[]{:S(2)}) collective-permute-start(bf16[512,512]{1,0:T(8,128)(2,1)} %collective-permute-done.21.refs_20_), channel_id=1, source_target_pairs={{0,2},{1,3},{2,0},{3,1},{4,6},{5,7},{6,4},{7,5},{8,10},{9,11},{10,... | collective-permute-start | bytes 1572872 | tf_op jit(solution)/shard_map/ppermute | solution.py:298
  136.1 34.0 %collective-permute-start.22 = (bf16[512,512]{1,0:T(8,128)(2,1)}, bf16[512,512]{1,0:T(8,128)(2,1)}, u32[]{:S(2)}, u32[]{:S(2)}) collective-permute-start(bf16[512,512]{1,0:T(8,128)(2,1)} %collective-permute-done.21.refs_20_), channel_id=1, source_target_pairs={{0,1},{1,0},{2,3},{3,2},{4,5},{5,4},{6,7},{7,6},{8,9},{9,8},{10,11... | collective-permute-start | bytes 1572872 | tf_op jit(solution)/shard_map/ppermute | solution.py:298
  148.4 21.8 %collective-permute-start.6 = (bf16[80,1024]{1,0:T(8,128)(2,1)S(1)}, bf16[80,1024]{1,0:T(8,128)(2,1)S(1)}, u32[]{:S(2)}, u32[]{:S(2)}) collective-permute-start(bf16[80,1024]{1,0:T(8,128)(2,1)S(1)} %collective-permute-done.2.refs_1_), channel_id=1, source_target_pairs={{0,4},{4,0},{8,12},{12,8},{16,20},{20,16},{24,28},{28,24},{1,5},{5... | collective-permute-start | bytes 491528 | tf_op jit(solution)/shard_map/ppermute | solution.py:298
  148.4 31.9 %collective-permute-start.16 = (bf16[512,512]{1,0:T(8,128)(2,1)S(1)}, bf16[512,512]{1,0:T(8,128)(2,1)S(1)}, u32[]{:S(2)}, u32[]{:S(2)}) collective-permute-start(bf16[512,512]{1,0:T(8,128)(2,1)S(1)} %collective-permute-done.15.refs_14_), channel_id=1, source_target_pairs={{0,1},{1,0},{2,3},{3,2},{4,5},{5,4},{6,7},{7,6},{8,9},{9,8},{10,11... | collective-permute-start | bytes 1572872 | tf_op jit(solution)/shard_map/ppermute | solution.py:298
  159.8 20.6 %collective-permute-start.20 = (bf16[512,512]{1,0:T(8,128)(2,1)}, bf16[512,512]{1,0:T(8,128)(2,1)S(1)}, u32[]{:S(2)}, u32[]{:S(2)}) collective-permute-start(bf16[512,512]{1,0:T(8,128)(2,1)} %collective-permute-done.19.refs_18_), channel_id=1, source_target_pairs={{0,1},{1,0},{2,3},{3,2},{4,5},{5,4},{6,7},{7,6},{8,9},{9,8},{10,11... | collective-permute-start | bytes 1572872 | tf_op jit(solution)/shard_map/ppermute | solution.py:298
  170.1 10.2 %collective-permute-start.24 = (bf16[512,512]{1,0:T(8,128)(2,1)}, bf16[512,512]{1,0:T(8,128)(2,1)S(1)}, u32[]{:S(2)}, u32[]{:S(2)}) collective-permute-start(bf16[512,512]{1,0:T(8,128)(2,1)} %collective-permute-done.23.refs_22_), channel_id=1, source_target_pairs={{0,1},{1,0},{2,3},{3,2},{4,5},{5,4},{6,7},{7,6},{8,9},{9,8},{10,11... | collective-permute-start | bytes 1572872 | tf_op jit(solution)/shard_map/ppermute | solution.py:298
  170.1 7.1 %collective-permute-start.7 = (bf16[80,1024]{1,0:T(8,128)(2,1)S(1)}, bf16[80,1024]{1,0:T(8,128)(2,1)S(1)}, u32[]{:S(2)}, u32[]{:S(2)}) collective-permute-start(bf16[80,1024]{1,0:T(8,128)(2,1)S(1)} %collective-permute-done.3.refs_2_), channel_id=1, source_target_pairs={{0,4},{4,0},{8,12},{12,8},{16,20},{20,16},{24,28},{28,24},{1,5},{5... | collective-permute-start | bytes 491528 | tf_op jit(solution)/shard_map/ppermute | solution.py:298
  170.2 10.1 %collective-permute-start.8 = (bf16[80,1024]{1,0:T(8,128)(2,1)S(1)}, bf16[80,1024]{1,0:T(8,128)(2,1)S(1)}, u32[]{:S(2)}, u32[]{:S(2)}) collective-permute-start(bf16[80,1024]{1,0:T(8,128)(2,1)S(1)} %collective-permute-done.4.refs_3_), channel_id=1, source_target_pairs={{0,4},{4,0},{8,12},{12,8},{16,20},{20,16},{24,28},{28,24},{1,5},{5... | collective-permute-start | bytes 491528 | tf_op jit(solution)/shard_map/ppermute | solution.py:298
  180.3 0.8 copy-start.8
  180.3 1.0 copy-start.9

commit v2 on v1

--- a/solution.py
+++ b/solution.py
@@ -14,6 +14,7 @@
 TILE = 128
 epsilon = 1e-06
 VMEM = pl.BlockSpec(memory_space=pltpu.VMEM)
+SMALL = pl.CostEstimate(flops=1, bytes_accessed=1, transcendentals=0)
 ANY = pl.BlockSpec(memory_space=pl.ANY)
 
 
@@ -23,6 +24,23 @@
 
 def dot(a, b):
     return jnp.dot(a, b, preferred_element_type=jnp.float32)
+
+
+def split(value):
+    high = value.astype(jnp.bfloat16)
+    rest = value - high.astype(jnp.float32)
+    middle = rest.astype(jnp.bfloat16)
+    return high, middle, (rest - middle.astype(jnp.float32)).astype(jnp.bfloat16)
+
+
+def keep_lse(ref, base, rows, head, lse):
+    n = (ref.shape[0] - base) // 4
+    across = jnp.transpose(lse)[: 4 * n, :]
+    row = lax.broadcasted_iota(jnp.int32, across.shape, 0)
+    kept = jnp.where(head == 0, 0.0, ref[base:, rows].astype(jnp.float32))
+    for i, term in enumerate(split(across)):
+        kept = jnp.where(row == head + i * n, term.astype(jnp.float32), kept)
+    ref[base:, rows] = kept.astype(jnp.bfloat16)
 
 
 def own_kernel(q_ref, k_ref, v_ref, mix_ref, lse_ref):
@@ -33,7 +51,6 @@
     col = lax.broadcasted_iota(jnp.int32, (TILE, TILE), 1)
     causal = col <= row
     values = jnp.concatenate([v_ref[...], jnp.ones((nbytes, size), jnp.bfloat16)], axis=1)
-    lane = lax.broadcasted_iota(jnp.int32, (TILE, TILE), 1)
 
     for start in range(0, nbytes, TILE):
         end = start + TILE
@@ -44,8 +61,7 @@
         expo = jnp.exp2((scores - peak) * factor).astype(jnp.bfloat16)
         total = dot(expo, values[:end])
         mix_ref[start:end, :] = total[:, :size] / total[:, size:]
-        lse = peak * factor + jnp.log2(total[:, size:])
-        lse_ref[start:end, :] = jnp.where(lane == head, lse, lse_ref[start:end, :])
+        keep_lse(lse_ref, 0, slice(start, end), head, peak * factor + jnp.log2(total[:, size:]))
 
 
 def own_attention(q, k, v):
@@ -55,110 +71,135 @@
         own_kernel,
         grid=(width // TILE,),
         in_specs=[block] * 3,
-        out_specs=[block, pl.BlockSpec((nbytes, TILE), lambda h: (0, 0))],
+        out_specs=[block, pl.BlockSpec((4 * (width // TILE), nbytes), lambda h: (0, 0))],
         out_shape=[
             jax.ShapeDtypeStruct((nbytes, width), jnp.float32),
-            jax.ShapeDtypeStruct((nbytes, TILE), jnp.float32),
+            jax.ShapeDtypeStruct((4 * (width // TILE), nbytes), jnp.bfloat16),
         ],
+        cost_estimate=SMALL,
         compiler_params=pltpu.CompilerParams(vmem_limit_bytes=24 * 2**20),
         name="own_attention",
     )(q, k, v)
 
 
-def cross_kernel(
-    lead_ref, q_ref, k_ref, v_ref, own_ref, lse_ref, gain_ref, query_ref, start_ref, next_ref,
-    enc_ref, pooled_ref, mix_ref,
-):
+def cross_kernel(q_ref, k_ref, v_ref, out_ref):
     head = pl.program_id(0)
-    heads = pl.num_programs(0)
     nbytes, size = q_ref.shape
-    slots = start_ref.shape[0]
-    width = mix_ref.shape[1]
     factor = size ** (-0.5) * LOG2E
     row = lax.broadcasted_iota(jnp.int32, (TILE, TILE), 0)
     col = lax.broadcasted_iota(jnp.int32, (TILE, TILE), 1)
-    later = (col > row) & (lead_ref[0] == 0)
-    bias = jnp.where(lead_ref[0] == 0, 0.0, LOW)
     values = jnp.concatenate([v_ref[...], jnp.ones((nbytes, size), jnp.bfloat16)], axis=1)
-    lane = lax.broadcasted_iota(jnp.int32, (TILE, TILE), 1)
+    columns = pl.ds(pl.multiple_of(head * size, size), size)
 
     for start in range(0, nbytes, TILE):
         end = start + TILE
         scores = dot_t(q_ref[start:end, :], k_ref[start:, :])
-        first = jnp.where(later, scores[:, :TILE], LOW)
-        if end < nbytes:
-            scores = jnp.concatenate([first, scores[:, TILE:] + bias], axis=1)
-        else:
-            scores = first
-        lse = jnp.sum(jnp.where(lane == head, lse_ref[start:end, :], 0.0), axis=1, keepdims=True)
-        peak = jnp.maximum(jnp.max(scores, axis=1, keepdims=True) * factor, lse)
-        expo = jnp.exp2(scores * factor - peak).astype(jnp.bfloat16)
-        total = dot(expo, values[start:])
-        share = jnp.exp2(lse - peak)
-        columns = pl.ds(pl.multiple_of(head * size, size), size)
-        mix_ref[start:end, columns] = (own_ref[start:end, :] * share + total[:, :size]) / (
-            share + total[:, size:]
-        )
-
-    @pl.when(head == heads - 1)
-    def _():
-        for start in range(0, nbytes, TILE):
-            end = start + TILE
-            mix = mix_ref[start:end, :]
-            scale = lax.rsqrt(jnp.mean(mix * mix, axis=1, keepdims=True) + epsilon)
-            enc_ref[start:end, :] = (mix * scale * gain_ref[...]).astype(jnp.bfloat16)
-        enc = enc_ref[...]
-        n_heads = query_ref.shape[0]
-        wide = jnp.concatenate([query_ref[...].astype(jnp.float32)] * n_heads, axis=1)
-        head_row = lax.broadcasted_iota(jnp.int32, wide.shape, 0)
-        head_col = lax.broadcasted_iota(jnp.int32, wide.shape, 1) // size
-        wide = jnp.where(head_row == head_col, wide, 0.0).astype(jnp.bfloat16)
-        scores = dot_t(wide, enc) * factor
-        place = lax.broadcasted_iota(jnp.int32, (slots, nbytes), 1)
-        member = (place >= start_ref[...]) & (place < next_ref[...])
-        for h in range(n_heads):
-            inside = jnp.where(member, scores[h : h + 1, :], LOW)
-            peak = jnp.max(inside, axis=1, keepdims=True)
-            expo = jnp.where(member, jnp.exp2(inside - peak), 0.0)
-            total = jnp.sum(expo, axis=1, keepdims=True)
-            weights = (expo * jnp.where(total > 0, 1.0 / total, 0.0)).astype(jnp.bfloat16)
-            pooled_ref[:, h * size : (h + 1) * size] = dot(
-                weights, enc[:, h * size : (h + 1) * size]
-            ).astype(jnp.bfloat16)
-
-
-def cross_attention(leading, q, k, v, own, lse, gain, pool_query, starts, ends):
+        first = jnp.where(col > row, scores[:, :TILE], LOW)
+        scores = jnp.concatenate([first, scores[:, TILE:]], axis=1) if end < nbytes else first
+        peak = jnp.max(scores, axis=1, keepdims=True)
+        expo = jnp.exp2((scores - peak) * factor)
+        if end == nbytes:
+            expo = jnp.where(col > row, expo, 0.0)
+        total = dot(expo.astype(jnp.bfloat16), values[start:])
+        norm = total[:, size:]
+        some = norm > 0
+        norm = jnp.where(some, norm, 1.0)
+        out_ref[start:end, columns] = (total[:, :size] / norm).astype(jnp.bfloat16)
+        lse = jnp.where(some, peak * factor + jnp.log2(norm), LOW)
+        keep_lse(out_ref, nbytes, slice(start, end), head, lse)
+
+
+def cross_attention(q, k, v, first, count):
     nbytes, width = q.shape
-    slots = starts.shape[0]
-    block = pl.BlockSpec((nbytes, TILE), lambda h: (0, h))
-
-    def whole(*shape):
-        return pl.BlockSpec(shape, lambda h: (0,) * len(shape))
-
+    block = pl.BlockSpec((nbytes, TILE), lambda h: (0, h + first))
+    out = (nbytes + 4 * count, count * TILE)
     return pl.pallas_call(
         cross_kernel,
-        grid=(width // TILE,),
-        in_specs=[
-            pl.BlockSpec(memory_space=pltpu.SMEM),
-            block,
-            block,
-            block,
-            block,
-            whole(nbytes, TILE),
-            whole(1, width),
-            whole(*pool_query.shape),
-            whole(slots, 1),
-            whole(slots, 1),
-        ],
-        out_specs=[whole(nbytes, width), whole(slots, width)],
+        grid=(count,),
+        in_specs=[pl.BlockSpec((nbytes, TILE), lambda h: (0, h)), block, block],
+        out_specs=pl.BlockSpec(out, lambda h: (0, 0)),
+        out_shape=jax.ShapeDtypeStruct(out, jnp.bfloat16),
+        cost_estimate=SMALL,
+        compiler_params=pltpu.CompilerParams(vmem_limit_bytes=24 * 2**20),
+        name="cross_attention",
+    )(q, k, v)
+
+
+def spread(terms, first, count):
+    n = terms.shape[0] // 4
+    row = lax.broadcasted_iota(jnp.int32, (4 * n, count * TILE), 0)
+    col = lax.broadcasted_iota(jnp.int32, (4 * n, count * TILE), 1) // TILE + first
+    one = jnp.where((row % n == col) & (row < 3 * n), 1.0, 0.0).astype(jnp.bfloat16)
+    return lax.dot_general(terms, one, (((0,), (0,)), ((), ())), preferred_element_type=jnp.float32)
+
+
+def pool_kernel(
+    lead_ref, own_ref, lse_ref, *refs
+):
+    *part_refs, gain_ref, query_ref, start_ref, next_ref, enc_ref, pooled_ref = refs
+    nbytes, width = own_ref.shape
+    slots = start_ref.shape[0]
+    size = TILE
+    factor = size ** (-0.5) * LOG2E
+    leading = lead_ref[0] != 0
+    for start in range(0, nbytes, TILE):
+        rows = slice(start, start + TILE)
+        mixes = []
+        squares = jnp.zeros((TILE, size), jnp.float32)
+        first = 0
+        for part_ref in part_refs:
+            count = part_ref.shape[1] // TILE
+            own_lse = spread(lse_ref[:, rows], first, count)
+            part_lse = spread(part_ref[nbytes:, rows], 0, count)
+            for h in range(count):
+                at = slice(h * size, (h + 1) * size)
+                gap = jnp.where(leading, LOW, part_lse[:, at] - own_lse[:, at])
+                share = 1.0 / (1.0 + jnp.exp2(gap))
+                own = own_ref[rows, (first + h) * size : (first + h + 1) * size]
+                part = part_ref[rows, at].astype(jnp.float32)
+                mix = part + (own - part) * share
+                squares += mix * mix
+                mixes.append(mix)
+            first += count
+        scale = lax.rsqrt(jnp.sum(squares, axis=1, keepdims=True) / width + epsilon)
+        for h, mix in enumerate(mixes):
+            at = slice(h * size, (h + 1) * size)
+            enc_ref[rows, at] = (mix * scale * gain_ref[:, at]).astype(jnp.bfloat16)
+    enc = enc_ref[...]
+    n_heads = query_ref.shape[0]
+    wide = jnp.concatenate([query_ref[...].astype(jnp.float32)] * n_heads, axis=1)
+    head_row = lax.broadcasted_iota(jnp.int32, wide.shape, 0)
+    head_col = lax.broadcasted_iota(jnp.int32, wide.shape, 1) // size
+    wide = jnp.where(head_row == head_col, wide, 0.0).astype(jnp.bfloat16)
+    scores = dot_t(wide, enc) * factor
+    place = lax.broadcasted_iota(jnp.int32, (slots, nbytes), 1)
+    member = (place >= start_ref[...]) & (place < next_ref[...])
+    for h in range(n_heads):
+        inside = jnp.where(member, scores[h : h + 1, :], LOW)
+        peak = jnp.max(inside, axis=1, keepdims=True)
+        expo = jnp.where(member, jnp.exp2(inside - peak), 0.0)
+        total = jnp.sum(expo, axis=1, keepdims=True)
+        weights = (expo * jnp.where(total > 0, 1.0 / total, 0.0)).astype(jnp.bfloat16)
+        pooled_ref[:, h * size : (h + 1) * size] = dot(
+            weights, enc[:, h * size : (h + 1) * size]
+        ).astype(jnp.bfloat16)
+
+
+def pool(leading, own, lse, parts, gain, pool_query, starts, ends):
+    nbytes, width = own.shape
+    slots = starts.shape[0]
+    return pl.pallas_call(
+        pool_kernel,
+        in_specs=[pl.BlockSpec(memory_space=pltpu.SMEM)] + [VMEM] * (len(parts) + 6),
+        out_specs=[VMEM, VMEM],
         out_shape=[
             jax.ShapeDtypeStruct((nbytes, width), jnp.bfloat16),
             jax.ShapeDtypeStruct((slots, width), jnp.bfloat16),
         ],
-        scratch_shapes=[pltpu.VMEM((nbytes, width), jnp.float32)],
+        cost_estimate=SMALL,
         compiler_params=pltpu.CompilerParams(vmem_limit_bytes=32 * 2**20),
-        name="cross_attention",
-    )(leading, q, k, v, own, lse, gain, pool_query, starts, ends)
+        name="pool",
+    )(leading, own, lse, *parts, gain, pool_query, starts, ends)
 
 
 def patch_kernel(n_blocks, plan, n_weights, at_ref, *refs):
@@ -166,7 +207,7 @@
     weights = refs[n_blocks : n_blocks + n_weights]
     (
         enc_ref, bias_ref, pgain_ref, ogain_ref, dgain_ref, start_col_ref, start_row_ref,
-        byte_ref, patch_ref, up_ref, kv_w_ref, kv_ref, mix_ref, in_ref, sems,
+        byte_ref, patch_ref, all_ref, up_ref, kv_w_ref, kv_ref, mix_ref, in_ref, sems,
     ) = refs[n_blocks + n_weights :]
     copies = plan(at_ref, weights, up_ref, kv_w_ref)
     copies = [
@@ -179,19 +220,18 @@
 
     slots = patch_ref.shape[0]
     offset = 0
-    for b, block in enumerate(blocks):
-        rows = block.shape[0]
-        step = rows if rows <= 4 * slots else 4 * slots
-        for r in range(0, rows, step):
-            lifted = dot(block[r : r + step, :], up_ref[...])
-            scale = lax.rsqrt(jnp.mean(lifted * lifted, axis=1, keepdims=True) + epsilon)
-            patch_in = (lifted * scale * pgain_ref[...]).astype(jnp.bfloat16)
-            if b == 0:
-                in_ref[...] = patch_in[:slots]
-            kv_ref[offset + r : offset + r + step, :] = dot(patch_in, kv_w_ref[...]).astype(
-                jnp.bfloat16
-            )
-        offset += rows
+    for block in blocks:
+        all_ref[offset : offset + block.shape[0], :] = block[...]
+        offset += block.shape[0]
+    step = 4 * slots
+    for r in range(0, offset, step):
+        rows = slice(r, min(r + step, offset))
+        lifted = dot(all_ref[rows, :], up_ref[...])
+        scale = lax.rsqrt(jnp.mean(lifted * lifted, axis=1, keepdims=True) + epsilon)
+        patch_in = (lifted * scale * pgain_ref[...]).astype(jnp.bfloat16)
+        if r == 0:
+            in_ref[...] = patch_in[:slots]
+        kv_ref[rows, :] = dot(patch_in, kv_w_ref[...]).astype(jnp.bfloat16)
 
     size = patch_ref.shape[1] // PATCH_QUERY_HEADS
     rows = kv_ref.shape[0]
@@ -282,6 +322,7 @@
             jax.ShapeDtypeStruct((slots, n_patch_width), jnp.bfloat16),
         ],
         scratch_shapes=[
+            pltpu.VMEM((rows, up_shape[0]), jnp.bfloat16),
             pltpu.VMEM(up_shape, jnp.bfloat16),
             pltpu.VMEM(kv_shape, jnp.bfloat16),
             pltpu.VMEM((rows, kv_shape[1]), jnp.bfloat16),
@@ -289,6 +330,7 @@
             pltpu.VMEM((slots, n_patch_width), jnp.bfloat16),
             pltpu.SemaphoreType.DMA((n_copies,)),
         ],
+        cost_estimate=SMALL,
         compiler_params=pltpu.CompilerParams(vmem_limit_bytes=48 * 2**20),
         name="patches",
     )(at, *blocks, *weights, encoded, bias, *gains, starts_col, starts_row)
@@ -300,7 +342,8 @@
 
 def passed_along(value, axis, steps):
     count = lax.axis_size(axis)
-    return lax.ppermute(value, axis, [(i, i + steps) for i in range(count - steps)])
+    pairs = [(i, i + steps) for i in range(count) if 0 <= i + steps < count]
+    return lax.ppermute(value, axis, pairs)
 
 
 def whole_plan(at_ref, weights, up_ref, kv_ref):
@@ -325,7 +368,7 @@
     return copies
 
 
-def quarter_weights(w_up, w_kv):
+def paired_weights(w_up, w_kv):
     doc = lax.axis_index("doc")
     y = lax.axis_index("seq") % 2
     up = lax.dynamic_slice_in_dim(w_up, doc * (w_up.shape[1] // 4), w_up.shape[1] // 4, 1)
@@ -342,12 +385,11 @@
     mine = jnp.concatenate(
         [low[:n], high[:n], jnp.concatenate([unpacked(low), unpacked(high)], axis=1)], axis=0
     )
-    blocks = [mine] + [exchanged(mine, "seq", 2 * j) for j in range(1, 4)]
-    out = []
-    for block in blocks:
-        across = exchanged(block, "doc", 2)
-        out += [block, exchanged(block, "doc", 1), across, exchanged(across, "doc", 1)]
-    return out
+    return mine, other
+
+
+def after(value, *others):
+    return lax.optimization_barrier((value,) + others)[0]
 
 
 def per_device(
@@ -361,23 +403,43 @@
     n_seq, n_doc = lax.axis_size("seq"), lax.axis_size("doc")
     paired = n_seq == 8 and n_doc == 4
 
-    k_tail = passed_along(byte_k, "seq", 1)
-    v_tail = passed_along(byte_v, "seq", 1)
+    count = byte_q.shape[1] // TILE // 2
+    halves = [byte_q[:, i * count * TILE : (i + 1) * count * TILE] for i in range(2)]
     if paired:
-        weights = quarter_weights(w_up, w_kv)
+        mine, other = paired_weights(w_up, w_kv)
+        halves = [after(h, other) for h in halves]
+        byte_q = after(byte_q, other)
+    q_next = [passed_along(h, "seq", -1) for h in halves]
+    if paired:
+        z_blocks = [exchanged(mine, "seq", 2 * j) for j in (1, 2)]
+        z_blocks.append(exchanged(after(mine, q_next[0]), "seq", 6))
+        across = [exchanged(mine, "doc", 2)]
+    own, lse = own_attention(byte_q, byte_k, byte_v)
+    first = [lse] + (across[:1] if paired else [])
+    low = cross_attention(after(q_next[0], *first), byte_k, byte_v, 0, count)
+    second = [low] + (z_blocks[:1] if paired else [])
+    high = cross_attention(after(q_next[1], *second), byte_k, byte_v, count, count)
+    parts = [passed_along(partial, "seq", 1) for partial in (low, high)]
+    if paired:
+        across += [exchanged(after(z, high), "doc", 2) for z in z_blocks[:2]]
+        parts[1] = after(parts[1], z_blocks[1], z_blocks[2], across[1])
+
+    starts = lax.dynamic_index_in_dim(patch_start, device, 0, keepdims=False)
+    ends = jnp.concatenate([starts[1:], jnp.full((1,), nbytes, jnp.int32)])
+    row = lambda g: g.astype(jnp.float32)[None, :]
+    encoded, pooled = pool(
+        (device == 0).astype(jnp.int32)[None], own, lse, parts, row(byte_gain), pool_query,
+        starts[:, None], ends[:, None],
+    )
+    if paired:
+        across.append(exchanged(after(z_blocks[2], pooled), "doc", 2))
+        weights = []
+        for z, x in zip([mine] + z_blocks, across):
+            weights += [z, exchanged(after(z, pooled), "doc", 1), x, exchanged(after(x, pooled), "doc", 1)]
         plan, n_copies = quarter_plan, 3 * len(weights)
     else:
         weights = [lax.all_gather(w, "seq", axis=0, tiled=True) for w in (w_up, w_kv)]
         plan, n_copies = whole_plan, 2
-
-    own, lse = own_attention(byte_q, byte_k, byte_v)
-    starts = lax.dynamic_index_in_dim(patch_start, device, 0, keepdims=False)
-    ends = jnp.concatenate([starts[1:], jnp.full((1,), nbytes, jnp.int32)])
-    row = lambda g: g.astype(jnp.float32)[None, :]
-    encoded, pooled = cross_attention(
-        (device == 0).astype(jnp.int32)[None], byte_q, k_tail, v_tail, own, lse, row(byte_gain),
-        pool_query, starts[:, None], ends[:, None],
-    )
 
     place = jnp.arange(slots, dtype=jnp.int32)
     own_allowed = (place[None, :] <= place[:, None]) & (starts < nbytes)[None, :]

time: 209 us -> 154 us (0.74)
  waiting for transfers between devices: 80.5 us -> 46.7 us
  starting transfers between devices: 69.4 us -> 48.1 us
  local copies, waits for them, and re-layouts: 9.48 us -> 12.9 us
  Pallas kernels: 47.5 us -> 44.5 us
    ppermute x23, waiting for transfers between devices: 80.5 us -> 46.7 us  [exchanged(): lax.ppermute(value, axis, [(i, i ^ mask) for i in range(lax.axis_size(axi...]
    ppermute x23, starting transfers between devices: 61.6 us -> 28.7 us  [exchanged(): lax.ppermute(value, axis, [(i, i ^ mask) for i in range(lax.axis_size(axi...]
    ppermute x2 -> x4, starting transfers between devices: 7.84 us -> 19.4 us  [passed_along(): return lax.ppermute(value, axis, pairs)]
    pallas_call x1, Pallas kernels: 26.9 us -> 19.9 us  [patches(): pl.pallas_call(functools.partial(patch_kernel, len(blocks), plan, len(wei...]
    pallas_call x1 -> x3, Pallas kernels: 9.94 us -> 13.6 us  [the longest x2 10.3 us: cross_attention(): pl.pallas_call(cross_kernel, grid=(count,), in_specs=[pl.BlockSpec((nbyte...]
    unnamed x30 -> x38, local copies, waits for them, and re-layouts: 7.19 us -> 8.57 us
  transfers between devices with their start and end apart: 25 -> 27, of which waited for: 8 -> 13; matrix products, arithmetic and copies ran while one was open for 1% -> 2% of each run, Pallas kernels for 10% -> 16%
where the time goes in v2:
time: 154 us
  starting transfers between devices  48.1 us (31%)
  waiting for transfers between devices  46.7 us (30%)
  Pallas kernels  44.5 us (29%)
  local copies, waits for them, and re-layouts  12.9 us (8%)
    ppermute x23, waiting for transfers between devices, exchanged(): lax.ppermute(value, axis, [(i, i ^ mask) for i in range(lax.axis_size(axi...  46.7 us
    ppermute x23, starting transfers between devices, exchanged(): lax.ppermute(value, axis, [(i, i ^ mask) for i in range(lax.axis_size(axi...  28.7 us
    pallas_call x1, Pallas kernels, patches(): pl.pallas_call(functools.partial(patch_kernel, len(blocks), plan, len(wei...  19.9 us
    ppermute x4, starting transfers between devices, passed_along(): return lax.ppermute(value, axis, pairs)  19.4 us
    pallas_call x1, Pallas kernels, own_attention(): pl.pallas_call(own_kernel, grid=(width // TILE,), in_specs=[block] * 3, o...  10.9 us
    pallas_call x2, Pallas kernels, cross_attention(): pl.pallas_call(cross_kernel, grid=(count,), in_specs=[pl.BlockSpec((nbyte...  10.3 us
    unnamed x38, local copies, waits for them, and re-layouts  8.57 us
    pallas_call x1, Pallas kernels, pool(): pl.pallas_call(pool_kernel, in_specs=[pl.BlockSpec(memory_space=pltpu.SME...  3.35 us
  transfers between devices with their start and end apart: 27, of which 13 were waited for; matrix products, arithmetic and copies ran while one was open for 2% of the time, Pallas kernels for 16%

profile of v2, /device:TPU:0, one launch (start us, length us, event | category | flops | bytes accessed | tf_op | source)
XLA Modules:
  0.0 153.7 jit_solution(10864390130191754526)
XLA Ops:
  0.6 0.0 copy-start
  0.7 1.0 copy-done
  1.7 0.9 constant_dynamic-slice_fusion
  2.6 3.0 %collective-permute-start = (bf16[256,512]{1,0:T(8,128)(2,1)S(1)}, bf16[256,512]{1,0:T(8,128)(2,1)S(1)}, u32[]{:S(2)}, u32[]{:S(2)}) collective-permute-start(bf16[256,512]{1,0:T(8,128)(2,1)S(1)} %maximum_maximum_fusion.1), channel_id=1, source_target_pairs={{0,4},{4,0},{8,12},{12,8},{16,20},{20,16},{24,28},{28,24},{1,5},{5... | collective-permute-start | bytes 786440 | tf_op jit(solution)/shard_map/ppermute | solution.py:340
  5.6 2.2 %fusion.2 = (bf16[512,512]{1,0:T(8,128)(2,1)}, bf16[512,512]{1,0:T(8,128)(2,1)}) fusion(bf16[512,1024]{1,0:T(8,128)(2,1)} %q_ref), kind=kLoop, calls=%fused_computation.21 | loop fusion | bytes 2097152 | tf_op jit(solution)/shard_map/slice | solution.py:407
  7.9 4.1 %collective-permute-done = bf16[256,512]{1,0:T(8,128)(2,1)S(1)} collective-permute-done((bf16[256,512]{1,0:T(8,128)(2,1)S(1)}, bf16[256,512]{1,0:T(8,128)(2,1)S(1)}, u32[]{:S(2)}, u32[]{:S(2)}) %collective-permute-start) | collective-permute-done | bytes 262176 | tf_op jit(solution)/shard_map/ppermute | solution.py:340
  11.9 0.1 broadcast_select_fusion.1
  12.1 1.3 collective-permute-start.1
  13.5 1.8 %collective-permute-start.2 = (bf16[512,512]{1,0:T(8,128)(2,1)S(1)}, bf16[512,512]{1,0:T(8,128)(2,1)}, u32[]{:S(2)}, u32[]{:S(2)}) collective-permute-start(bf16[512,512]{1,0:T(8,128)(2,1)S(1)} %maximum_maximum_fusion.refs_8_), channel_id=1, source_target_pairs={{0,2},{1,3},{2,0},{3,1},{4,6},{5,7},{6,4},{7,5},{8,10},{9,11},{10,... | collective-permute-start | bytes 1572872 | tf_op jit(solution)/shard_map/ppermute | solution.py:340
  15.2 3.6 %collective-permute-start.5 = (bf16[512,512]{1,0:T(8,128)(2,1)S(1)}, bf16[512,512]{1,0:T(8,128)(2,1)}, u32[]{:S(2)}, u32[]{:S(2)}) collective-permute-start(bf16[512,512]{1,0:T(8,128)(2,1)S(1)} %maximum_maximum_fusion.refs_8_), channel_id=1, source_target_pairs={{0,8},{4,12},{8,0},{12,4},{16,24},{20,28},{24,16},{28,20},{1,9},{5... | collective-permute-start | bytes 1572872 | tf_op jit(solution)/shard_map/ppermute | solution.py:340
  18.8 1.3 collective-permute-start.4
  20.1 3.3 %collective-permute-start.7 = (bf16[512,512]{1,0:T(8,128)(2,1)S(1)}, bf16[512,512]{1,0:T(8,128)(2,1)}, u32[]{:S(2)}, u32[]{:S(2)}) collective-permute-start(bf16[512,512]{1,0:T(8,128)(2,1)S(1)} %maximum_maximum_fusion.refs_8_), channel_id=1, source_target_pairs={{0,16},{4,20},{8,24},{12,28},{16,0},{20,4},{24,8},{28,12},{1,17},{... | collective-permute-start | bytes 1572872 | tf_op jit(solution)/shard_map/ppermute | solution.py:340
  23.5 1.2 copy-done.3
  24.7 10.9 %own_attention.1 = (f32[512,1024]{1,0:T(8,128)S(1)}, bf16[32,512]{1,0:T(8,128)(2,1)S(1)}) custom-call(bf16[512,1024]{1,0:T(8,128)(2,1)S(1)} %copy-done.3, bf16[512,1024]{1,0:T(8,128)(2,1)S(1)} %copy-done.1, bf16[512,1024]{1,0:T(8,128)(2,1)S(1)} %copy-done.2), custom_call_target="tpu_custom_call" | custom-call | flops 1 | bytes 1 | tf_op jit(solution)/shard_map/own_attention/pallas_call | solution.py:70
  35.6 1.3 copy-done.4
  37.0 2.3 %collective-permute-start.8 = (bf16[512,512]{1,0:T(8,128)(2,1)S(1)}, bf16[512,512]{1,0:T(8,128)(2,1)}, u32[]{:S(2)}, u32[]{:S(2)}) collective-permute-start(bf16[512,512]{1,0:T(8,128)(2,1)S(1)} %maximum_maximum_fusion.refs_8_), channel_id=1, source_target_pairs={{0,24},{4,28},{8,16},{12,20},{16,8},{20,12},{24,0},{28,4},{1,25},{... | collective-permute-start | bytes 1572872 | tf_op jit(solution)/shard_map/ppermute | solution.py:340
  39.3 5.1 %cross_attention.2 = bf16[528,512]{1,0:T(8,128)(2,1)} custom-call(bf16[512,512]{1,0:T(8,128)(2,1)} %collective-permute-done.1.q_ref, bf16[512,1024]{1,0:T(8,128)(2,1)S(1)} %copy-done.1, bf16[512,1024]{1,0:T(8,128)(2,1)S(1)} %copy-done.2), custom_call_target="tpu_custom_call" | custom-call | flops 1 | bytes 1 | tf_op jit(solution)/shard_map/cross_attention/pallas_call | solution.py:116
  44.5 3.1 %collective-permute-start.3 = (bf16[528,512]{1,0:T(8,128)(2,1)}, bf16[528,512]{1,0:T(8,128)(2,1)}, u32[]{:S(2)}, u32[]{:S(2)}) collective-permute-start(bf16[528,512]{1,0:T(8,128)(2,1)} %cross_attention.2), channel_id=1, source_target_pairs={{0,4},{4,8},{8,12},{12,16},{16,20},{20,24},{24,28},{1,5},{5,9},{9,... | collective-permute-start | bytes 1622024 | tf_op jit(solution)/shard_map/ppermute | solution.py:346
  47.6 3.8 %collective-permute-done.5.refs_12_ = bf16[512,512]{1,0:T(8,128)(2,1)} collective-permute-done((bf16[512,512]{1,0:T(8,128)(2,1)S(1)}, bf16[512,512]{1,0:T(8,128)(2,1)}, u32[]{:S(2)}, u32[]{:S(2)}) %collective-permute-start.5) | collective-permute-done | bytes 524320 | tf_op jit(solution)/shard_map/ppermute | solution.py:340
  51.4 5.1 %cross_attention.3 = bf16[528,512]{1,0:T(8,128)(2,1)} custom-call(bf16[512,512]{1,0:T(8,128)(2,1)} %collective-permute-done.4.q_ref, bf16[512,1024]{1,0:T(8,128)(2,1)S(1)} %copy-done.1, bf16[512,1024]{1,0:T(8,128)(2,1)S(1)} %copy-done.2), custom_call_target="tpu_custom_call" | custom-call | flops 1 | bytes 1 | tf_op jit(solution)/shard_map/cross_attention/pallas_call | solution.py:116
  56.6 13.7 %collective-permute-start.6 = (bf16[528,512]{1,0:T(8,128)(2,1)}, bf16[528,512]{1,0:T(8,128)(2,1)S(1)}, u32[]{:S(2)}, u32[]{:S(2)}) collective-permute-start(bf16[528,512]{1,0:T(8,128)(2,1)} %cross_attention.3), channel_id=1, source_target_pairs={{0,4},{4,8},{8,12},{12,16},{16,20},{20,24},{24,28},{1,5},{5,9},{9,... | collective-permute-start | bytes 1622024 | tf_op jit(solution)/shard_map/ppermute | solution.py:346
  70.3 6.1 %collective-permute-done.7.refs_16_ = bf16[512,512]{1,0:T(8,128)(2,1)} collective-permute-done((bf16[512,512]{1,0:T(8,128)(2,1)S(1)}, bf16[512,512]{1,0:T(8,128)(2,1)}, u32[]{:S(2)}, u32[]{:S(2)}) %collective-permute-start.7) | collective-permute-done | bytes 524320 | tf_op jit(solution)/shard_map/ppermute | solution.py:340
  76.4 1.5 collective-permute-start.9
  77.9 0.5 collective-permute-start.22
  78.4 0.1 slice_bitcast_fusion
  78.5 0.1 add_bitcast_fusion
  78.5 0.1 copy.14.refs_5_
  78.6 0.1 copy.13.refs_4_.refs_29_
  78.7 0.1 stack.59
  78.9 8.8 %collective-permute-done.9.refs_14_ = bf16[512,512]{1,0:T(8,128)(2,1)S(1)} collective-permute-done((bf16[512,512]{1,0:T(8,128)(2,1)}, bf16[512,512]{1,0:T(8,128)(2,1)S(1)}, u32[]{:S(2)}, u32[]{:S(2)}) %collective-permute-start.9) | collective-permute-done | bytes 524320 | tf_op jit(solution)/shard_map/ppermute | solution.py:340
  87.7 1.6 %copy-done.5 = f32[512,1024]{1,0:T(8,128)S(1)} copy-done((f32[512,1024]{1,0:T(8,128)S(1)}, f32[512,1024]{1,0:T(8,128)}, u32[]{:S(2)}) %copy-start.5) | copy-done | bytes 2097176
  89.3 3.3 %pool.1 = (bf16[512,1024]{1,0:T(8,128)(2,1)S(1)}, bf16[80,1024]{1,0:T(8,128)(2,1)S(1)}) custom-call(s32[1]{0:T(128)} %bitcast.2.lead_ref, f32[512,1024]{1,0:T(8,128)S(1)} %copy-done.5, bf16[32,512]{1,0:T(8,128)(2,1)S(1)} %get-tuple-element.25.lse_ref, bf16[528,512]{1,0:T(8,128)(2,1)} %collective-permute-done.3.refs_0_, ...), custom_call_target="tpu_custom_call" | custom-call | flops 1 | bytes 1 | tf_op jit(solution)/shard_map/pool/pallas_call | solution.py:191
  92.7 1.0 copy-done.6
  93.7 6.6 %collective-permute-start.11 = (bf16[80,1024]{1,0:T(8,128)(2,1)S(1)}, bf16[80,1024]{1,0:T(8,128)(2,1)S(1)}, u32[]{:S(2)}, u32[]{:S(2)}) collective-permute-start(bf16[80,1024]{1,0:T(8,128)(2,1)S(1)} %get-tuple-element.33.refs_0_), channel_id=1, source_target_pairs={{0,16},{4,20},{8,24},{12,28},{16,0},{20,4},{24,8},{28,12},{1,17},{... | collective-permute-start | bytes 491528 | tf_op jit(solution)/shard_map/ppermute | solution.py:340
  100.3 0.3 collective-permute-start.10
  100.7 0.5 collective-permute-start.25
  101.2 0.2 collective-permute-done.12.refs_3_
  101.4 0.3 collective-permute-start.18
  101.7 8.5 %collective-permute-done.11.refs_2_ = bf16[80,1024]{1,0:T(8,128)(2,1)S(1)} collective-permute-done((bf16[80,1024]{1,0:T(8,128)(2,1)S(1)}, bf16[80,1024]{1,0:T(8,128)(2,1)S(1)}, u32[]{:S(2)}, u32[]{:S(2)}) %collective-permute-start.11) | collective-permute-done | bytes 163872 | tf_op jit(solution)/shard_map/ppermute | solution.py:340
  110.2 0.6 gather_fusion
  110.8 0.1 stack.67
  110.9 1.8 %collective-permute-start.16 = (bf16[80,1024]{1,0:T(8,128)(2,1)S(1)}, bf16[80,1024]{1,0:T(8,128)(2,1)S(1)}, u32[]{:S(2)}, u32[]{:S(2)}) collective-permute-start(bf16[80,1024]{1,0:T(8,128)(2,1)S(1)} %collective-permute-done.12.refs_3_), channel_id=1, source_target_pairs={{0,4},{4,0},{8,12},{12,8},{16,20},{20,16},{24,28},{28,24},{1,5},{5... | collective-permute-start | bytes 491528 | tf_op jit(solution)/shard_map/ppermute | solution.py:340
  112.7 4.9 %collective-permute-done.16.refs_7_ = bf16[80,1024]{1,0:T(8,128)(2,1)S(1)} collective-permute-done((bf16[80,1024]{1,0:T(8,128)(2,1)S(1)}, bf16[80,1024]{1,0:T(8,128)(2,1)S(1)}, u32[]{:S(2)}, u32[]{:S(2)}) %collective-permute-start.16) | collective-permute-done | bytes 163872 | tf_op jit(solution)/shard_map/ppermute | solution.py:340
  117.5 0.7 copy-done.7
  118.2 1.7 %collective-permute-start.15 = (bf16[80,1024]{1,0:T(8,128)(2,1)S(1)}, bf16[80,1024]{1,0:T(8,128)(2,1)}, u32[]{:S(2)}, u32[]{:S(2)}) collective-permute-start(bf16[80,1024]{1,0:T(8,128)(2,1)S(1)} %collective-permute-done.11.refs_2_), channel_id=1, source_target_pairs={{0,4},{4,0},{8,12},{12,8},{16,20},{20,16},{24,28},{28,24},{1,5},{5... | collective-permute-start | bytes 491528 | tf_op jit(solution)/shard_map/ppermute | solution.py:340
  119.9 0.3 collective-permute-start.14
  120.2 0.1 broadcast_and_fusion
  120.3 0.1 reshape.364
  120.4 0.1 pad.1.clone
  120.5 4.9 %collective-permute-done.15.refs_6_ = bf16[80,1024]{1,0:T(8,128)(2,1)} collective-permute-done((bf16[80,1024]{1,0:T(8,128)(2,1)S(1)}, bf16[80,1024]{1,0:T(8,128)(2,1)}, u32[]{:S(2)}, u32[]{:S(2)}) %collective-permute-start.15) | collective-permute-done | bytes 163872 | tf_op jit(solution)/shard_map/ppermute | solution.py:340
  125.4 2.2 %collective-permute-done.14.refs_5_ = bf16[80,1024]{1,0:T(8,128)(2,1)} collective-permute-done((bf16[80,1024]{1,0:T(8,128)(2,1)}, bf16[80,1024]{1,0:T(8,128)(2,1)}, u32[]{:S(2)}, u32[]{:S(2)}) %collective-permute-start.14) | collective-permute-done | bytes 163872 | tf_op jit(solution)/shard_map/ppermute | solution.py:340
  127.6 0.5 collective-permute-start.21
  128.1 0.1 collective-permute-start.23
  128.2 0.4 collective-permute-start.26
  128.7 0.1 pad_add_fusion.at_ref
  128.8 1.4 collective-permute-done.20.refs_15_
  130.2 0.3 collective-permute-done.21.refs_17_
  130.5 0.7 collective-permute-done.23.refs_19_
  131.3 0.7 collective-permute-done.26.refs_23_
  132.0 0.0 copy-done.12
  132.0 0.2 copy-done.10
  132.3 0.5 copy-done.13
  132.8 0.9 copy-done.8
  133.7 19.9 %patches.1 = (bf16[512,1024]{1,0:T(8,128)(2,1)}, bf16[80,2048]{1,0:T(8,128)(2,1)}) custom-call(s32[2]{0:T(128)S(1)} %pad_add_fusion.at_ref, bf16[80,1024]{1,0:T(8,128)(2,1)S(1)} %get-tuple-element.33.refs_0_, bf16[80,1024]{1,0:T(8,128)(2,1)} %collective-permute-done.10.refs_1_, bf16[80,1024]{1,0:T(8,128)(2,1)S(1)} %collective-permute-done.11.refs_2_, ...), custom_call_target="tpu_custom_call" | custom-call | flops 1 | bytes 1 | tf_op jit(solution)/shard_map/patches/pallas_call | solution.py:313
  (64 shorter events, 0.3 us)
Async XLA Ops:
  0.6 1.0 copy-start
  2.6 9.3 %collective-permute-start = (bf16[256,512]{1,0:T(8,128)(2,1)S(1)}, bf16[256,512]{1,0:T(8,128)(2,1)S(1)}, u32[]{:S(2)}, u32[]{:S(2)}) collective-permute-start(bf16[256,512]{1,0:T(8,128)(2,1)S(1)} %maximum_maximum_fusion.1), channel_id=1, source_target_pairs={{0,4},{4,0},{8,12},{12,8},{16,20},{20,16},{24,28},{28,24},{1,5},{5... | collective-permute-start | bytes 786440 | tf_op jit(solution)/shard_map/ppermute | solution.py:340
  7.9 15.5 %copy-start.17 = (bf16[1024]{0:T(1024)(128)(2,1)S(1)}, bf16[1024]{0:T(1024)(128)(2,1)}, u32[]{:S(2)}) copy-start(bf16[1024]{0:T(1024)(128)(2,1)} %param.14) | copy-start | bytes 6148
  7.9 15.5 %copy-start.14 = (s32[8,80]{1,0:T(8,128)S(1)}, s32[8,80]{1,0:T(8,128)}, u32[]{:S(2)}) copy-start(s32[8,80]{1,0:T(8,128)} %param.21) | copy-start | bytes 7684
  7.9 15.6 %copy-start.1 = (bf16[512,1024]{1,0:T(8,128)(2,1)S(1)}, bf16[512,1024]{1,0:T(8,128)(2,1)}, u32[]{:S(2)}) copy-start(bf16[512,1024]{1,0:T(8,128)(2,1)} %k_ref.5) | copy-start | bytes 3145732
  7.9 15.6 %copy-start.2 = (bf16[512,1024]{1,0:T(8,128)(2,1)S(1)}, bf16[512,1024]{1,0:T(8,128)(2,1)}, u32[]{:S(2)}) copy-start(bf16[512,1024]{1,0:T(8,128)(2,1)} %v_ref.5) | copy-start | bytes 3145732
  12.1 24.9 %collective-permute-start.1 = (bf16[512,512]{1,0:T(8,128)(2,1)}, bf16[512,512]{1,0:T(8,128)(2,1)}, u32[]{:S(2)}, u32[]{:S(2)}) collective-permute-start(bf16[512,512]{1,0:T(8,128)(2,1)} %get-tuple-element.26), channel_id=1, source_target_pairs={{4,0},{8,4},{12,8},{16,12},{20,16},{24,20},{28,24},{5,1},{9,5},{13... | collective-permute-start | bytes 1572872 | tf_op jit(solution)/shard_map/ppermute | solution.py:346
  13.5 25.9 %collective-permute-start.2 = (bf16[512,512]{1,0:T(8,128)(2,1)S(1)}, bf16[512,512]{1,0:T(8,128)(2,1)}, u32[]{:S(2)}, u32[]{:S(2)}) collective-permute-start(bf16[512,512]{1,0:T(8,128)(2,1)S(1)} %maximum_maximum_fusion.refs_8_), channel_id=1, source_target_pairs={{0,2},{1,3},{2,0},{3,1},{4,6},{5,7},{6,4},{7,5},{8,10},{9,11},{10,... | collective-permute-start | bytes 1572872 | tf_op jit(solution)/shard_map/ppermute | solution.py:340
  15.2 36.2 %collective-permute-start.5 = (bf16[512,512]{1,0:T(8,128)(2,1)S(1)}, bf16[512,512]{1,0:T(8,128)(2,1)}, u32[]{:S(2)}, u32[]{:S(2)}) collective-permute-start(bf16[512,512]{1,0:T(8,128)(2,1)S(1)} %maximum_maximum_fusion.refs_8_), channel_id=1, source_target_pairs={{0,8},{4,12},{8,0},{12,4},{16,24},{20,28},{24,16},{28,20},{1,9},{5... | collective-permute-start | bytes 1572872 | tf_op jit(solution)/shard_map/ppermute | solution.py:340
  18.8 32.6 %collective-permute-start.4 = (bf16[512,512]{1,0:T(8,128)(2,1)}, bf16[512,512]{1,0:T(8,128)(2,1)}, u32[]{:S(2)}, u32[]{:S(2)}) collective-permute-start(bf16[512,512]{1,0:T(8,128)(2,1)} %get-tuple-element.28), channel_id=1, source_target_pairs={{4,0},{8,4},{12,8},{16,12},{20,16},{24,20},{28,24},{5,1},{9,5},{13... | collective-permute-start | bytes 1572872 | tf_op jit(solution)/shard_map/ppermute | solution.py:346
  20.1 56.2 %collective-permute-start.7 = (bf16[512,512]{1,0:T(8,128)(2,1)S(1)}, bf16[512,512]{1,0:T(8,128)(2,1)}, u32[]{:S(2)}, u32[]{:S(2)}) collective-permute-start(bf16[512,512]{1,0:T(8,128)(2,1)S(1)} %maximum_maximum_fusion.refs_8_), channel_id=1, source_target_pairs={{0,16},{4,20},{8,24},{12,28},{16,0},{20,4},{24,8},{28,12},{1,17},{... | collective-permute-start | bytes 1572872 | tf_op jit(solution)/shard_map/ppermute | solution.py:340
  23.4 1.2 copy-start.3
  35.6 1.3 copy-start.4
  37.0 41.9 %collective-permute-start.8 = (bf16[512,512]{1,0:T(8,128)(2,1)S(1)}, bf16[512,512]{1,0:T(8,128)(2,1)}, u32[]{:S(2)}, u32[]{:S(2)}) collective-permute-start(bf16[512,512]{1,0:T(8,128)(2,1)S(1)} %maximum_maximum_fusion.refs_8_), channel_id=1, source_target_pairs={{0,24},{4,28},{8,16},{12,20},{16,8},{20,12},{24,0},{28,4},{1,25},{... | collective-permute-start | bytes 1572872 | tf_op jit(solution)/shard_map/ppermute | solution.py:340
  44.5 43.2 %copy-start.9 = (bf16[8,128]{1,0:T(8,128)(2,1)S(1)}, bf16[8,128]{1,0:T(8,128)(2,1)}, u32[]{:S(2)}) copy-start(bf16[8,128]{1,0:T(8,128)(2,1)} %refs_3_.1) | copy-start | bytes 6148
  44.5 43.2 %collective-permute-start.3 = (bf16[528,512]{1,0:T(8,128)(2,1)}, bf16[528,512]{1,0:T(8,128)(2,1)}, u32[]{:S(2)}, u32[]{:S(2)}) collective-permute-start(bf16[528,512]{1,0:T(8,128)(2,1)} %cross_attention.2), channel_id=1, source_target_pairs={{0,4},{4,8},{8,12},{12,16},{16,20},{20,24},{24,28},{1,5},{5,9},{9,... | collective-permute-start | bytes 1622024 | tf_op jit(solution)/shard_map/ppermute | solution.py:346
  56.6 63.8 %copy-start.18 = (bf16[1024]{0:T(1024)(128)(2,1)S(1)}, bf16[1024]{0:T(1024)(128)(2,1)}, u32[]{:S(2)}) copy-start(bf16[1024]{0:T(1024)(128)(2,1)} %param.20) | copy-start | bytes 6148
  56.6 63.8 %copy-start.15 = (bf16[2048]{0:T(1024)(128)(2,1)S(1)}, bf16[2048]{0:T(1024)(128)(2,1)}, u32[]{:S(2)}) copy-start(bf16[2048]{0:T(1024)(128)(2,1)} %param.17) | copy-start | bytes 12292
  56.6 63.8 %copy-start.16 = (bf16[2048]{0:T(1024)(128)(2,1)S(1)}, bf16[2048]{0:T(1024)(128)(2,1)}, u32[]{:S(2)}) copy-start(bf16[2048]{0:T(1024)(128)(2,1)} %param.19) | copy-start | bytes 12292
  56.6 31.1 %collective-permute-start.6 = (bf16[528,512]{1,0:T(8,128)(2,1)}, bf16[528,512]{1,0:T(8,128)(2,1)S(1)}, u32[]{:S(2)}, u32[]{:S(2)}) collective-permute-start(bf16[528,512]{1,0:T(8,128)(2,1)} %cross_attention.3), channel_id=1, source_target_pairs={{0,4},{4,8},{8,12},{12,16},{16,20},{20,24},{24,28},{1,5},{5,9},{9,... | collective-permute-start | bytes 1622024 | tf_op jit(solution)/shard_map/ppermute | solution.py:346
  76.4 11.3 %collective-permute-start.9 = (bf16[512,512]{1,0:T(8,128)(2,1)}, bf16[512,512]{1,0:T(8,128)(2,1)S(1)}, u32[]{:S(2)}, u32[]{:S(2)}) collective-permute-start(bf16[512,512]{1,0:T(8,128)(2,1)} %collective-permute-done.5.refs_12_), channel_id=1, source_target_pairs={{0,2},{1,3},{2,0},{3,1},{4,6},{5,7},{6,4},{7,5},{8,10},{9,11},{10,... | collective-permute-start | bytes 1572872 | tf_op jit(solution)/shard_map/ppermute | solution.py:340
  77.9 22.8 %collective-permute-start.22 = (bf16[512,512]{1,0:T(8,128)(2,1)}, bf16[512,512]{1,0:T(8,128)(2,1)}, u32[]{:S(2)}, u32[]{:S(2)}) collective-permute-start(bf16[512,512]{1,0:T(8,128)(2,1)} %collective-permute-done.7.refs_16_), channel_id=1, source_target_pairs={{0,2},{1,3},{2,0},{3,1},{4,6},{5,7},{6,4},{7,5},{8,10},{9,11},{10,... | collective-permute-start | bytes 1572872 | tf_op jit(solution)/shard_map/ppermute | solution.py:340
  87.7 1.6 %copy-start.5 = (f32[512,1024]{1,0:T(8,128)S(1)}, f32[512,1024]{1,0:T(8,128)}, u32[]{:S(2)}) copy-start(f32[512,1024]{1,0:T(8,128)} %copy-done.4) | copy-start | bytes 6291460
  92.7 1.0 copy-start.6
  93.7 7.5 %collective-permute-start.13 = (bf16[80,1024]{1,0:T(8,128)(2,1)S(1)}, bf16[80,1024]{1,0:T(8,128)(2,1)S(1)}, u32[]{:S(2)}, u32[]{:S(2)}) collective-permute-start(bf16[80,1024]{1,0:T(8,128)(2,1)S(1)} %get-tuple-element.33.refs_0_), channel_id=1, source_target_pairs={{0,4},{4,0},{8,12},{12,8},{16,20},{20,16},{24,28},{28,24},{1,5},{5... | collective-permute-start | bytes 491528 | tf_op jit(solution)/shard_map/ppermute | solution.py:340
  93.7 7.7 %collective-permute-start.12 = (bf16[80,1024]{1,0:T(8,128)(2,1)S(1)}, bf16[80,1024]{1,0:T(8,128)(2,1)S(1)}, u32[]{:S(2)}, u32[]{:S(2)}) collective-permute-start(bf16[80,1024]{1,0:T(8,128)(2,1)S(1)} %get-tuple-element.33.refs_0_), channel_id=1, source_target_pairs={{0,24},{4,28},{8,16},{12,20},{16,8},{20,12},{24,0},{28,4},{1,25},{... | collective-permute-start | bytes 491528 | tf_op jit(solution)/shard_map/ppermute | solution.py:340
  93.7 16.5 %collective-permute-start.11 = (bf16[80,1024]{1,0:T(8,128)(2,1)S(1)}, bf16[80,1024]{1,0:T(8,128)(2,1)S(1)}, u32[]{:S(2)}, u32[]{:S(2)}) collective-permute-start(bf16[80,1024]{1,0:T(8,128)(2,1)S(1)} %get-tuple-element.33.refs_0_), channel_id=1, source_target_pairs={{0,16},{4,20},{8,24},{12,28},{16,0},{20,4},{24,8},{28,12},{1,17},{... | collective-permute-start | bytes 491528 | tf_op jit(solution)/shard_map/ppermute | solution.py:340
  100.3 10.6 %collective-permute-start.10 = (bf16[80,1024]{1,0:T(8,128)(2,1)S(1)}, bf16[80,1024]{1,0:T(8,128)(2,1)}, u32[]{:S(2)}, u32[]{:S(2)}) collective-permute-start(bf16[80,1024]{1,0:T(8,128)(2,1)S(1)} %get-tuple-element.33.refs_0_), channel_id=1, source_target_pairs={{0,8},{4,12},{8,0},{12,4},{16,24},{20,28},{24,16},{28,20},{1,9},{5... | collective-permute-start | bytes 491528 | tf_op jit(solution)/shard_map/ppermute | solution.py:340
  100.7 19.3 %collective-permute-start.25 = (bf16[512,512]{1,0:T(8,128)(2,1)}, bf16[512,512]{1,0:T(8,128)(2,1)}, u32[]{:S(2)}, u32[]{:S(2)}) collective-permute-start(bf16[512,512]{1,0:T(8,128)(2,1)} %collective-permute-done.8.refs_20_), channel_id=1, source_target_pairs={{0,2},{1,3},{2,0},{3,1},{4,6},{5,7},{6,4},{7,5},{8,10},{9,11},{10,... | collective-permute-start | bytes 1572872 | tf_op jit(solution)/shard_map/ppermute | solution.py:340
  101.2 26.4 %collective-permute-start.17 = (bf16[512,512]{1,0:T(8,128)(2,1)S(1)}, bf16[512,512]{1,0:T(8,128)(2,1)S(1)}, u32[]{:S(2)}, u32[]{:S(2)}) collective-permute-start(bf16[512,512]{1,0:T(8,128)(2,1)S(1)} %maximum_maximum_fusion.refs_8_), channel_id=1, source_target_pairs={{0,1},{1,0},{2,3},{3,2},{4,5},{5,4},{6,7},{7,6},{8,9},{9,8},{10,11... | collective-permute-start | bytes 1572872 | tf_op jit(solution)/shard_map/ppermute | solution.py:340
  101.4 26.7 %collective-permute-start.18 = (bf16[512,512]{1,0:T(8,128)(2,1)}, bf16[512,512]{1,0:T(8,128)(2,1)S(1)}, u32[]{:S(2)}, u32[]{:S(2)}) collective-permute-start(bf16[512,512]{1,0:T(8,128)(2,1)} %collective-permute-done.2.refs_10_), channel_id=1, source_target_pairs={{0,1},{1,0},{2,3},{3,2},{4,5},{5,4},{6,7},{7,6},{8,9},{9,8},{10,11... | collective-permute-start | bytes 1572872 | tf_op jit(solution)/shard_map/ppermute | solution.py:340
  110.2 18.0 %collective-permute-start.19 = (bf16[512,512]{1,0:T(8,128)(2,1)}, bf16[512,512]{1,0:T(8,128)(2,1)}, u32[]{:S(2)}, u32[]{:S(2)}) collective-permute-start(bf16[512,512]{1,0:T(8,128)(2,1)} %collective-permute-done.5.refs_12_), channel_id=1, source_target_pairs={{0,1},{1,0},{2,3},{3,2},{4,5},{5,4},{6,7},{7,6},{8,9},{9,8},{10,11... | collective-permute-start | bytes 1572872 | tf_op jit(solution)/shard_map/ppermute | solution.py:340
  110.9 6.7 %collective-permute-start.16 = (bf16[80,1024]{1,0:T(8,128)(2,1)S(1)}, bf16[80,1024]{1,0:T(8,128)(2,1)S(1)}, u32[]{:S(2)}, u32[]{:S(2)}) collective-permute-start(bf16[80,1024]{1,0:T(8,128)(2,1)S(1)} %collective-permute-done.12.refs_3_), channel_id=1, source_target_pairs={{0,4},{4,0},{8,12},{12,8},{16,20},{20,16},{24,28},{28,24},{1,5},{5... | collective-permute-start | bytes 491528 | tf_op jit(solution)/shard_map/ppermute | solution.py:340
  117.5 0.7 copy-start.7
  118.2 7.2 %collective-permute-start.15 = (bf16[80,1024]{1,0:T(8,128)(2,1)S(1)}, bf16[80,1024]{1,0:T(8,128)(2,1)}, u32[]{:S(2)}, u32[]{:S(2)}) collective-permute-start(bf16[80,1024]{1,0:T(8,128)(2,1)S(1)} %collective-permute-done.11.refs_2_), channel_id=1, source_target_pairs={{0,4},{4,0},{8,12},{12,8},{16,20},{20,16},{24,28},{28,24},{1,5},{5... | collective-permute-start | bytes 491528 | tf_op jit(solution)/shard_map/ppermute | solution.py:340
  119.9 7.7 %collective-permute-start.14 = (bf16[80,1024]{1,0:T(8,128)(2,1)}, bf16[80,1024]{1,0:T(8,128)(2,1)}, u32[]{:S(2)}, u32[]{:S(2)}) collective-permute-start(bf16[80,1024]{1,0:T(8,128)(2,1)} %collective-permute-done.10.refs_1_), channel_id=1, source_target_pairs={{0,4},{4,0},{8,12},{12,8},{16,20},{20,16},{24,28},{28,24},{1,5},{5... | collective-permute-start | bytes 491528 | tf_op jit(solution)/shard_map/ppermute | solution.py:340
  125.4 5.9 %collective-permute-start.24 = (bf16[512,512]{1,0:T(8,128)(2,1)}, bf16[512,512]{1,0:T(8,128)(2,1)S(1)}, u32[]{:S(2)}, u32[]{:S(2)}) collective-permute-start(bf16[512,512]{1,0:T(8,128)(2,1)} %collective-permute-done.8.refs_20_), channel_id=1, source_target_pairs={{0,1},{1,0},{2,3},{3,2},{4,5},{5,4},{6,7},{7,6},{8,9},{9,8},{10,11... | collective-permute-start | bytes 1572872 | tf_op jit(solution)/shard_map/ppermute | solution.py:340
  127.6 2.6 %collective-permute-start.20 = (bf16[512,512]{1,0:T(8,128)(2,1)S(1)}, bf16[512,512]{1,0:T(8,128)(2,1)S(1)}, u32[]{:S(2)}, u32[]{:S(2)}) collective-permute-start(bf16[512,512]{1,0:T(8,128)(2,1)S(1)} %collective-permute-done.9.refs_14_), channel_id=1, source_target_pairs={{0,1},{1,0},{2,3},{3,2},{4,5},{5,4},{6,7},{7,6},{8,9},{9,8},{10,11... | collective-permute-start | bytes 1572872 | tf_op jit(solution)/shard_map/ppermute | solution.py:340
  127.6 2.9 %collective-permute-start.21 = (bf16[512,512]{1,0:T(8,128)(2,1)}, bf16[512,512]{1,0:T(8,128)(2,1)S(1)}, u32[]{:S(2)}, u32[]{:S(2)}) collective-permute-start(bf16[512,512]{1,0:T(8,128)(2,1)} %collective-permute-done.7.refs_16_), channel_id=1, source_target_pairs={{0,1},{1,0},{2,3},{3,2},{4,5},{5,4},{6,7},{7,6},{8,9},{9,8},{10,11... | collective-permute-start | bytes 1572872 | tf_op jit(solution)/shard_map/ppermute | solution.py:340
  128.1 3.1 %collective-permute-start.23 = (bf16[512,512]{1,0:T(8,128)(2,1)}, bf16[512,512]{1,0:T(8,128)(2,1)S(1)}, u32[]{:S(2)}, u32[]{:S(2)}) collective-permute-start(bf16[512,512]{1,0:T(8,128)(2,1)} %collective-permute-done.22.refs_18_), channel_id=1, source_target_pairs={{0,1},{1,0},{2,3},{3,2},{4,5},{5,4},{6,7},{7,6},{8,9},{9,8},{10,11... | collective-permute-start | bytes 1572872 | tf_op jit(solution)/shard_map/ppermute | solution.py:340
  128.2 3.8 %collective-permute-start.26 = (bf16[512,512]{1,0:T(8,128)(2,1)}, bf16[512,512]{1,0:T(8,128)(2,1)S(1)}, u32[]{:S(2)}, u32[]{:S(2)}) collective-permute-start(bf16[512,512]{1,0:T(8,128)(2,1)} %collective-permute-done.25.refs_22_), channel_id=1, source_target_pairs={{0,1},{1,0},{2,3},{3,2},{4,5},{5,4},{6,7},{7,6},{8,9},{9,8},{10,11... | collective-permute-start | bytes 1572872 | tf_op jit(solution)/shard_map/ppermute | solution.py:340
  130.5 1.5 copy-start.11
  131.2 0.8 copy-start.12
  131.3 1.0 copy-start.10
  132.0 0.8 copy-start.13
  132.8 0.9 copy-start.8

commit v3 on v2

--- a/solution.py
+++ b/solution.py
@@ -12,6 +12,7 @@
 LOG2E = 1.4426950408889634
 LOW = -1e30
 TILE = 128
+GROUP = 4
 epsilon = 1e-06
 VMEM = pl.BlockSpec(memory_space=pltpu.VMEM)
 SMALL = pl.CostEstimate(flops=1, bytes_accessed=1, transcendentals=0)
@@ -33,92 +34,114 @@
     return high, middle, (rest - middle.astype(jnp.float32)).astype(jnp.bfloat16)
 
 
-def keep_lse(ref, base, rows, head, lse):
-    n = (ref.shape[0] - base) // 4
-    across = jnp.transpose(lse)[: 4 * n, :]
-    row = lax.broadcasted_iota(jnp.int32, across.shape, 0)
-    kept = jnp.where(head == 0, 0.0, ref[base:, rows].astype(jnp.float32))
-    for i, term in enumerate(split(across)):
-        kept = jnp.where(row == head + i * n, term.astype(jnp.float32), kept)
-    ref[base:, rows] = kept.astype(jnp.bfloat16)
-
-
-def own_kernel(q_ref, k_ref, v_ref, mix_ref, lse_ref):
-    head = pl.program_id(0)
-    nbytes, size = q_ref.shape
+def keep_lse(ref, base, columns_ref, count):
+    for start in range(0, columns_ref.shape[0], TILE):
+        rows = slice(start, start + TILE)
+        across = jnp.transpose(columns_ref[rows, :])[:count, :]
+        terms = [term.astype(jnp.float32) for term in split(across)]
+        terms.append(jnp.zeros_like(across))
+        ref[base:, rows] = jnp.concatenate(terms, axis=0).astype(jnp.bfloat16)
+
+
+def own_kernel(q_ref, k_ref, v_ref, mix_ref, lse_ref, columns_ref):
+    step = pl.program_id(0)
+    nbytes, width = q_ref.shape
+    size = TILE
     factor = size ** (-0.5) * LOG2E
     row = lax.broadcasted_iota(jnp.int32, (TILE, TILE), 0)
     col = lax.broadcasted_iota(jnp.int32, (TILE, TILE), 1)
     causal = col <= row
-    values = jnp.concatenate([v_ref[...], jnp.ones((nbytes, size), jnp.bfloat16)], axis=1)
-
-    for start in range(0, nbytes, TILE):
-        end = start + TILE
-        scores = dot_t(q_ref[start:end, :], k_ref[:end, :])
-        last = jnp.where(causal, scores[:, start:end], LOW)
-        scores = last if start == 0 else jnp.concatenate([scores[:, :start], last], axis=1)
-        peak = jnp.max(scores, axis=1, keepdims=True)
-        expo = jnp.exp2((scores - peak) * factor).astype(jnp.bfloat16)
-        total = dot(expo, values[:end])
-        mix_ref[start:end, :] = total[:, :size] / total[:, size:]
-        keep_lse(lse_ref, 0, slice(start, end), head, peak * factor + jnp.log2(total[:, size:]))
+    ones = jnp.ones((nbytes, size), jnp.bfloat16)
+
+    for h in range(width // size):
+        at = slice(h * size, (h + 1) * size)
+        values = jnp.concatenate([v_ref[:, at], ones], axis=1)
+        head = step * (width // size) + h
+        for start in range(0, nbytes, TILE):
+            end = start + TILE
+            scores = dot_t(q_ref[start:end, at], k_ref[:end, at])
+            last = jnp.where(causal, scores[:, start:end], LOW)
+            scores = last if start == 0 else jnp.concatenate([scores[:, :start], last], axis=1)
+            peak = jnp.max(scores, axis=1, keepdims=True)
+            expo = jnp.exp2((scores - peak) * factor).astype(jnp.bfloat16)
+            total = dot(expo, values[:end])
+            mix_ref[start:end, at] = (total[:, :size] / total[:, size:]).astype(jnp.bfloat16)
+            lse = peak * factor + jnp.log2(total[:, size:])
+            columns_ref[start:end, :] = jnp.where(col == head, lse, columns_ref[start:end, :])
+
+    @pl.when(step == pl.num_programs(0) - 1)
+    def _():
+        keep_lse(lse_ref, 0, columns_ref, lse_ref.shape[0] // 4)
 
 
 def own_attention(q, k, v):
     nbytes, width = q.shape
-    block = pl.BlockSpec((nbytes, TILE), lambda h: (0, h))
+    block = pl.BlockSpec((nbytes, GROUP * TILE), lambda h: (0, h))
+    rows = (4 * (width // TILE), nbytes)
     return pl.pallas_call(
-        own_kernel,
-        grid=(width // TILE,),
+        functools.partial(own_kernel),
+        grid=(width // TILE // GROUP,),
         in_specs=[block] * 3,
-        out_specs=[block, pl.BlockSpec((4 * (width // TILE), nbytes), lambda h: (0, 0))],
+        out_specs=[block, pl.BlockSpec(rows, lambda h: (0, 0))],
         out_shape=[
-            jax.ShapeDtypeStruct((nbytes, width), jnp.float32),
-            jax.ShapeDtypeStruct((4 * (width // TILE), nbytes), jnp.bfloat16),
+            jax.ShapeDtypeStruct((nbytes, width), jnp.bfloat16),
+            jax.ShapeDtypeStruct(rows, jnp.bfloat16),
         ],
+        scratch_shapes=[pltpu.VMEM((nbytes, TILE), jnp.float32)],
         cost_estimate=SMALL,
         compiler_params=pltpu.CompilerParams(vmem_limit_bytes=24 * 2**20),
         name="own_attention",
     )(q, k, v)
 
 
-def cross_kernel(q_ref, k_ref, v_ref, out_ref):
-    head = pl.program_id(0)
-    nbytes, size = q_ref.shape
+def cross_kernel(steps, q_ref, k_ref, v_ref, out_ref, columns_ref):
+    step = pl.program_id(0)
+    nbytes, width = q_ref.shape
+    size = TILE
     factor = size ** (-0.5) * LOG2E
     row = lax.broadcasted_iota(jnp.int32, (TILE, TILE), 0)
     col = lax.broadcasted_iota(jnp.int32, (TILE, TILE), 1)
-    values = jnp.concatenate([v_ref[...], jnp.ones((nbytes, size), jnp.bfloat16)], axis=1)
-    columns = pl.ds(pl.multiple_of(head * size, size), size)
-
-    for start in range(0, nbytes, TILE):
-        end = start + TILE
-        scores = dot_t(q_ref[start:end, :], k_ref[start:, :])
-        first = jnp.where(col > row, scores[:, :TILE], LOW)
-        scores = jnp.concatenate([first, scores[:, TILE:]], axis=1) if end < nbytes else first
-        peak = jnp.max(scores, axis=1, keepdims=True)
-        expo = jnp.exp2((scores - peak) * factor)
-        if end == nbytes:
-            expo = jnp.where(col > row, expo, 0.0)
-        total = dot(expo.astype(jnp.bfloat16), values[start:])
-        norm = total[:, size:]
-        some = norm > 0
-        norm = jnp.where(some, norm, 1.0)
-        out_ref[start:end, columns] = (total[:, :size] / norm).astype(jnp.bfloat16)
-        lse = jnp.where(some, peak * factor + jnp.log2(norm), LOW)
-        keep_lse(out_ref, nbytes, slice(start, end), head, lse)
+    ones = jnp.ones((nbytes, size), jnp.bfloat16)
+
+    for h in range(width // size):
+        at = slice(h * size, (h + 1) * size)
+        values = jnp.concatenate([v_ref[:, at], ones], axis=1)
+        head = step * (width // size) + h
+        columns = pl.ds(pl.multiple_of(head * size, size), size)
+        for start in range(0, nbytes, TILE):
+            end = start + TILE
+            scores = dot_t(q_ref[start:end, at], k_ref[start:, at])
+            first = jnp.where(col > row, scores[:, :TILE], LOW)
+            scores = jnp.concatenate([first, scores[:, TILE:]], axis=1) if end < nbytes else first
+            peak = jnp.max(scores, axis=1, keepdims=True)
+            expo = jnp.exp2((scores - peak) * factor)
+            if end == nbytes:
+                expo = jnp.where(col > row, expo, 0.0)
+            total = dot(expo.astype(jnp.bfloat16), values[start:])
+            norm = total[:, size:]
+            some = norm > 0
+            norm = jnp.where(some, norm, 1.0)
+            out_ref[start:end, columns] = (total[:, :size] / norm).astype(jnp.bfloat16)
+            lse = jnp.where(some, peak * factor + jnp.log2(norm), LOW)
+            columns_ref[start:end, :] = jnp.where(col == head, lse, columns_ref[start:end, :])
+
+    @pl.when(step == steps - 1)
+    def _():
+        keep_lse(out_ref, nbytes, columns_ref, steps * (width // size))
 
 
 def cross_attention(q, k, v, first, count):
     nbytes, width = q.shape
-    block = pl.BlockSpec((nbytes, TILE), lambda h: (0, h + first))
+    size = GROUP * TILE
+    block = pl.BlockSpec((nbytes, size), lambda h: (0, h + first // GROUP))
     out = (nbytes + 4 * count, count * TILE)
     return pl.pallas_call(
-        cross_kernel,
-        grid=(count,),
-        in_specs=[pl.BlockSpec((nbytes, TILE), lambda h: (0, h)), block, block],
+        functools.partial(cross_kernel, count // GROUP),
+        grid=(count // GROUP,),
+        in_specs=[pl.BlockSpec((nbytes, size), lambda h: (0, h)), block, block],
         out_specs=pl.BlockSpec(out, lambda h: (0, 0)),
         out_shape=jax.ShapeDtypeStruct(out, jnp.bfloat16),
+        scratch_shapes=[pltpu.VMEM((nbytes, TILE), jnp.float32)],
         cost_estimate=SMALL,
         compiler_params=pltpu.CompilerParams(vmem_limit_bytes=24 * 2**20),
         name="cross_attention",
@@ -155,7 +178,7 @@
                 at = slice(h * size, (h + 1) * size)
                 gap = jnp.where(leading, LOW, part_lse[:, at] - own_lse[:, at])
                 share = 1.0 / (1.0 + jnp.exp2(gap))
-                own = own_ref[rows, (first + h) * size : (first + h + 1) * size]
+                own = own_ref[rows, (first + h) * size : (first + h + 1) * size].astype(jnp.float32)
                 part = part_ref[rows, at].astype(jnp.float32)
                 mix = part + (own - part) * share
                 squares += mix * mix
@@ -209,14 +232,11 @@
         enc_ref, bias_ref, pgain_ref, ogain_ref, dgain_ref, start_col_ref, start_row_ref,
         byte_ref, patch_ref, all_ref, up_ref, kv_w_ref, kv_ref, mix_ref, in_ref, sems,
     ) = refs[n_blocks + n_weights :]
-    copies = plan(at_ref, weights, up_ref, kv_w_ref)
-    copies = [
-        pltpu.make_async_copy(source, target, sems.at[i]) for i, (source, target) in enumerate(copies)
-    ]
-    for copy in copies:
+    ups, kvs = plan(at_ref, weights, up_ref, kv_w_ref)
+    ups = [pltpu.make_async_copy(*copy, sems.at[i]) for i, copy in enumerate(ups)]
+    kvs = [pltpu.make_async_copy(*copy, sems.at[len(ups) + i]) for i, copy in enumerate(kvs)]
+    for copy in ups:
         copy.start()
-    for copy in copies:
-        copy.wait()
 
     slots = patch_ref.shape[0]
     offset = 0
@@ -224,14 +244,20 @@
         all_ref[offset : offset + block.shape[0], :] = block[...]
         offset += block.shape[0]
     step = 4 * slots
+    for copy in ups:
+        copy.wait()
+    for copy in kvs:
+        copy.start()
     for r in range(0, offset, step):
         rows = slice(r, min(r + step, offset))
         lifted = dot(all_ref[rows, :], up_ref[...])
         scale = lax.rsqrt(jnp.mean(lifted * lifted, axis=1, keepdims=True) + epsilon)
-        patch_in = (lifted * scale * pgain_ref[...]).astype(jnp.bfloat16)
-        if r == 0:
-            in_ref[...] = patch_in[:slots]
-        kv_ref[rows, :] = dot(patch_in, kv_w_ref[...]).astype(jnp.bfloat16)
+        in_ref[rows, :] = (lifted * scale * pgain_ref[...]).astype(jnp.bfloat16)
+    for copy in kvs:
+        copy.wait()
+    for r in range(0, offset, step):
+        rows = slice(r, min(r + step, offset))
+        kv_ref[rows, :] = dot(in_ref[rows, :], kv_w_ref[...]).astype(jnp.bfloat16)
 
     size = patch_ref.shape[1] // PATCH_QUERY_HEADS
     rows = kv_ref.shape[0]
@@ -251,7 +277,7 @@
             queries = []
             for g in range(groups):
                 at = (first + g) // 2 * pair
-                q = in_ref[:, at : at + pair].astype(jnp.float32)
+                q = in_ref[:slots, at : at + pair].astype(jnp.float32)
                 if g % 2 != half:
                     q = pltpu.roll(q, size, 1)
                 queries.append(jnp.where(lane_half == half, q, 0.0).astype(jnp.bfloat16))
@@ -279,14 +305,14 @@
     size = TILE
     factor = size ** (-0.5) * LOG2E
     ones = jnp.ones((slots, size), jnp.bfloat16)
-    for start in range(0, nbytes, TILE):
-        place = lax.broadcasted_iota(jnp.int32, (TILE, slots), 0) + start
+    for start in range(0, nbytes, 512):
+        place = lax.broadcasted_iota(jnp.int32, (512, slots), 0) + start
         allowed = start_row_ref[...] <= place
         crosses = []
-        squares = jnp.zeros((TILE, size), jnp.float32)
+        squares = jnp.zeros((512, size), jnp.float32)
         for h in range(width // size):
             scores = dot_t(
-                enc_ref[start : start + TILE, h * size : (h + 1) * size],
+                enc_ref[start : start + 512, h * size : (h + 1) * size],
                 patch_ref[:, 2 * h * size : (2 * h + 1) * size],
             )
             scores = jnp.where(allowed, scores * factor, LOW)
@@ -302,7 +328,7 @@
         scale = lax.rsqrt(jnp.sum(squares, axis=1, keepdims=True) / width + epsilon)
         for h, cross in enumerate(crosses):
             at = h * size
-            byte_ref[start : start + TILE, at : at + size] = (
+            byte_ref[start : start + 512, at : at + size] = (
                 cross * scale * dgain_ref[:, at : at + size]
             ).astype(jnp.bfloat16)
 
@@ -327,7 +353,7 @@
             pltpu.VMEM(kv_shape, jnp.bfloat16),
             pltpu.VMEM((rows, kv_shape[1]), jnp.bfloat16),
             pltpu.VMEM((slots, n_patch_width), jnp.float32),
-            pltpu.VMEM((slots, n_patch_width), jnp.bfloat16),
+            pltpu.VMEM((rows, n_patch_width), jnp.bfloat16),
             pltpu.SemaphoreType.DMA((n_copies,)),
         ],
         cost_estimate=SMALL,
@@ -347,25 +373,25 @@
 
 
 def whole_plan(at_ref, weights, up_ref, kv_ref):
-    return [(weights[0], up_ref), (weights[1], kv_ref)]
+    return [(weights[0], up_ref)], [(weights[1], kv_ref)]
 
 
 def quarter_plan(at_ref, weights, up_ref, kv_ref):
     z, doc = at_ref[0] // 2, at_ref[1]
     up_rows, up_cols = up_ref.shape[0] // 4, up_ref.shape[1] // 4
     kv_rows, kv_cols = kv_ref.shape[0] // 8, kv_ref.shape[1] // 4
-    copies = []
+    ups, kvs = [], []
     for i, ref in enumerate(weights):
         block, part = i // 4, i % 4
         zb, q = z ^ block, doc ^ part
         cols = pl.ds(pl.multiple_of(q * up_cols, up_cols), up_cols)
         rows = pl.ds(pl.multiple_of(zb * up_rows, up_rows), up_rows)
-        copies.append((ref.at[:up_rows, :], up_ref.at[rows, cols]))
+        ups.append((ref.at[:up_rows, :], up_ref.at[rows, cols]))
         cols = pl.ds(pl.multiple_of(q * kv_cols, kv_cols), kv_cols)
         for y in range(2):
             rows = pl.ds(pl.multiple_of((2 * zb + y) * kv_rows, kv_rows), kv_rows)
-            copies.append((ref.at[up_rows:, y * kv_cols : (y + 1) * kv_cols], kv_ref.at[rows, cols]))
-    return copies
+            kvs.append((ref.at[up_rows:, y * kv_cols : (y + 1) * kv_cols], kv_ref.at[rows, cols]))
+    return ups, kvs
 
 
 def paired_weights(w_up, w_kv):
@@ -412,16 +438,16 @@
     q_next = [passed_along(h, "seq", -1) for h in halves]
     if paired:
         z_blocks = [exchanged(mine, "seq", 2 * j) for j in (1, 2)]
-        z_blocks.append(exchanged(after(mine, q_next[0]), "seq", 6))
+        z_blocks.append(exchanged(z_blocks[1], "seq", 2))
         across = [exchanged(mine, "doc", 2)]
     own, lse = own_attention(byte_q, byte_k, byte_v)
     first = [lse] + (across[:1] if paired else [])
     low = cross_attention(after(q_next[0], *first), byte_k, byte_v, 0, count)
-    second = [low] + (z_blocks[:1] if paired else [])
+    second = [low]
     high = cross_attention(after(q_next[1], *second), byte_k, byte_v, count, count)
     parts = [passed_along(partial, "seq", 1) for partial in (low, high)]
     if paired:
-        across += [exchanged(after(z, high), "doc", 2) for z in z_blocks[:2]]
+        across += [exchanged(after(z, high), "doc", 2) for z in z_blocks]
         parts[1] = after(parts[1], z_blocks[1], z_blocks[2], across[1])
 
     starts = lax.dynamic_index_in_dim(patch_start, device, 0, keepdims=False)
@@ -432,7 +458,6 @@
         starts[:, None], ends[:, None],
     )
     if paired:
-        across.append(exchanged(after(z_blocks[2], pooled), "doc", 2))
         weights = []
         for z, x in zip([mine] + z_blocks, across):
             weights += [z, exchanged(after(z, pooled), "doc", 1), x, exchanged(after(x, pooled), "doc", 1)]
@@ -444,7 +469,8 @@
     place = jnp.arange(slots, dtype=jnp.int32)
     own_allowed = (place[None, :] <= place[:, None]) & (starts < nbytes)[None, :]
     if paired:
-        zs = [exchanged(pooled, "seq", 2 * j) for j in range(1, 4)]
+        zs = [exchanged(pooled, "seq", 2 * j) for j in range(1, 3)]
+        zs.append(exchanged(zs[1], "seq", 2))
         ys = [exchanged(b, "seq", 1) for b in [pooled] + zs]
         blocks = [pooled] + zs + ys
         order = jnp.stack([device ^ m for m in (2, 4, 6, 1, 3, 5, 7)])

time: 154 us -> 136 us (0.88)
  Pallas kernels: 44.5 us -> 32.6 us
  local copies, waits for them, and re-layouts: 12.9 us -> 7.68 us
    pallas_call x3, Pallas kernels: 21.2 us -> 12.1 us  [the longest x2 6.11 us: cross_attention(): pl.pallas_call(functools.partial(cross_kernel, count // GROUP), grid=(cou...]
    ppermute x23, waiting for transfers between devices: 46.7 us -> 38.3 us  [exchanged(): lax.ppermute(value, axis, [(i, i ^ mask) for i in range(lax.axis_size(axi...]
    ppermute x4, waiting for transfers between devices: 0.01 us -> 7.04 us  [passed_along(): return lax.ppermute(value, axis, pairs)]
    ppermute x4, starting transfers between devices: 19.4 us -> 23.3 us  [passed_along(): return lax.ppermute(value, axis, pairs)]
    ppermute x23, starting transfers between devices: 28.7 us -> 25.4 us  [exchanged(): lax.ppermute(value, axis, [(i, i ^ mask) for i in range(lax.axis_size(axi...]
    unnamed x38, local copies, waits for them, and re-layouts: 8.57 us -> 5.47 us
    pallas_call x1, Pallas kernels: 19.9 us -> 17 us  [patches(): pl.pallas_call(functools.partial(patch_kernel, len(blocks), plan, len(wei...]
    slice x1, local copies, waits for them, and re-layouts: 2.23 us -> 0.07 us  [per_device(): byte_q[:, i * count * TILE:(i + 1) * count * TILE]]
  transfers between devices with their start and end apart: 27 -> 27, of which waited for: 13 -> 15; matrix products, arithmetic and copies ran while one was open for 2% -> 1% of each run, Pallas kernels for 16% -> 12%
where the time goes in v3:
time: 136 us
  starting transfers between devices  48.7 us (36%)
  waiting for transfers between devices  45.3 us (33%)
  Pallas kernels  32.6 us (24%)
  local copies, waits for them, and re-layouts  7.68 us (6%)
    ppermute x23, waiting for transfers between devices, exchanged(): lax.ppermute(value, axis, [(i, i ^ mask) for i in range(lax.axis_size(axi...  38.3 us
    ppermute x23, starting transfers between devices, exchanged(): lax.ppermute(value, axis, [(i, i ^ mask) for i in range(lax.axis_size(axi...  25.4 us
    ppermute x4, starting transfers between devices, passed_along(): return lax.ppermute(value, axis, pairs)  23.3 us
    pallas_call x1, Pallas kernels, patches(): pl.pallas_call(functools.partial(patch_kernel, len(blocks), plan, len(wei...  17 us
    ppermute x4, waiting for transfers between devices, passed_along(): return lax.ppermute(value, axis, pairs)  7.04 us
    pallas_call x2, Pallas kernels, cross_attention(): pl.pallas_call(functools.partial(cross_kernel, count // GROUP), grid=(cou...  6.11 us
    pallas_call x1, Pallas kernels, own_attention(): pl.pallas_call(functools.partial(own_kernel), grid=(width // TILE // GROU...  5.95 us
    unnamed x38, local copies, waits for them, and re-layouts  5.47 us
  transfers between devices with their start and end apart: 27, of which 15 were waited for; matrix products, arithmetic and copies ran while one was open for 1% of the time, Pallas kernels for 12%

profile of v3, /device:TPU:0, one launch (start us, length us, event | category | flops | bytes accessed | tf_op | source)
XLA Modules:
  0.0 135.8 jit_solution(14649722949728372789)
XLA Ops:
  0.6 0.0 copy-start
  0.7 1.0 copy-done
  1.7 0.9 constant_dynamic-slice_fusion
  2.6 3.0 %collective-permute-start = (bf16[256,512]{1,0:T(8,128)(2,1)S(1)}, bf16[256,512]{1,0:T(8,128)(2,1)S(1)}, u32[]{:S(2)}, u32[]{:S(2)}) collective-permute-start(bf16[256,512]{1,0:T(8,128)(2,1)S(1)} %maximum_maximum_fusion.1), channel_id=1, source_target_pairs={{0,4},{4,0},{8,12},{12,8},{16,20},{20,16},{24,28},{28,24},{1,5},{5... | collective-permute-start | bytes 786440 | tf_op jit(solution)/shard_map/ppermute | solution.py:366
  5.6 0.1 fusion.2
  5.7 6.2 %collective-permute-done = bf16[256,512]{1,0:T(8,128)(2,1)S(1)} collective-permute-done((bf16[256,512]{1,0:T(8,128)(2,1)S(1)}, bf16[256,512]{1,0:T(8,128)(2,1)S(1)}, u32[]{:S(2)}, u32[]{:S(2)}) %collective-permute-start) | collective-permute-done | bytes 262176 | tf_op jit(solution)/shard_map/ppermute | solution.py:366
  11.9 0.1 broadcast_select_fusion.1
  12.2 1.8 %collective-permute-start.2 = (bf16[512,512]{1,0:T(8,128)(2,1)S(1)}, bf16[512,512]{1,0:T(8,128)(2,1)S(1)}, u32[]{:S(2)}, u32[]{:S(2)}) collective-permute-start(bf16[512,512]{1,0:T(8,128)(2,1)S(1)} %maximum_maximum_fusion.refs_8_), channel_id=1, source_target_pairs={{0,2},{1,3},{2,0},{3,1},{4,6},{5,7},{6,4},{7,5},{8,10},{9,11},{10,... | collective-permute-start | bytes 1572872 | tf_op jit(solution)/shard_map/ppermute | solution.py:366
  14.0 1.3 collective-permute-start.1
  15.2 1.3 collective-permute-start.4
  16.5 4.8 %collective-permute-start.8 = (bf16[512,512]{1,0:T(8,128)(2,1)S(1)}, bf16[512,512]{1,0:T(8,128)(2,1)}, u32[]{:S(2)}, u32[]{:S(2)}) collective-permute-start(bf16[512,512]{1,0:T(8,128)(2,1)S(1)} %maximum_maximum_fusion.refs_8_), channel_id=1, source_target_pairs={{0,8},{4,12},{8,0},{12,4},{16,24},{20,28},{24,16},{28,20},{1,9},{5... | collective-permute-start | bytes 1572872 | tf_op jit(solution)/shard_map/ppermute | solution.py:366
  21.3 2.6 %collective-permute-start.6 = (bf16[512,512]{1,0:T(8,128)(2,1)S(1)}, bf16[512,512]{1,0:T(8,128)(2,1)}, u32[]{:S(2)}, u32[]{:S(2)}) collective-permute-start(bf16[512,512]{1,0:T(8,128)(2,1)S(1)} %maximum_maximum_fusion.refs_8_), channel_id=1, source_target_pairs={{0,16},{4,20},{8,24},{12,28},{16,0},{20,4},{24,8},{28,12},{1,17},{... | collective-permute-start | bytes 1572872 | tf_op jit(solution)/shard_map/ppermute | solution.py:366
  23.9 5.9 %own_attention.1 = (bf16[512,1024]{1,0:T(8,128)(2,1)S(1)}, bf16[32,512]{1,0:T(8,128)(2,1)S(1)}) custom-call(bf16[512,1024]{1,0:T(8,128)(2,1)S(1)} %copy-done.3, bf16[512,1024]{1,0:T(8,128)(2,1)S(1)} %copy-done.1, bf16[512,1024]{1,0:T(8,128)(2,1)S(1)} %copy-done.2), custom_call_target="tpu_custom_call" | custom-call | flops 1 | bytes 1 | tf_op jit(solution)/shard_map/own_attention/pallas_call | solution.py:81
  29.9 0.8 collective-permute-done.1.q_ref
  30.7 2.7 %cross_attention.2 = bf16[528,512]{1,0:T(8,128)(2,1)S(1)} custom-call(bf16[512,512]{1,0:T(8,128)(2,1)S(1)} %collective-permute-done.1.q_ref, bf16[512,1024]{1,0:T(8,128)(2,1)S(1)} %copy-done.1, bf16[512,1024]{1,0:T(8,128)(2,1)S(1)} %copy-done.2), custom_call_target="tpu_custom_call" | custom-call | flops 1 | bytes 1 | tf_op jit(solution)/shard_map/cross_attention/pallas_call | solution.py:138
  33.3 6.2 %collective-permute-done.4.q_ref = bf16[512,512]{1,0:T(8,128)(2,1)S(1)} collective-permute-done((bf16[512,512]{1,0:T(8,128)(2,1)S(1)}, bf16[512,512]{1,0:T(8,128)(2,1)S(1)}, u32[]{:S(2)}, u32[]{:S(2)}) %collective-permute-start.4) | collective-permute-done | bytes 524320 | tf_op jit(solution)/shard_map/ppermute | solution.py:372
  39.6 3.5 %cross_attention.3 = bf16[528,512]{1,0:T(8,128)(2,1)} custom-call(bf16[512,512]{1,0:T(8,128)(2,1)S(1)} %collective-permute-done.4.q_ref, bf16[512,1024]{1,0:T(8,128)(2,1)S(1)} %copy-done.1, bf16[512,1024]{1,0:T(8,128)(2,1)S(1)} %copy-done.2), custom_call_target="tpu_custom_call" | custom-call | flops 1 | bytes 1 | tf_op jit(solution)/shard_map/cross_attention/pallas_call | solution.py:138
  43.0 18.6 %collective-permute-start.5 = (bf16[528,512]{1,0:T(8,128)(2,1)}, bf16[528,512]{1,0:T(8,128)(2,1)}, u32[]{:S(2)}, u32[]{:S(2)}) collective-permute-start(bf16[528,512]{1,0:T(8,128)(2,1)} %cross_attention.3), channel_id=1, source_target_pairs={{0,4},{4,8},{8,12},{12,16},{16,20},{20,24},{24,28},{1,5},{5,9},{9,... | collective-permute-start | bytes 1622024 | tf_op jit(solution)/shard_map/ppermute | solution.py:372
  61.7 2.1 %collective-permute-start.3 = (bf16[528,512]{1,0:T(8,128)(2,1)S(1)}, bf16[528,512]{1,0:T(8,128)(2,1)}, u32[]{:S(2)}, u32[]{:S(2)}) collective-permute-start(bf16[528,512]{1,0:T(8,128)(2,1)S(1)} %cross_attention.2), channel_id=1, source_target_pairs={{0,4},{4,8},{8,12},{12,16},{16,20},{20,24},{24,28},{1,5},{5,9},{9,... | collective-permute-start | bytes 1622024 | tf_op jit(solution)/shard_map/ppermute | solution.py:372
  63.7 3.5 %collective-permute-start.7 = (bf16[512,512]{1,0:T(8,128)(2,1)}, bf16[512,512]{1,0:T(8,128)(2,1)}, u32[]{:S(2)}, u32[]{:S(2)}) collective-permute-start(bf16[512,512]{1,0:T(8,128)(2,1)} %collective-permute-done.6.refs_16_), channel_id=1, source_target_pairs={{0,8},{4,12},{8,0},{12,4},{16,24},{20,28},{24,16},{28,20},{1,9},{5... | collective-permute-start | bytes 1572872 | tf_op jit(solution)/shard_map/ppermute | solution.py:366
  67.3 0.5 collective-permute-start.9
  67.8 0.7 copy-done.17
  68.5 0.0 copy-done.14
  68.5 0.1 slice_bitcast_fusion
  68.6 1.5 %collective-permute-start.22 = (bf16[512,512]{1,0:T(8,128)(2,1)}, bf16[512,512]{1,0:T(8,128)(2,1)}, u32[]{:S(2)}, u32[]{:S(2)}) collective-permute-start(bf16[512,512]{1,0:T(8,128)(2,1)} %collective-permute-done.6.refs_16_), channel_id=1, source_target_pairs={{0,2},{1,3},{2,0},{3,1},{4,6},{5,7},{6,4},{7,5},{8,10},{9,11},{10,... | collective-permute-start | bytes 1572872 | tf_op jit(solution)/shard_map/ppermute | solution.py:366
  70.1 0.1 add_bitcast_fusion
  70.2 0.1 copy.14.refs_5_
  70.3 0.1 copy.13.refs_4_.refs_29_
  70.4 0.1 stack.59
  70.5 5.4 %collective-permute-done.7.refs_20_ = bf16[512,512]{1,0:T(8,128)(2,1)} collective-permute-done((bf16[512,512]{1,0:T(8,128)(2,1)}, bf16[512,512]{1,0:T(8,128)(2,1)}, u32[]{:S(2)}, u32[]{:S(2)}) %collective-permute-start.7) | collective-permute-done | bytes 524320 | tf_op jit(solution)/shard_map/ppermute | solution.py:366
  75.9 6.6 %collective-permute-done.9.refs_14_ = bf16[512,512]{1,0:T(8,128)(2,1)} collective-permute-done((bf16[512,512]{1,0:T(8,128)(2,1)}, bf16[512,512]{1,0:T(8,128)(2,1)}, u32[]{:S(2)}, u32[]{:S(2)}) %collective-permute-start.9) | collective-permute-done | bytes 524320 | tf_op jit(solution)/shard_map/ppermute | solution.py:366
  82.5 0.7 copy-done.9
  83.1 3.6 %pool.1 = (bf16[512,1024]{1,0:T(8,128)(2,1)S(1)}, bf16[80,1024]{1,0:T(8,128)(2,1)S(1)}) custom-call(s32[1]{0:T(128)} %bitcast.2.lead_ref, bf16[512,1024]{1,0:T(8,128)(2,1)S(1)} %get-tuple-element.24.own_ref, bf16[32,512]{1,0:T(8,128)(2,1)S(1)} %get-tuple-element.25.lse_ref, bf16[528,512]{1,0:T(8,128)(2,1)} %collective-permute-done.3.refs_0_, ...), custom_call_target="tpu_custom_call" | custom-call | flops 1 | bytes 1 | tf_op jit(solution)/shard_map/pool/pallas_call | solution.py:214
  86.7 1.0 copy-done.4
  87.7 0.6 collective-permute-start.25
  88.3 1.0 collective-permute-start.13
  89.3 2.5 %collective-permute-start.10 = (bf16[80,1024]{1,0:T(8,128)(2,1)S(1)}, bf16[80,1024]{1,0:T(8,128)(2,1)}, u32[]{:S(2)}, u32[]{:S(2)}) collective-permute-start(bf16[80,1024]{1,0:T(8,128)(2,1)S(1)} %get-tuple-element.32.refs_0_), channel_id=1, source_target_pairs={{0,8},{4,12},{8,0},{12,4},{16,24},{20,28},{24,16},{28,20},{1,9},{5... | collective-permute-start | bytes 491528 | tf_op jit(solution)/shard_map/ppermute | solution.py:366
  91.8 3.4 %collective-permute-done.11.refs_2_ = bf16[80,1024]{1,0:T(8,128)(2,1)S(1)} collective-permute-done((bf16[80,1024]{1,0:T(8,128)(2,1)S(1)}, bf16[80,1024]{1,0:T(8,128)(2,1)S(1)}, u32[]{:S(2)}, u32[]{:S(2)}) %collective-permute-start.11) | collective-permute-done | bytes 163872 | tf_op jit(solution)/shard_map/ppermute | solution.py:366
  95.3 0.1 collective-permute-start.17
  95.4 0.7 copy-done.7
  96.0 0.5 collective-permute-start.18
  96.5 0.4 collective-permute-done.10.refs_1_
  96.9 0.6 gather_fusion
  97.5 0.1 stack.67
  97.5 3.1 %collective-permute-done.15.refs_6_ = bf16[80,1024]{1,0:T(8,128)(2,1)} collective-permute-done((bf16[80,1024]{1,0:T(8,128)(2,1)S(1)}, bf16[80,1024]{1,0:T(8,128)(2,1)}, u32[]{:S(2)}, u32[]{:S(2)}) %collective-permute-start.15) | collective-permute-done | bytes 163872 | tf_op jit(solution)/shard_map/ppermute | solution.py:366
  100.7 5.4 %collective-permute-done.12.refs_3_ = bf16[80,1024]{1,0:T(8,128)(2,1)} collective-permute-done((bf16[80,1024]{1,0:T(8,128)(2,1)S(1)}, bf16[80,1024]{1,0:T(8,128)(2,1)}, u32[]{:S(2)}, u32[]{:S(2)}) %collective-permute-start.12) | collective-permute-done | bytes 163872 | tf_op jit(solution)/shard_map/ppermute | solution.py:366
  106.1 2.0 %collective-permute-start.16 = (bf16[80,1024]{1,0:T(8,128)(2,1)}, bf16[80,1024]{1,0:T(8,128)(2,1)}, u32[]{:S(2)}, u32[]{:S(2)}) collective-permute-start(bf16[80,1024]{1,0:T(8,128)(2,1)} %collective-permute-done.12.refs_3_), channel_id=1, source_target_pairs={{0,4},{4,0},{8,12},{12,8},{16,20},{20,16},{24,28},{28,24},{1,5},{5... | collective-permute-start | bytes 491528 | tf_op jit(solution)/shard_map/ppermute | solution.py:366
  108.1 0.1 broadcast_and_fusion
  108.2 0.1 reshape.364
  108.3 0.6 copy-done.15
  108.9 0.1 pad.1.clone
  109.0 2.8 %collective-permute-done.14.refs_5_ = bf16[80,1024]{1,0:T(8,128)(2,1)} collective-permute-done((bf16[80,1024]{1,0:T(8,128)(2,1)}, bf16[80,1024]{1,0:T(8,128)(2,1)}, u32[]{:S(2)}, u32[]{:S(2)}) %collective-permute-start.14) | collective-permute-done | bytes 163872 | tf_op jit(solution)/shard_map/ppermute | solution.py:366
  111.7 1.8 %collective-permute-done.16.refs_7_ = bf16[80,1024]{1,0:T(8,128)(2,1)} collective-permute-done((bf16[80,1024]{1,0:T(8,128)(2,1)}, bf16[80,1024]{1,0:T(8,128)(2,1)}, u32[]{:S(2)}, u32[]{:S(2)}) %collective-permute-start.16) | collective-permute-done | bytes 163872 | tf_op jit(solution)/shard_map/ppermute | solution.py:366
  113.5 0.5 collective-permute-start.23
  114.0 0.1 collective-permute-start.24
  114.1 0.4 collective-permute-start.26
  114.5 0.1 pad_add_fusion.at_ref
  114.7 1.0 collective-permute-done.21.refs_17_
  115.6 0.7 collective-permute-done.23.refs_19_
  116.4 0.7 collective-permute-done.24.refs_21_
  117.1 0.7 collective-permute-done.26.refs_23_
  117.9 0.0 copy-done.12
  117.9 0.7 copy-done.13
  118.7 17.0 %patches.1 = (bf16[512,1024]{1,0:T(8,128)(2,1)}, bf16[80,2048]{1,0:T(8,128)(2,1)}) custom-call(s32[2]{0:T(128)S(1)} %pad_add_fusion.at_ref, bf16[80,1024]{1,0:T(8,128)(2,1)S(1)} %get-tuple-element.32.refs_0_, bf16[80,1024]{1,0:T(8,128)(2,1)} %collective-permute-done.10.refs_1_, bf16[80,1024]{1,0:T(8,128)(2,1)S(1)} %collective-permute-done.11.refs_2_, ...), custom_call_target="tpu_custom_call" | custom-call | flops 1 | bytes 1 | tf_op jit(solution)/shard_map/patches/pallas_call | solution.py:339
  (64 shorter events, 0.3 us)
Async XLA Ops:
  0.6 1.0 copy-start
  0.6 5.0 %copy-start.3 = (bf16[512,1024]{1,0:T(8,128)(2,1)S(1)}, bf16[512,1024]{1,0:T(8,128)(2,1)}, u32[]{:S(2)}) copy-start(bf16[512,1024]{1,0:T(8,128)(2,1)} %q_ref) | copy-start | bytes 3145732
  2.6 9.3 %collective-permute-start = (bf16[256,512]{1,0:T(8,128)(2,1)S(1)}, bf16[256,512]{1,0:T(8,128)(2,1)S(1)}, u32[]{:S(2)}, u32[]{:S(2)}) collective-permute-start(bf16[256,512]{1,0:T(8,128)(2,1)S(1)} %maximum_maximum_fusion.1), channel_id=1, source_target_pairs={{0,4},{4,0},{8,12},{12,8},{16,20},{20,16},{24,28},{28,24},{1,5},{5... | collective-permute-start | bytes 786440 | tf_op jit(solution)/shard_map/ppermute | solution.py:366
  12.0 11.9 %copy-start.1 = (bf16[512,1024]{1,0:T(8,128)(2,1)S(1)}, bf16[512,1024]{1,0:T(8,128)(2,1)}, u32[]{:S(2)}) copy-start(bf16[512,1024]{1,0:T(8,128)(2,1)} %k_ref.5) | copy-start | bytes 3145732
  12.1 11.9 %copy-start.2 = (bf16[512,1024]{1,0:T(8,128)(2,1)S(1)}, bf16[512,1024]{1,0:T(8,128)(2,1)}, u32[]{:S(2)}) copy-start(bf16[512,1024]{1,0:T(8,128)(2,1)} %v_ref.5) | copy-start | bytes 3145732
  12.2 17.7 %collective-permute-start.2 = (bf16[512,512]{1,0:T(8,128)(2,1)S(1)}, bf16[512,512]{1,0:T(8,128)(2,1)S(1)}, u32[]{:S(2)}, u32[]{:S(2)}) collective-permute-start(bf16[512,512]{1,0:T(8,128)(2,1)S(1)} %maximum_maximum_fusion.refs_8_), channel_id=1, source_target_pairs={{0,2},{1,3},{2,0},{3,1},{4,6},{5,7},{6,4},{7,5},{8,10},{9,11},{10,... | collective-permute-start | bytes 1572872 | tf_op jit(solution)/shard_map/ppermute | solution.py:366
  14.0 16.7 %collective-permute-start.1 = (bf16[512,512]{1,0:T(8,128)(2,1)S(1)}, bf16[512,512]{1,0:T(8,128)(2,1)S(1)}, u32[]{:S(2)}, u32[]{:S(2)}) collective-permute-start(bf16[512,512]{1,0:T(8,128)(2,1)S(1)} %get-tuple-element.26), channel_id=1, source_target_pairs={{4,0},{8,4},{12,8},{16,12},{20,16},{24,20},{28,24},{5,1},{9,5},{13... | collective-permute-start | bytes 1572872 | tf_op jit(solution)/shard_map/ppermute | solution.py:372
  15.2 24.3 %collective-permute-start.4 = (bf16[512,512]{1,0:T(8,128)(2,1)S(1)}, bf16[512,512]{1,0:T(8,128)(2,1)S(1)}, u32[]{:S(2)}, u32[]{:S(2)}) collective-permute-start(bf16[512,512]{1,0:T(8,128)(2,1)S(1)} %get-tuple-element.28), channel_id=1, source_target_pairs={{4,0},{8,4},{12,8},{16,12},{20,16},{24,20},{28,24},{5,1},{9,5},{13... | collective-permute-start | bytes 1572872 | tf_op jit(solution)/shard_map/ppermute | solution.py:372
  16.5 47.2 %collective-permute-start.8 = (bf16[512,512]{1,0:T(8,128)(2,1)S(1)}, bf16[512,512]{1,0:T(8,128)(2,1)}, u32[]{:S(2)}, u32[]{:S(2)}) collective-permute-start(bf16[512,512]{1,0:T(8,128)(2,1)S(1)} %maximum_maximum_fusion.refs_8_), channel_id=1, source_target_pairs={{0,8},{4,12},{8,0},{12,4},{16,24},{20,28},{24,16},{28,20},{1,9},{5... | collective-permute-start | bytes 1572872 | tf_op jit(solution)/shard_map/ppermute | solution.py:366
  21.3 42.4 %collective-permute-start.6 = (bf16[512,512]{1,0:T(8,128)(2,1)S(1)}, bf16[512,512]{1,0:T(8,128)(2,1)}, u32[]{:S(2)}, u32[]{:S(2)}) collective-permute-start(bf16[512,512]{1,0:T(8,128)(2,1)S(1)} %maximum_maximum_fusion.refs_8_), channel_id=1, source_target_pairs={{0,16},{4,20},{8,24},{12,28},{16,0},{20,4},{24,8},{28,12},{1,17},{... | collective-permute-start | bytes 1572872 | tf_op jit(solution)/shard_map/ppermute | solution.py:366
  29.9 3.5 %copy-start.5 = (bf16[512,512]{1,0:T(8,128)(2,1)}, bf16[512,512]{1,0:T(8,128)(2,1)S(1)}, u32[]{:S(2)}) copy-start(bf16[512,512]{1,0:T(8,128)(2,1)S(1)} %collective-permute-done.2.refs_10_) | copy-start | bytes 1572868
  43.0 39.4 %collective-permute-start.5 = (bf16[528,512]{1,0:T(8,128)(2,1)}, bf16[528,512]{1,0:T(8,128)(2,1)}, u32[]{:S(2)}, u32[]{:S(2)}) collective-permute-start(bf16[528,512]{1,0:T(8,128)(2,1)} %cross_attention.3), channel_id=1, source_target_pairs={{0,4},{4,8},{8,12},{12,16},{16,20},{20,24},{24,28},{1,5},{5,9},{9,... | collective-permute-start | bytes 1622024 | tf_op jit(solution)/shard_map/ppermute | solution.py:372
  61.7 20.8 %collective-permute-start.3 = (bf16[528,512]{1,0:T(8,128)(2,1)S(1)}, bf16[528,512]{1,0:T(8,128)(2,1)}, u32[]{:S(2)}, u32[]{:S(2)}) collective-permute-start(bf16[528,512]{1,0:T(8,128)(2,1)S(1)} %cross_attention.2), channel_id=1, source_target_pairs={{0,4},{4,8},{8,12},{12,16},{16,20},{20,24},{24,28},{1,5},{5,9},{9,... | collective-permute-start | bytes 1622024 | tf_op jit(solution)/shard_map/ppermute | solution.py:372
  63.7 12.1 %collective-permute-start.7 = (bf16[512,512]{1,0:T(8,128)(2,1)}, bf16[512,512]{1,0:T(8,128)(2,1)}, u32[]{:S(2)}, u32[]{:S(2)}) collective-permute-start(bf16[512,512]{1,0:T(8,128)(2,1)} %collective-permute-done.6.refs_16_), channel_id=1, source_target_pairs={{0,8},{4,12},{8,0},{12,4},{16,24},{20,28},{24,16},{28,20},{1,9},{5... | collective-permute-start | bytes 1572872 | tf_op jit(solution)/shard_map/ppermute | solution.py:366
  67.3 15.2 %collective-permute-start.9 = (bf16[512,512]{1,0:T(8,128)(2,1)}, bf16[512,512]{1,0:T(8,128)(2,1)}, u32[]{:S(2)}, u32[]{:S(2)}) collective-permute-start(bf16[512,512]{1,0:T(8,128)(2,1)} %collective-permute-done.8.refs_12_), channel_id=1, source_target_pairs={{0,2},{1,3},{2,0},{3,1},{4,6},{5,7},{6,4},{7,5},{8,10},{9,11},{10,... | collective-permute-start | bytes 1572872 | tf_op jit(solution)/shard_map/ppermute | solution.py:366
  67.8 0.7 copy-start.17
  67.8 0.7 copy-start.14
  68.6 26.7 %collective-permute-start.22 = (bf16[512,512]{1,0:T(8,128)(2,1)}, bf16[512,512]{1,0:T(8,128)(2,1)}, u32[]{:S(2)}, u32[]{:S(2)}) collective-permute-start(bf16[512,512]{1,0:T(8,128)(2,1)} %collective-permute-done.6.refs_16_), channel_id=1, source_target_pairs={{0,2},{1,3},{2,0},{3,1},{4,6},{5,7},{6,4},{7,5},{8,10},{9,11},{10,... | collective-permute-start | bytes 1572872 | tf_op jit(solution)/shard_map/ppermute | solution.py:366
  82.4 0.7 copy-start.9
  83.1 12.9 %copy-start.6 = (bf16[512,512]{1,0:T(8,128)(2,1)S(1)}, bf16[512,512]{1,0:T(8,128)(2,1)}, u32[]{:S(2)}) copy-start(bf16[512,512]{1,0:T(8,128)(2,1)} %copy-done.5) | copy-start | bytes 1572868
  83.1 25.8 %copy-start.16 = (bf16[2048]{0:T(1024)(128)(2,1)S(1)}, bf16[2048]{0:T(1024)(128)(2,1)}, u32[]{:S(2)}) copy-start(bf16[2048]{0:T(1024)(128)(2,1)} %param.19) | copy-start | bytes 12292
  86.7 1.0 copy-start.4
  87.7 7.5 %collective-permute-start.11 = (bf16[80,1024]{1,0:T(8,128)(2,1)S(1)}, bf16[80,1024]{1,0:T(8,128)(2,1)S(1)}, u32[]{:S(2)}, u32[]{:S(2)}) collective-permute-start(bf16[80,1024]{1,0:T(8,128)(2,1)S(1)} %get-tuple-element.32.refs_0_), channel_id=1, source_target_pairs={{0,16},{4,20},{8,24},{12,28},{16,0},{20,4},{24,8},{28,12},{1,17},{... | collective-permute-start | bytes 491528 | tf_op jit(solution)/shard_map/ppermute | solution.py:366
  87.7 18.4 %collective-permute-start.25 = (bf16[512,512]{1,0:T(8,128)(2,1)}, bf16[512,512]{1,0:T(8,128)(2,1)}, u32[]{:S(2)}, u32[]{:S(2)}) collective-permute-start(bf16[512,512]{1,0:T(8,128)(2,1)} %collective-permute-done.7.refs_20_), channel_id=1, source_target_pairs={{0,2},{1,3},{2,0},{3,1},{4,6},{5,7},{6,4},{7,5},{8,10},{9,11},{10,... | collective-permute-start | bytes 1572872 | tf_op jit(solution)/shard_map/ppermute | solution.py:366
  88.3 7.0 %collective-permute-start.13 = (bf16[80,1024]{1,0:T(8,128)(2,1)S(1)}, bf16[80,1024]{1,0:T(8,128)(2,1)S(1)}, u32[]{:S(2)}, u32[]{:S(2)}) collective-permute-start(bf16[80,1024]{1,0:T(8,128)(2,1)S(1)} %get-tuple-element.32.refs_0_), channel_id=1, source_target_pairs={{0,4},{4,0},{8,12},{12,8},{16,20},{20,16},{24,28},{28,24},{1,5},{5... | collective-permute-start | bytes 491528 | tf_op jit(solution)/shard_map/ppermute | solution.py:366
  89.3 7.5 %collective-permute-start.10 = (bf16[80,1024]{1,0:T(8,128)(2,1)S(1)}, bf16[80,1024]{1,0:T(8,128)(2,1)}, u32[]{:S(2)}, u32[]{:S(2)}) collective-permute-start(bf16[80,1024]{1,0:T(8,128)(2,1)S(1)} %get-tuple-element.32.refs_0_), channel_id=1, source_target_pairs={{0,8},{4,12},{8,0},{12,4},{16,24},{20,28},{24,16},{28,20},{1,9},{5... | collective-permute-start | bytes 491528 | tf_op jit(solution)/shard_map/ppermute | solution.py:366
  95.2 5.4 %collective-permute-start.15 = (bf16[80,1024]{1,0:T(8,128)(2,1)S(1)}, bf16[80,1024]{1,0:T(8,128)(2,1)}, u32[]{:S(2)}, u32[]{:S(2)}) collective-permute-start(bf16[80,1024]{1,0:T(8,128)(2,1)S(1)} %collective-permute-done.11.refs_2_), channel_id=1, source_target_pairs={{0,4},{4,0},{8,12},{12,8},{16,20},{20,16},{24,28},{28,24},{1,5},{5... | collective-permute-start | bytes 491528 | tf_op jit(solution)/shard_map/ppermute | solution.py:366
  95.3 18.2 %collective-permute-start.17 = (bf16[512,512]{1,0:T(8,128)(2,1)S(1)}, bf16[512,512]{1,0:T(8,128)(2,1)S(1)}, u32[]{:S(2)}, u32[]{:S(2)}) collective-permute-start(bf16[512,512]{1,0:T(8,128)(2,1)S(1)} %maximum_maximum_fusion.refs_8_), channel_id=1, source_target_pairs={{0,1},{1,0},{2,3},{3,2},{4,5},{5,4},{6,7},{7,6},{8,9},{9,8},{10,11... | collective-permute-start | bytes 1572872 | tf_op jit(solution)/shard_map/ppermute | solution.py:366
  95.3 0.7 copy-start.7
  96.0 18.0 %collective-permute-start.18 = (bf16[512,512]{1,0:T(8,128)(2,1)S(1)}, bf16[512,512]{1,0:T(8,128)(2,1)S(1)}, u32[]{:S(2)}, u32[]{:S(2)}) collective-permute-start(bf16[512,512]{1,0:T(8,128)(2,1)S(1)} %copy-done.6), channel_id=1, source_target_pairs={{0,1},{1,0},{2,3},{3,2},{4,5},{5,4},{6,7},{7,6},{8,9},{9,8},{10,11... | collective-permute-start | bytes 1572872 | tf_op jit(solution)/shard_map/ppermute | solution.py:366
  96.9 17.2 %collective-permute-start.19 = (bf16[512,512]{1,0:T(8,128)(2,1)}, bf16[512,512]{1,0:T(8,128)(2,1)S(1)}, u32[]{:S(2)}, u32[]{:S(2)}) collective-permute-start(bf16[512,512]{1,0:T(8,128)(2,1)} %collective-permute-done.8.refs_12_), channel_id=1, source_target_pairs={{0,1},{1,0},{2,3},{3,2},{4,5},{5,4},{6,7},{7,6},{8,9},{9,8},{10,11... | collective-permute-start | bytes 1572872 | tf_op jit(solution)/shard_map/ppermute | solution.py:366
  100.7 5.4 %collective-permute-start.12 = (bf16[80,1024]{1,0:T(8,128)(2,1)S(1)}, bf16[80,1024]{1,0:T(8,128)(2,1)}, u32[]{:S(2)}, u32[]{:S(2)}) collective-permute-start(bf16[80,1024]{1,0:T(8,128)(2,1)S(1)} %collective-permute-done.11.refs_2_), channel_id=1, source_target_pairs={{0,8},{4,12},{8,0},{12,4},{16,24},{20,28},{24,16},{28,20},{1,9},{5... | collective-permute-start | bytes 491528 | tf_op jit(solution)/shard_map/ppermute | solution.py:366
  100.7 7.6 %copy-start.18 = (bf16[1024]{0:T(1024)(128)(2,1)S(1)}, bf16[1024]{0:T(1024)(128)(2,1)}, u32[]{:S(2)}) copy-start(bf16[1024]{0:T(1024)(128)(2,1)} %param.20) | copy-start | bytes 6148
  106.1 5.6 %collective-permute-start.14 = (bf16[80,1024]{1,0:T(8,128)(2,1)}, bf16[80,1024]{1,0:T(8,128)(2,1)}, u32[]{:S(2)}, u32[]{:S(2)}) collective-permute-start(bf16[80,1024]{1,0:T(8,128)(2,1)} %collective-permute-done.10.refs_1_), channel_id=1, source_target_pairs={{0,4},{4,0},{8,12},{12,8},{16,20},{20,16},{24,28},{28,24},{1,5},{5... | collective-permute-start | bytes 491528 | tf_op jit(solution)/shard_map/ppermute | solution.py:366
  106.1 7.4 %collective-permute-start.16 = (bf16[80,1024]{1,0:T(8,128)(2,1)}, bf16[80,1024]{1,0:T(8,128)(2,1)}, u32[]{:S(2)}, u32[]{:S(2)}) collective-permute-start(bf16[80,1024]{1,0:T(8,128)(2,1)} %collective-permute-done.12.refs_3_), channel_id=1, source_target_pairs={{0,4},{4,0},{8,12},{12,8},{16,20},{20,16},{24,28},{28,24},{1,5},{5... | collective-permute-start | bytes 491528 | tf_op jit(solution)/shard_map/ppermute | solution.py:366
  108.2 0.7 copy-start.15
  108.3 10.4 %copy-start.8 = (bf16[80,1024]{1,0:T(8,128)(2,1)S(1)}, bf16[80,1024]{1,0:T(8,128)(2,1)}, u32[]{:S(2)}) copy-start(bf16[80,1024]{1,0:T(8,128)(2,1)} %copy-done.7) | copy-start | bytes 491524
  111.7 2.9 %collective-permute-start.20 = (bf16[512,512]{1,0:T(8,128)(2,1)}, bf16[512,512]{1,0:T(8,128)(2,1)S(1)}, u32[]{:S(2)}, u32[]{:S(2)}) collective-permute-start(bf16[512,512]{1,0:T(8,128)(2,1)} %collective-permute-done.9.refs_14_), channel_id=1, source_target_pairs={{0,1},{1,0},{2,3},{3,2},{4,5},{5,4},{6,7},{7,6},{8,9},{9,8},{10,11... | collective-permute-start | bytes 1572872 | tf_op jit(solution)/shard_map/ppermute | solution.py:366
  113.5 2.1 %collective-permute-start.21 = (bf16[512,512]{1,0:T(8,128)(2,1)}, bf16[512,512]{1,0:T(8,128)(2,1)S(1)}, u32[]{:S(2)}, u32[]{:S(2)}) collective-permute-start(bf16[512,512]{1,0:T(8,128)(2,1)} %collective-permute-done.6.refs_16_), channel_id=1, source_target_pairs={{0,1},{1,0},{2,3},{3,2},{4,5},{5,4},{6,7},{7,6},{8,9},{9,8},{10,11... | collective-permute-start | bytes 1572872 | tf_op jit(solution)/shard_map/ppermute | solution.py:366
  113.5 2.9 %collective-permute-start.23 = (bf16[512,512]{1,0:T(8,128)(2,1)}, bf16[512,512]{1,0:T(8,128)(2,1)S(1)}, u32[]{:S(2)}, u32[]{:S(2)}) collective-permute-start(bf16[512,512]{1,0:T(8,128)(2,1)} %collective-permute-done.22.refs_18_), channel_id=1, source_target_pairs={{0,1},{1,0},{2,3},{3,2},{4,5},{5,4},{6,7},{7,6},{8,9},{9,8},{10,11... | collective-permute-start | bytes 1572872 | tf_op jit(solution)/shard_map/ppermute | solution.py:366
  114.0 3.1 %collective-permute-start.24 = (bf16[512,512]{1,0:T(8,128)(2,1)}, bf16[512,512]{1,0:T(8,128)(2,1)S(1)}, u32[]{:S(2)}, u32[]{:S(2)}) collective-permute-start(bf16[512,512]{1,0:T(8,128)(2,1)} %collective-permute-done.7.refs_20_), channel_id=1, source_target_pairs={{0,1},{1,0},{2,3},{3,2},{4,5},{5,4},{6,7},{7,6},{8,9},{9,8},{10,11... | collective-permute-start | bytes 1572872 | tf_op jit(solution)/shard_map/ppermute | solution.py:366
  114.1 3.8 %collective-permute-start.26 = (bf16[512,512]{1,0:T(8,128)(2,1)}, bf16[512,512]{1,0:T(8,128)(2,1)S(1)}, u32[]{:S(2)}, u32[]{:S(2)}) collective-permute-start(bf16[512,512]{1,0:T(8,128)(2,1)} %collective-permute-done.25.refs_22_), channel_id=1, source_target_pairs={{0,1},{1,0},{2,3},{3,2},{4,5},{5,4},{6,7},{7,6},{8,9},{9,8},{10,11... | collective-permute-start | bytes 1572872 | tf_op jit(solution)/shard_map/ppermute | solution.py:366
  115.6 2.3 %copy-start.10 = (bf16[512,512]{1,0:T(8,128)(2,1)}, bf16[512,512]{1,0:T(8,128)(2,1)S(1)}, u32[]{:S(2)}) copy-start(bf16[512,512]{1,0:T(8,128)(2,1)S(1)} %collective-permute-done.21.refs_17_) | copy-start | bytes 1572868
  116.4 1.5 %copy-start.11 = (bf16[512,512]{1,0:T(8,128)(2,1)}, bf16[512,512]{1,0:T(8,128)(2,1)S(1)}, u32[]{:S(2)}) copy-start(bf16[512,512]{1,0:T(8,128)(2,1)S(1)} %collective-permute-done.23.refs_19_) | copy-start | bytes 1572868
  117.1 0.8 copy-start.12
  117.9 0.8 copy-start.13

commit v4 on v3

--- a/solution.py
+++ b/solution.py
@@ -448,7 +448,7 @@
     parts = [passed_along(partial, "seq", 1) for partial in (low, high)]
     if paired:
         across += [exchanged(after(z, high), "doc", 2) for z in z_blocks]
-        parts[1] = after(parts[1], z_blocks[1], z_blocks[2], across[1])
+        parts[1] = after(parts[1], z_blocks[1], across[1])
 
     starts = lax.dynamic_index_in_dim(patch_start, device, 0, keepdims=False)
     ends = jnp.concatenate([starts[1:], jnp.full((1,), nbytes, jnp.int32)])

time: 136 us -> 132 us (0.971)
  starting transfers between devices: 48.7 us -> 45.6 us
  waiting for transfers between devices: 45.3 us -> 43.8 us
    ppermute x23, starting transfers between devices: 25.4 us -> 22.3 us  [exchanged(): lax.ppermute(value, axis, [(i, i ^ mask) for i in range(lax.axis_size(axi...]
    ppermute x23, waiting for transfers between devices: 38.3 us -> 36.7 us  [exchanged(): lax.ppermute(value, axis, [(i, i ^ mask) for i in range(lax.axis_size(axi...]
  transfers between devices with their start and end apart: 27 -> 27, of which waited for: 15 -> 14; matrix products, arithmetic and copies ran while one was open for 1% -> 1% of each run, Pallas kernels for 12% -> 12%
where the time goes in v4:
time: 132 us; the launch traced here: 131 us
  starting transfers between devices  45.6 us (35%)
  waiting for transfers between devices  43.8 us (33%)
  Pallas kernels  32.6 us (25%)
  local copies, waits for them, and re-layouts  7.68 us (6%)
    ppermute x23, waiting for transfers between devices, exchanged(): lax.ppermute(value, axis, [(i, i ^ mask) for i in range(lax.axis_size(axi...  36.7 us
    ppermute x4, starting transfers between devices, passed_along(): return lax.ppermute(value, axis, pairs)  23.3 us
    ppermute x23, starting transfers between devices, exchanged(): lax.ppermute(value, axis, [(i, i ^ mask) for i in range(lax.axis_size(axi...  22.3 us
    pallas_call x1, Pallas kernels, patches(): pl.pallas_call(functools.partial(patch_kernel, len(blocks), plan, len(wei...  17 us
    ppermute x4, waiting for transfers between devices, passed_along(): return lax.ppermute(value, axis, pairs)  7.04 us
    pallas_call x2, Pallas kernels, cross_attention(): pl.pallas_call(functools.partial(cross_kernel, count // GROUP), grid=(cou...  6.11 us
    pallas_call x1, Pallas kernels, own_attention(): pl.pallas_call(functools.partial(own_kernel), grid=(width // TILE // GROU...  5.95 us
    unnamed x38, local copies, waits for them, and re-layouts  5.47 us
  transfers between devices with their start and end apart: 27, of which 14 were waited for; matrix products, arithmetic and copies ran while one was open for 1% of the time, Pallas kernels for 12%

profile of v4, /device:TPU:0, one launch (start us, length us, event | category | flops | bytes accessed | tf_op | source)
XLA Modules:
  0.0 131.1 jit_solution(12012897304568088922)
XLA Ops:
  0.6 0.0 copy-start
  0.7 1.0 copy-done
  1.7 0.9 constant_dynamic-slice_fusion
  2.6 3.0 %collective-permute-start = (bf16[256,512]{1,0:T(8,128)(2,1)S(1)}, bf16[256,512]{1,0:T(8,128)(2,1)S(1)}, u32[]{:S(2)}, u32[]{:S(2)}) collective-permute-start(bf16[256,512]{1,0:T(8,128)(2,1)S(1)} %maximum_maximum_fusion.1), channel_id=1, source_target_pairs={{0,4},{4,0},{8,12},{12,8},{16,20},{20,16},{24,28},{28,24},{1,5},{5... | collective-permute-start | bytes 786440 | tf_op jit(solution)/shard_map/ppermute | solution.py:366
  5.6 0.1 fusion.2
  5.7 6.2 %collective-permute-done = bf16[256,512]{1,0:T(8,128)(2,1)S(1)} collective-permute-done((bf16[256,512]{1,0:T(8,128)(2,1)S(1)}, bf16[256,512]{1,0:T(8,128)(2,1)S(1)}, u32[]{:S(2)}, u32[]{:S(2)}) %collective-permute-start) | collective-permute-done | bytes 262176 | tf_op jit(solution)/shard_map/ppermute | solution.py:366
  11.9 0.1 broadcast_select_fusion.1
  12.1 0.0 copy-start.2
  12.2 1.8 %collective-permute-start.2 = (bf16[512,512]{1,0:T(8,128)(2,1)S(1)}, bf16[512,512]{1,0:T(8,128)(2,1)S(1)}, u32[]{:S(2)}, u32[]{:S(2)}) collective-permute-start(bf16[512,512]{1,0:T(8,128)(2,1)S(1)} %maximum_maximum_fusion.refs_8_), channel_id=1, source_target_pairs={{0,2},{1,3},{2,0},{3,1},{4,6},{5,7},{6,4},{7,5},{8,10},{9,11},{10,... | collective-permute-start | bytes 1572872 | tf_op jit(solution)/shard_map/ppermute | solution.py:366
  14.0 1.3 collective-permute-start.1
  15.2 1.3 collective-permute-start.4
  16.5 4.8 %collective-permute-start.7 = (bf16[512,512]{1,0:T(8,128)(2,1)S(1)}, bf16[512,512]{1,0:T(8,128)(2,1)}, u32[]{:S(2)}, u32[]{:S(2)}) collective-permute-start(bf16[512,512]{1,0:T(8,128)(2,1)S(1)} %maximum_maximum_fusion.refs_8_), channel_id=1, source_target_pairs={{0,8},{4,12},{8,0},{12,4},{16,24},{20,28},{24,16},{28,20},{1,9},{5... | collective-permute-start | bytes 1572872 | tf_op jit(solution)/shard_map/ppermute | solution.py:366
  21.3 2.6 %collective-permute-start.6 = (bf16[512,512]{1,0:T(8,128)(2,1)S(1)}, bf16[512,512]{1,0:T(8,128)(2,1)}, u32[]{:S(2)}, u32[]{:S(2)}) collective-permute-start(bf16[512,512]{1,0:T(8,128)(2,1)S(1)} %maximum_maximum_fusion.refs_8_), channel_id=1, source_target_pairs={{0,16},{4,20},{8,24},{12,28},{16,0},{20,4},{24,8},{28,12},{1,17},{... | collective-permute-start | bytes 1572872 | tf_op jit(solution)/shard_map/ppermute | solution.py:366
  23.9 5.9 %own_attention.1 = (bf16[512,1024]{1,0:T(8,128)(2,1)S(1)}, bf16[32,512]{1,0:T(8,128)(2,1)S(1)}) custom-call(bf16[512,1024]{1,0:T(8,128)(2,1)S(1)} %copy-done.3, bf16[512,1024]{1,0:T(8,128)(2,1)S(1)} %copy-done.1, bf16[512,1024]{1,0:T(8,128)(2,1)S(1)} %copy-done.2), custom_call_target="tpu_custom_call" | custom-call | flops 1 | bytes 1 | tf_op jit(solution)/shard_map/own_attention/pallas_call | solution.py:81
  29.9 0.8 collective-permute-done.1.q_ref
  30.7 2.7 %cross_attention.2 = bf16[528,512]{1,0:T(8,128)(2,1)S(1)} custom-call(bf16[512,512]{1,0:T(8,128)(2,1)S(1)} %collective-permute-done.1.q_ref, bf16[512,1024]{1,0:T(8,128)(2,1)S(1)} %copy-done.1, bf16[512,1024]{1,0:T(8,128)(2,1)S(1)} %copy-done.2), custom_call_target="tpu_custom_call" | custom-call | flops 1 | bytes 1 | tf_op jit(solution)/shard_map/cross_attention/pallas_call | solution.py:138
  33.3 6.2 %collective-permute-done.4.q_ref = bf16[512,512]{1,0:T(8,128)(2,1)S(1)} collective-permute-done((bf16[512,512]{1,0:T(8,128)(2,1)S(1)}, bf16[512,512]{1,0:T(8,128)(2,1)S(1)}, u32[]{:S(2)}, u32[]{:S(2)}) %collective-permute-start.4) | collective-permute-done | bytes 524320 | tf_op jit(solution)/shard_map/ppermute | solution.py:372
  39.6 3.5 %cross_attention.3 = bf16[528,512]{1,0:T(8,128)(2,1)} custom-call(bf16[512,512]{1,0:T(8,128)(2,1)S(1)} %collective-permute-done.4.q_ref, bf16[512,1024]{1,0:T(8,128)(2,1)S(1)} %copy-done.1, bf16[512,1024]{1,0:T(8,128)(2,1)S(1)} %copy-done.2), custom_call_target="tpu_custom_call" | custom-call | flops 1 | bytes 1 | tf_op jit(solution)/shard_map/cross_attention/pallas_call | solution.py:138
  43.0 18.6 %collective-permute-start.5 = (bf16[528,512]{1,0:T(8,128)(2,1)}, bf16[528,512]{1,0:T(8,128)(2,1)}, u32[]{:S(2)}, u32[]{:S(2)}) collective-permute-start(bf16[528,512]{1,0:T(8,128)(2,1)} %cross_attention.3), channel_id=1, source_target_pairs={{0,4},{4,8},{8,12},{12,16},{16,20},{20,24},{24,28},{1,5},{5,9},{9,... | collective-permute-start | bytes 1622024 | tf_op jit(solution)/shard_map/ppermute | solution.py:372
  61.7 2.1 %collective-permute-start.3 = (bf16[528,512]{1,0:T(8,128)(2,1)S(1)}, bf16[528,512]{1,0:T(8,128)(2,1)}, u32[]{:S(2)}, u32[]{:S(2)}) collective-permute-start(bf16[528,512]{1,0:T(8,128)(2,1)S(1)} %cross_attention.2), channel_id=1, source_target_pairs={{0,4},{4,8},{8,12},{12,16},{16,20},{20,24},{24,28},{1,5},{5,9},{9,... | collective-permute-start | bytes 1622024 | tf_op jit(solution)/shard_map/ppermute | solution.py:372
  63.7 0.5 collective-permute-start.8
  64.3 0.7 copy-done.17
  65.0 0.0 copy-done.14
  65.0 2.3 %collective-permute-start.23 = (bf16[512,512]{1,0:T(8,128)(2,1)}, bf16[512,512]{1,0:T(8,128)(2,1)}, u32[]{:S(2)}, u32[]{:S(2)}) collective-permute-start(bf16[512,512]{1,0:T(8,128)(2,1)} %collective-permute-done.6.refs_16_), channel_id=1, source_target_pairs={{0,8},{4,12},{8,0},{12,4},{16,24},{20,28},{24,16},{28,20},{1,9},{5... | collective-permute-start | bytes 1572872 | tf_op jit(solution)/shard_map/ppermute | solution.py:366
  67.3 0.1 slice_bitcast_fusion
  67.3 0.5 collective-permute-start.21
  67.9 0.1 add_bitcast_fusion
  67.9 0.1 copy.14.refs_5_
  68.1 0.1 copy.13.refs_4_.refs_29_
  68.2 0.1 stack.59
  68.3 10.7 %collective-permute-done.8.refs_14_ = bf16[512,512]{1,0:T(8,128)(2,1)} collective-permute-done((bf16[512,512]{1,0:T(8,128)(2,1)}, bf16[512,512]{1,0:T(8,128)(2,1)}, u32[]{:S(2)}, u32[]{:S(2)}) %collective-permute-start.8) | collective-permute-done | bytes 524320 | tf_op jit(solution)/shard_map/ppermute | solution.py:366
  78.9 0.7 copy-done.9
  79.6 3.6 %pool.1 = (bf16[512,1024]{1,0:T(8,128)(2,1)S(1)}, bf16[80,1024]{1,0:T(8,128)(2,1)S(1)}) custom-call(s32[1]{0:T(128)} %bitcast.2.lead_ref, bf16[512,1024]{1,0:T(8,128)(2,1)S(1)} %get-tuple-element.24.own_ref, bf16[32,512]{1,0:T(8,128)(2,1)S(1)} %get-tuple-element.25.lse_ref, bf16[528,512]{1,0:T(8,128)(2,1)} %collective-permute-done.3.refs_0_, ...), custom_call_target="tpu_custom_call" | custom-call | flops 1 | bytes 1 | tf_op jit(solution)/shard_map/pool/pallas_call | solution.py:214
  83.2 1.0 copy-done.4
  84.2 0.6 collective-permute-start.25
  84.8 0.1 collective-permute-start.12
  84.9 2.5 %collective-permute-start.9 = (bf16[80,1024]{1,0:T(8,128)(2,1)S(1)}, bf16[80,1024]{1,0:T(8,128)(2,1)}, u32[]{:S(2)}, u32[]{:S(2)}) collective-permute-start(bf16[80,1024]{1,0:T(8,128)(2,1)S(1)} %get-tuple-element.32.refs_0_), channel_id=1, source_target_pairs={{0,8},{4,12},{8,0},{12,4},{16,24},{20,28},{24,16},{28,20},{1,9},{5... | collective-permute-start | bytes 491528 | tf_op jit(solution)/shard_map/ppermute | solution.py:366
  87.4 3.2 %collective-permute-done.10.refs_2_ = bf16[80,1024]{1,0:T(8,128)(2,1)S(1)} collective-permute-done((bf16[80,1024]{1,0:T(8,128)(2,1)S(1)}, bf16[80,1024]{1,0:T(8,128)(2,1)S(1)}, u32[]{:S(2)}, u32[]{:S(2)}) %collective-permute-start.10) | collective-permute-done | bytes 163872 | tf_op jit(solution)/shard_map/ppermute | solution.py:366
  90.6 0.1 collective-permute-start.16
  90.7 0.7 copy-done.7
  91.3 0.5 collective-permute-start.17
  91.8 0.5 collective-permute-done.9.refs_1_
  92.3 0.6 gather_fusion
  92.9 0.1 stack.67
  93.0 3.0 %collective-permute-done.14.refs_6_ = bf16[80,1024]{1,0:T(8,128)(2,1)} collective-permute-done((bf16[80,1024]{1,0:T(8,128)(2,1)S(1)}, bf16[80,1024]{1,0:T(8,128)(2,1)}, u32[]{:S(2)}, u32[]{:S(2)}) %collective-permute-start.14) | collective-permute-done | bytes 163872 | tf_op jit(solution)/shard_map/ppermute | solution.py:366
  96.0 5.4 %collective-permute-done.11.refs_3_ = bf16[80,1024]{1,0:T(8,128)(2,1)} collective-permute-done((bf16[80,1024]{1,0:T(8,128)(2,1)S(1)}, bf16[80,1024]{1,0:T(8,128)(2,1)}, u32[]{:S(2)}, u32[]{:S(2)}) %collective-permute-start.11) | collective-permute-done | bytes 163872 | tf_op jit(solution)/shard_map/ppermute | solution.py:366
  101.4 2.0 %collective-permute-start.15 = (bf16[80,1024]{1,0:T(8,128)(2,1)}, bf16[80,1024]{1,0:T(8,128)(2,1)}, u32[]{:S(2)}, u32[]{:S(2)}) collective-permute-start(bf16[80,1024]{1,0:T(8,128)(2,1)} %collective-permute-done.11.refs_3_), channel_id=1, source_target_pairs={{0,4},{4,0},{8,12},{12,8},{16,20},{20,16},{24,28},{28,24},{1,5},{5... | collective-permute-start | bytes 491528 | tf_op jit(solution)/shard_map/ppermute | solution.py:366
  103.4 0.1 broadcast_and_fusion
  103.5 0.1 reshape.364
  103.6 0.6 copy-done.15
  104.2 0.1 pad.1.clone
  104.3 2.8 %collective-permute-done.13.refs_5_ = bf16[80,1024]{1,0:T(8,128)(2,1)} collective-permute-done((bf16[80,1024]{1,0:T(8,128)(2,1)}, bf16[80,1024]{1,0:T(8,128)(2,1)}, u32[]{:S(2)}, u32[]{:S(2)}) %collective-permute-start.13) | collective-permute-done | bytes 163872 | tf_op jit(solution)/shard_map/ppermute | solution.py:366
  107.1 1.8 %collective-permute-done.15.refs_7_ = bf16[80,1024]{1,0:T(8,128)(2,1)} collective-permute-done((bf16[80,1024]{1,0:T(8,128)(2,1)}, bf16[80,1024]{1,0:T(8,128)(2,1)}, u32[]{:S(2)}, u32[]{:S(2)}) %collective-permute-start.15) | collective-permute-done | bytes 163872 | tf_op jit(solution)/shard_map/ppermute | solution.py:366
  108.8 0.5 collective-permute-start.22
  109.3 0.1 collective-permute-start.24
  109.4 0.4 collective-permute-start.26
  109.8 0.1 pad_add_fusion.at_ref
  110.0 1.0 collective-permute-done.20.refs_17_
  110.9 0.7 collective-permute-done.22.refs_19_
  111.7 0.7 collective-permute-done.24.refs_21_
  112.4 0.7 collective-permute-done.26.refs_23_
  113.2 0.0 copy-done.12
  113.2 0.7 copy-done.13
  114.0 17.0 %patches.1 = (bf16[512,1024]{1,0:T(8,128)(2,1)}, bf16[80,2048]{1,0:T(8,128)(2,1)}) custom-call(s32[2]{0:T(128)S(1)} %pad_add_fusion.at_ref, bf16[80,1024]{1,0:T(8,128)(2,1)S(1)} %get-tuple-element.32.refs_0_, bf16[80,1024]{1,0:T(8,128)(2,1)} %collective-permute-done.9.refs_1_, bf16[80,1024]{1,0:T(8,128)(2,1)S(1)} %collective-permute-done.10.refs_2_, ...), custom_call_target="tpu_custom_call" | custom-call | flops 1 | bytes 1 | tf_op jit(solution)/shard_map/patches/pallas_call | solution.py:339
  (64 shorter events, 0.3 us)
Async XLA Ops:
  0.6 1.0 copy-start
  0.6 5.0 %copy-start.3 = (bf16[512,1024]{1,0:T(8,128)(2,1)S(1)}, bf16[512,1024]{1,0:T(8,128)(2,1)}, u32[]{:S(2)}) copy-start(bf16[512,1024]{1,0:T(8,128)(2,1)} %q_ref) | copy-start | bytes 3145732
  2.6 9.3 %collective-permute-start = (bf16[256,512]{1,0:T(8,128)(2,1)S(1)}, bf16[256,512]{1,0:T(8,128)(2,1)S(1)}, u32[]{:S(2)}, u32[]{:S(2)}) collective-permute-start(bf16[256,512]{1,0:T(8,128)(2,1)S(1)} %maximum_maximum_fusion.1), channel_id=1, source_target_pairs={{0,4},{4,0},{8,12},{12,8},{16,20},{20,16},{24,28},{28,24},{1,5},{5... | collective-permute-start | bytes 786440 | tf_op jit(solution)/shard_map/ppermute | solution.py:366
  12.0 11.9 %copy-start.1 = (bf16[512,1024]{1,0:T(8,128)(2,1)S(1)}, bf16[512,1024]{1,0:T(8,128)(2,1)}, u32[]{:S(2)}) copy-start(bf16[512,1024]{1,0:T(8,128)(2,1)} %k_ref.5) | copy-start | bytes 3145732
  12.1 11.9 %copy-start.2 = (bf16[512,1024]{1,0:T(8,128)(2,1)S(1)}, bf16[512,1024]{1,0:T(8,128)(2,1)}, u32[]{:S(2)}) copy-start(bf16[512,1024]{1,0:T(8,128)(2,1)} %v_ref.5) | copy-start | bytes 3145732
  12.2 17.7 %collective-permute-start.2 = (bf16[512,512]{1,0:T(8,128)(2,1)S(1)}, bf16[512,512]{1,0:T(8,128)(2,1)S(1)}, u32[]{:S(2)}, u32[]{:S(2)}) collective-permute-start(bf16[512,512]{1,0:T(8,128)(2,1)S(1)} %maximum_maximum_fusion.refs_8_), channel_id=1, source_target_pairs={{0,2},{1,3},{2,0},{3,1},{4,6},{5,7},{6,4},{7,5},{8,10},{9,11},{10,... | collective-permute-start | bytes 1572872 | tf_op jit(solution)/shard_map/ppermute | solution.py:366
  14.0 16.7 %collective-permute-start.1 = (bf16[512,512]{1,0:T(8,128)(2,1)S(1)}, bf16[512,512]{1,0:T(8,128)(2,1)S(1)}, u32[]{:S(2)}, u32[]{:S(2)}) collective-permute-start(bf16[512,512]{1,0:T(8,128)(2,1)S(1)} %get-tuple-element.26), channel_id=1, source_target_pairs={{4,0},{8,4},{12,8},{16,12},{20,16},{24,20},{28,24},{5,1},{9,5},{13... | collective-permute-start | bytes 1572872 | tf_op jit(solution)/shard_map/ppermute | solution.py:372
  15.2 24.3 %collective-permute-start.4 = (bf16[512,512]{1,0:T(8,128)(2,1)S(1)}, bf16[512,512]{1,0:T(8,128)(2,1)S(1)}, u32[]{:S(2)}, u32[]{:S(2)}) collective-permute-start(bf16[512,512]{1,0:T(8,128)(2,1)S(1)} %get-tuple-element.28), channel_id=1, source_target_pairs={{4,0},{8,4},{12,8},{16,12},{20,16},{24,20},{28,24},{5,1},{9,5},{13... | collective-permute-start | bytes 1572872 | tf_op jit(solution)/shard_map/ppermute | solution.py:372
  16.5 47.2 %collective-permute-start.7 = (bf16[512,512]{1,0:T(8,128)(2,1)S(1)}, bf16[512,512]{1,0:T(8,128)(2,1)}, u32[]{:S(2)}, u32[]{:S(2)}) collective-permute-start(bf16[512,512]{1,0:T(8,128)(2,1)S(1)} %maximum_maximum_fusion.refs_8_), channel_id=1, source_target_pairs={{0,8},{4,12},{8,0},{12,4},{16,24},{20,28},{24,16},{28,20},{1,9},{5... | collective-permute-start | bytes 1572872 | tf_op jit(solution)/shard_map/ppermute | solution.py:366
  21.3 43.7 %collective-permute-start.6 = (bf16[512,512]{1,0:T(8,128)(2,1)S(1)}, bf16[512,512]{1,0:T(8,128)(2,1)}, u32[]{:S(2)}, u32[]{:S(2)}) collective-permute-start(bf16[512,512]{1,0:T(8,128)(2,1)S(1)} %maximum_maximum_fusion.refs_8_), channel_id=1, source_target_pairs={{0,16},{4,20},{8,24},{12,28},{16,0},{20,4},{24,8},{28,12},{1,17},{... | collective-permute-start | bytes 1572872 | tf_op jit(solution)/shard_map/ppermute | solution.py:366
  29.9 3.5 %copy-start.5 = (bf16[512,512]{1,0:T(8,128)(2,1)}, bf16[512,512]{1,0:T(8,128)(2,1)S(1)}, u32[]{:S(2)}) copy-start(bf16[512,512]{1,0:T(8,128)(2,1)S(1)} %collective-permute-done.2.refs_10_) | copy-start | bytes 1572868
  43.0 35.9 %collective-permute-start.5 = (bf16[528,512]{1,0:T(8,128)(2,1)}, bf16[528,512]{1,0:T(8,128)(2,1)}, u32[]{:S(2)}, u32[]{:S(2)}) collective-permute-start(bf16[528,512]{1,0:T(8,128)(2,1)} %cross_attention.3), channel_id=1, source_target_pairs={{0,4},{4,8},{8,12},{12,16},{16,20},{20,24},{24,28},{1,5},{5,9},{9,... | collective-permute-start | bytes 1622024 | tf_op jit(solution)/shard_map/ppermute | solution.py:372
  61.7 17.3 %collective-permute-start.3 = (bf16[528,512]{1,0:T(8,128)(2,1)S(1)}, bf16[528,512]{1,0:T(8,128)(2,1)}, u32[]{:S(2)}, u32[]{:S(2)}) collective-permute-start(bf16[528,512]{1,0:T(8,128)(2,1)S(1)} %cross_attention.2), channel_id=1, source_target_pairs={{0,4},{4,8},{8,12},{12,16},{16,20},{20,24},{24,28},{1,5},{5,9},{9,... | collective-permute-start | bytes 1622024 | tf_op jit(solution)/shard_map/ppermute | solution.py:372
  63.7 15.2 %collective-permute-start.8 = (bf16[512,512]{1,0:T(8,128)(2,1)}, bf16[512,512]{1,0:T(8,128)(2,1)}, u32[]{:S(2)}, u32[]{:S(2)}) collective-permute-start(bf16[512,512]{1,0:T(8,128)(2,1)} %collective-permute-done.7.refs_12_), channel_id=1, source_target_pairs={{0,2},{1,3},{2,0},{3,1},{4,6},{5,7},{6,4},{7,5},{8,10},{9,11},{10,... | collective-permute-start | bytes 1572872 | tf_op jit(solution)/shard_map/ppermute | solution.py:366
  64.3 0.7 copy-start.17
  64.3 0.7 copy-start.14
  65.0 19.2 %collective-permute-start.23 = (bf16[512,512]{1,0:T(8,128)(2,1)}, bf16[512,512]{1,0:T(8,128)(2,1)}, u32[]{:S(2)}, u32[]{:S(2)}) collective-permute-start(bf16[512,512]{1,0:T(8,128)(2,1)} %collective-permute-done.6.refs_16_), channel_id=1, source_target_pairs={{0,8},{4,12},{8,0},{12,4},{16,24},{20,28},{24,16},{28,20},{1,9},{5... | collective-permute-start | bytes 1572872 | tf_op jit(solution)/shard_map/ppermute | solution.py:366
  67.3 23.2 %collective-permute-start.21 = (bf16[512,512]{1,0:T(8,128)(2,1)}, bf16[512,512]{1,0:T(8,128)(2,1)}, u32[]{:S(2)}, u32[]{:S(2)}) collective-permute-start(bf16[512,512]{1,0:T(8,128)(2,1)} %collective-permute-done.6.refs_16_), channel_id=1, source_target_pairs={{0,2},{1,3},{2,0},{3,1},{4,6},{5,7},{6,4},{7,5},{8,10},{9,11},{10,... | collective-permute-start | bytes 1572872 | tf_op jit(solution)/shard_map/ppermute | solution.py:366
  78.9 0.7 copy-start.9
  79.6 11.7 %copy-start.6 = (bf16[512,512]{1,0:T(8,128)(2,1)S(1)}, bf16[512,512]{1,0:T(8,128)(2,1)}, u32[]{:S(2)}) copy-start(bf16[512,512]{1,0:T(8,128)(2,1)} %copy-done.5) | copy-start | bytes 1572868
  79.6 24.6 %copy-start.16 = (bf16[2048]{0:T(1024)(128)(2,1)S(1)}, bf16[2048]{0:T(1024)(128)(2,1)}, u32[]{:S(2)}) copy-start(bf16[2048]{0:T(1024)(128)(2,1)} %param.19) | copy-start | bytes 12292
  83.2 1.0 copy-start.4
  84.2 6.4 %collective-permute-start.10 = (bf16[80,1024]{1,0:T(8,128)(2,1)S(1)}, bf16[80,1024]{1,0:T(8,128)(2,1)S(1)}, u32[]{:S(2)}, u32[]{:S(2)}) collective-permute-start(bf16[80,1024]{1,0:T(8,128)(2,1)S(1)} %get-tuple-element.32.refs_0_), channel_id=1, source_target_pairs={{0,16},{4,20},{8,24},{12,28},{16,0},{20,4},{24,8},{28,12},{1,17},{... | collective-permute-start | bytes 491528 | tf_op jit(solution)/shard_map/ppermute | solution.py:366
  84.2 17.2 %collective-permute-start.25 = (bf16[512,512]{1,0:T(8,128)(2,1)}, bf16[512,512]{1,0:T(8,128)(2,1)}, u32[]{:S(2)}, u32[]{:S(2)}) collective-permute-start(bf16[512,512]{1,0:T(8,128)(2,1)} %collective-permute-done.23.refs_20_), channel_id=1, source_target_pairs={{0,2},{1,3},{2,0},{3,1},{4,6},{5,7},{6,4},{7,5},{8,10},{9,11},{10,... | collective-permute-start | bytes 1572872 | tf_op jit(solution)/shard_map/ppermute | solution.py:366
  84.8 5.9 %collective-permute-start.12 = (bf16[80,1024]{1,0:T(8,128)(2,1)S(1)}, bf16[80,1024]{1,0:T(8,128)(2,1)S(1)}, u32[]{:S(2)}, u32[]{:S(2)}) collective-permute-start(bf16[80,1024]{1,0:T(8,128)(2,1)S(1)} %get-tuple-element.32.refs_0_), channel_id=1, source_target_pairs={{0,4},{4,0},{8,12},{12,8},{16,20},{20,16},{24,28},{28,24},{1,5},{5... | collective-permute-start | bytes 491528 | tf_op jit(solution)/shard_map/ppermute | solution.py:366
  84.9 7.5 %collective-permute-start.9 = (bf16[80,1024]{1,0:T(8,128)(2,1)S(1)}, bf16[80,1024]{1,0:T(8,128)(2,1)}, u32[]{:S(2)}, u32[]{:S(2)}) collective-permute-start(bf16[80,1024]{1,0:T(8,128)(2,1)S(1)} %get-tuple-element.32.refs_0_), channel_id=1, source_target_pairs={{0,8},{4,12},{8,0},{12,4},{16,24},{20,28},{24,16},{28,20},{1,9},{5... | collective-permute-start | bytes 491528 | tf_op jit(solution)/shard_map/ppermute | solution.py:366
  90.6 5.4 %collective-permute-start.14 = (bf16[80,1024]{1,0:T(8,128)(2,1)S(1)}, bf16[80,1024]{1,0:T(8,128)(2,1)}, u32[]{:S(2)}, u32[]{:S(2)}) collective-permute-start(bf16[80,1024]{1,0:T(8,128)(2,1)S(1)} %collective-permute-done.10.refs_2_), channel_id=1, source_target_pairs={{0,4},{4,0},{8,12},{12,8},{16,20},{20,16},{24,28},{28,24},{1,5},{5... | collective-permute-start | bytes 491528 | tf_op jit(solution)/shard_map/ppermute | solution.py:366
  90.6 18.2 %collective-permute-start.16 = (bf16[512,512]{1,0:T(8,128)(2,1)S(1)}, bf16[512,512]{1,0:T(8,128)(2,1)S(1)}, u32[]{:S(2)}, u32[]{:S(2)}) collective-permute-start(bf16[512,512]{1,0:T(8,128)(2,1)S(1)} %maximum_maximum_fusion.refs_8_), channel_id=1, source_target_pairs={{0,1},{1,0},{2,3},{3,2},{4,5},{5,4},{6,7},{7,6},{8,9},{9,8},{10,11... | collective-permute-start | bytes 1572872 | tf_op jit(solution)/shard_map/ppermute | solution.py:366
  90.7 0.7 copy-start.7
  91.3 18.0 %collective-permute-start.17 = (bf16[512,512]{1,0:T(8,128)(2,1)S(1)}, bf16[512,512]{1,0:T(8,128)(2,1)S(1)}, u32[]{:S(2)}, u32[]{:S(2)}) collective-permute-start(bf16[512,512]{1,0:T(8,128)(2,1)S(1)} %copy-done.6), channel_id=1, source_target_pairs={{0,1},{1,0},{2,3},{3,2},{4,5},{5,4},{6,7},{7,6},{8,9},{9,8},{10,11... | collective-permute-start | bytes 1572872 | tf_op jit(solution)/shard_map/ppermute | solution.py:366
  92.3 17.1 %collective-permute-start.18 = (bf16[512,512]{1,0:T(8,128)(2,1)}, bf16[512,512]{1,0:T(8,128)(2,1)S(1)}, u32[]{:S(2)}, u32[]{:S(2)}) collective-permute-start(bf16[512,512]{1,0:T(8,128)(2,1)} %collective-permute-done.7.refs_12_), channel_id=1, source_target_pairs={{0,1},{1,0},{2,3},{3,2},{4,5},{5,4},{6,7},{7,6},{8,9},{9,8},{10,11... | collective-permute-start | bytes 1572872 | tf_op jit(solution)/shard_map/ppermute | solution.py:366
  96.0 5.4 %collective-permute-start.11 = (bf16[80,1024]{1,0:T(8,128)(2,1)S(1)}, bf16[80,1024]{1,0:T(8,128)(2,1)}, u32[]{:S(2)}, u32[]{:S(2)}) collective-permute-start(bf16[80,1024]{1,0:T(8,128)(2,1)S(1)} %collective-permute-done.10.refs_2_), channel_id=1, source_target_pairs={{0,8},{4,12},{8,0},{12,4},{16,24},{20,28},{24,16},{28,20},{1,9},{5... | collective-permute-start | bytes 491528 | tf_op jit(solution)/shard_map/ppermute | solution.py:366
  96.0 7.6 %copy-start.18 = (bf16[1024]{0:T(1024)(128)(2,1)S(1)}, bf16[1024]{0:T(1024)(128)(2,1)}, u32[]{:S(2)}) copy-start(bf16[1024]{0:T(1024)(128)(2,1)} %param.20) | copy-start | bytes 6148
  101.4 5.6 %collective-permute-start.13 = (bf16[80,1024]{1,0:T(8,128)(2,1)}, bf16[80,1024]{1,0:T(8,128)(2,1)}, u32[]{:S(2)}, u32[]{:S(2)}) collective-permute-start(bf16[80,1024]{1,0:T(8,128)(2,1)} %collective-permute-done.9.refs_1_), channel_id=1, source_target_pairs={{0,4},{4,0},{8,12},{12,8},{16,20},{20,16},{24,28},{28,24},{1,5},{5... | collective-permute-start | bytes 491528 | tf_op jit(solution)/shard_map/ppermute | solution.py:366
  101.4 7.4 %collective-permute-start.15 = (bf16[80,1024]{1,0:T(8,128)(2,1)}, bf16[80,1024]{1,0:T(8,128)(2,1)}, u32[]{:S(2)}, u32[]{:S(2)}) collective-permute-start(bf16[80,1024]{1,0:T(8,128)(2,1)} %collective-permute-done.11.refs_3_), channel_id=1, source_target_pairs={{0,4},{4,0},{8,12},{12,8},{16,20},{20,16},{24,28},{28,24},{1,5},{5... | collective-permute-start | bytes 491528 | tf_op jit(solution)/shard_map/ppermute | solution.py:366
  103.5 0.7 copy-start.15
  103.6 10.4 %copy-start.8 = (bf16[80,1024]{1,0:T(8,128)(2,1)S(1)}, bf16[80,1024]{1,0:T(8,128)(2,1)}, u32[]{:S(2)}) copy-start(bf16[80,1024]{1,0:T(8,128)(2,1)} %copy-done.7) | copy-start | bytes 491524
  107.1 2.9 %collective-permute-start.19 = (bf16[512,512]{1,0:T(8,128)(2,1)}, bf16[512,512]{1,0:T(8,128)(2,1)S(1)}, u32[]{:S(2)}, u32[]{:S(2)}) collective-permute-start(bf16[512,512]{1,0:T(8,128)(2,1)} %collective-permute-done.8.refs_14_), channel_id=1, source_target_pairs={{0,1},{1,0},{2,3},{3,2},{4,5},{5,4},{6,7},{7,6},{8,9},{9,8},{10,11... | collective-permute-start | bytes 1572872 | tf_op jit(solution)/shard_map/ppermute | solution.py:366
  108.8 2.1 %collective-permute-start.20 = (bf16[512,512]{1,0:T(8,128)(2,1)}, bf16[512,512]{1,0:T(8,128)(2,1)S(1)}, u32[]{:S(2)}, u32[]{:S(2)}) collective-permute-start(bf16[512,512]{1,0:T(8,128)(2,1)} %collective-permute-done.6.refs_16_), channel_id=1, source_target_pairs={{0,1},{1,0},{2,3},{3,2},{4,5},{5,4},{6,7},{7,6},{8,9},{9,8},{10,11... | collective-permute-start | bytes 1572872 | tf_op jit(solution)/shard_map/ppermute | solution.py:366
  108.8 2.9 %collective-permute-start.22 = (bf16[512,512]{1,0:T(8,128)(2,1)}, bf16[512,512]{1,0:T(8,128)(2,1)S(1)}, u32[]{:S(2)}, u32[]{:S(2)}) collective-permute-start(bf16[512,512]{1,0:T(8,128)(2,1)} %collective-permute-done.21.refs_18_), channel_id=1, source_target_pairs={{0,1},{1,0},{2,3},{3,2},{4,5},{5,4},{6,7},{7,6},{8,9},{9,8},{10,11... | collective-permute-start | bytes 1572872 | tf_op jit(solution)/shard_map/ppermute | solution.py:366
  109.3 3.1 %collective-permute-start.24 = (bf16[512,512]{1,0:T(8,128)(2,1)}, bf16[512,512]{1,0:T(8,128)(2,1)S(1)}, u32[]{:S(2)}, u32[]{:S(2)}) collective-permute-start(bf16[512,512]{1,0:T(8,128)(2,1)} %collective-permute-done.23.refs_20_), channel_id=1, source_target_pairs={{0,1},{1,0},{2,3},{3,2},{4,5},{5,4},{6,7},{7,6},{8,9},{9,8},{10,11... | collective-permute-start | bytes 1572872 | tf_op jit(solution)/shard_map/ppermute | solution.py:366
  109.4 3.8 %collective-permute-start.26 = (bf16[512,512]{1,0:T(8,128)(2,1)}, bf16[512,512]{1,0:T(8,128)(2,1)S(1)}, u32[]{:S(2)}, u32[]{:S(2)}) collective-permute-start(bf16[512,512]{1,0:T(8,128)(2,1)} %collective-permute-done.25.refs_22_), channel_id=1, source_target_pairs={{0,1},{1,0},{2,3},{3,2},{4,5},{5,4},{6,7},{7,6},{8,9},{9,8},{10,11... | collective-permute-start | bytes 1572872 | tf_op jit(solution)/shard_map/ppermute | solution.py:366
  110.9 2.3 %copy-start.10 = (bf16[512,512]{1,0:T(8,128)(2,1)}, bf16[512,512]{1,0:T(8,128)(2,1)S(1)}, u32[]{:S(2)}) copy-start(bf16[512,512]{1,0:T(8,128)(2,1)S(1)} %collective-permute-done.20.refs_17_) | copy-start | bytes 1572868
  111.7 1.5 %copy-start.11 = (bf16[512,512]{1,0:T(8,128)(2,1)}, bf16[512,512]{1,0:T(8,128)(2,1)S(1)}, u32[]{:S(2)}) copy-start(bf16[512,512]{1,0:T(8,128)(2,1)S(1)} %collective-permute-done.22.refs_19_) | copy-start | bytes 1572868
  112.4 0.8 copy-start.12
  113.2 0.8 copy-start.13
